TPU v7x, 32 devices: a whole 2x2x4 slice. The times are simulated.
32 devices in a mesh: group: 2 (over y), col: 8 (over z, x), batch: 2 (over core).
Axes of the slice: x: 2, y: 2, z: 4, core: 2. Of those that a mesh axis runs over, the one named last changes fastest.
Arguments:
- base_input: bfloat16 [1024, 131072], P(('group', 'batch'), 'col'), parts along dimension 0, may hold values from -6 to 6
- cotangent: bfloat16 [1024, 131072], P(('group', 'batch'), 'col'), parts along dimension 0, may hold values from -1.5 to 1.5
- u_factor: bfloat16 [131072, 1024], P(('col', 'batch')), may hold values from -0.1875 to 0.1875
- v_factor: bfloat16 [131072, 1024], P(('col', 'batch')), may hold values from -0.015625 to 0.015625
- bias: bfloat16 [131072], P('col'), may hold values from -4 to 4
Outputs:
- grad_input: bfloat16 [1024, 131072], P(('group', 'batch'), 'col'), parts along dimension 0
- grad_u: bfloat16 [262144, 1024], P(('group', 'col', 'batch')), parts along dimension 0
- grad_v: bfloat16 [262144, 1024], P(('group', 'col', 'batch')), parts along dimension 0
- grad_bias: float32 [262144], P(('group', 'col', 'batch')), parts along dimension 0
There are 2 independent parts, one for each index of `group`. A program takes and returns all parts, laid end to end along the dimension named above; an argument that names none is the same for every part. Nothing has to cross between parts.
All inputs are finite; a program needn't handle non-finite values.
Results may differ from a plain program's by a relative error of at most 0.0058.
Values may be sent and summed in bfloat16 or wider, within the bound.
No kernel may reach another device: no remote copies, remote signals or barrier semaphores. Data moves between devices by JAX's collectives and lax.ppermute only.
A program may use at most 640 MiB of HBM per device.

v0:
```python
import jax
import jax.numpy as jnp
from jax import lax
from jax.experimental import pallas as pl
from jax.experimental.pallas import tpu as pltpu
from jax.sharding import PartitionSpec as P

BF, F32 = jnp.bfloat16, jnp.float32
MIB = 1 << 20
NT = (((1,), (1,)), ((), ()))


class Place:
    def __getitem__(self, i):
        return lax.axis_index(("batch", "col")[i])


def call(body, name, ins, outs, scratch=(), flops=0, aliases=None, mib=4, after=(), us=0.3, carry=(), ahead=()):
    specs = {"v": pl.BlockSpec(memory_space=pltpu.VMEM), "h": pl.BlockSpec(memory_space=pl.ANY)}
    spaces = {"v": pltpu.VMEM, "h": pltpu.HBM}
    n_ins, n_ahead, n_outs, n_after = len(ins), len(ahead), len(outs), len(after)
    aliases = dict(aliases or {})
    aliases.update({n_ins + n_ahead + i: n_outs + n_ahead + i for i in range(len(carry))})
    ins = list(ins) + [(a, "h") for a, _, _ in ahead] + [(a, "v") for a in carry]
    ins += [a if isinstance(a, tuple) else (a, "v") for a in after]
    outs = list(outs) + [((rows, a.shape[1]), a.dtype, "v") for a, _, rows in ahead] + [(a.shape, a.dtype, "v") for a in carry]
    args = [pltpu.with_memory_space_constraint(a, spaces[w]) for a, w in ins]

    def whole(*refs):
        first = len(ins)
        sems = refs[-1] if n_ahead else None
        scratch_refs = refs[first + len(outs) : len(refs) - (n_ahead > 0)]
        fetches = [
            pltpu.make_async_copy(refs[n_ins + i].at[pl.ds(row, rows), :], refs[first + n_outs + i], sems.at[i])
            for i, (_, row, rows) in enumerate(ahead)
        ]
        body(Place(), *refs[:n_ins], *refs[first : first + n_outs], *scratch_refs, fetch=lambda: [f.start() for f in fetches])
        for f in fetches:
            f.wait()

    return pl.pallas_call(
        whole if n_ahead else lambda *refs: body(Place(), *refs[:n_ins], *refs[len(ins) : len(ins) + n_outs], *refs[len(ins) + len(outs) :]),
        out_shape=tuple(spaces[w](dims, dtype) for dims, dtype, w in outs),
        in_specs=[specs[w] for _, w in ins],
        out_specs=tuple(specs[w] for _, _, w in outs),
        scratch_shapes=list(scratch) + ([pltpu.SemaphoreType.DMA((n_ahead,))] if n_ahead else []),
        input_output_aliases=aliases,
        compiler_params=pltpu.CompilerParams(vmem_limit_bytes=mib * MIB),
        cost_estimate=pl.CostEstimate(flops=int(1.7 * flops + us * 1.15e9), bytes_accessed=0, transcendentals=0),
        name=name,
    )(*args)


def nothing():
    pass


def at_block(i, size):
    return pl.ds(pl.multiple_of(i * size, size), size)


def dma(n):
    return pltpu.SemaphoreType.DMA((n,))


def copy(src, dst, sem):
    return pltpu.make_async_copy(src, dst, sem)


def cut_half(x, half, after=()):
    rows = x.shape[0]
    n = 8
    step = rows // n

    def body(at_ref, x_ref, o_ref, sems):
        def cut(i):
            here = pl.ds(i * step, step)
            return copy(x_ref.at[here, at_block(1 - at_ref[0], half)], o_ref.at[here, :], sems.at[i])

        for i in range(n):
            cut(i).start()
        for i in range(n):
            cut(i).wait()

    return call(body, "cut_half", [(x, "h")], [((rows, half), BF, "v")], [dma(n)], us=2.2, after=after)[0]


VPARTS = 4


def project_own(x, v, c, after=()):
    rows, (half, rank) = x.shape[0], v.shape
    part = half // VPARTS
    tk = min(1024, part)
    n = half // tk
    each = part // tk

    def body(at_ref, x_ref, v_ref, c_ref, p_ref, xv_ref, cs_ref, *refs):
        vv, (acc, x_sem, v_sem, c_sem) = refs[:VPARTS], refs[VPARTS:]

        def cut(ref, dst, core, k, sem):
            src = ref.at[:, pl.ds(pl.multiple_of(core * half + k * tk, tk), tk)]
            return copy(src, dst.at[:, at_block(k, tk)], sem.at[k])

        def x_copy(k):
            return cut(x_ref, xv_ref, at_ref[0], k, x_sem)

        def c_copy(k):
            return cut(c_ref, cs_ref, 1 - at_ref[0], k, c_sem)

        def v_copy(k, i, j):
            return copy(v_ref.at[at_block(k, tk), :], vv[i].at[at_block(j, tk), :], v_sem.at[k])

        for k in range(n):
            x_copy(k).start()
            v_copy(k, k // each, k % each).start()
        for k in range(n):
            c_copy(k).start()
        acc[...] = jnp.zeros_like(acc)
        for i in range(VPARTS):

            @pl.loop(0, each)
            def _(j):
                k = i * each + j
                x_copy(k).wait()
                v_copy(k, i, j).wait()
                acc[...] += jnp.dot(xv_ref[:, at_block(k, tk)], vv[i][at_block(j, tk), :], preferred_element_type=F32)

        p_ref[...] = acc[...].astype(BF)
        for k in range(n):
            c_copy(k).wait()

    return call(
        body,
        "project_own",
        [(x, "h"), (v, "h"), (c, "h")],
        [((rows, rank), BF, "v"), ((rows, half), BF, "v"), ((rows, half), BF, "v")] + [((part, rank), BF, "v")] * VPARTS,
        [pltpu.VMEM((rows, rank), F32)] + [dma(n)] * 3,
        flops=2 * rows * half * rank,
        mib=8,
        after=after,
    )


def write_halves(at_ref, total, outs):
    if len(outs) == 1:
        outs[0][...] = total(slice(None))
        return
    each = outs[0].shape[0]
    bit = at_ref[1] & 1
    for i, o_ref in ((bit, outs[0]), (1 - bit, outs[1])):
        o_ref[...] = total(at_block(i, each)).astype(BF)


def halves_of(rows, rank, direct):
    return [((rows // 2, rank), BF, "v")] * 2 if direct else [((rows, rank), F32, "v")]


def project_other(x_o, vs, theirs, direct):
    rows, half = x_o.shape
    part, rank = vs[0].shape
    tk = min(1024, part)
    each = part // tk

    def body(at_ref, x_ref, t_ref, *refs):
        vv, outs, acc = refs[:VPARTS], refs[VPARTS:-1], refs[-1]
        acc[...] = t_ref[...].astype(F32)
        for i in range(VPARTS):

            @pl.loop(0, each)
            def _(j):
                acc[...] += jnp.dot(x_ref[:, at_block(i * each + j, tk)], vv[i][at_block(j, tk), :], preferred_element_type=F32)

        write_halves(at_ref, lambda here: acc[here, :], outs)

    return call(
        body,
        "project_other",
        [(x_o, "v"), (theirs, "v")] + [(a, "v") for a in vs],
        halves_of(rows, rank, direct),
        [pltpu.VMEM((rows, rank), F32)],
        flops=2 * rows * half * rank,
        mib=8,
    )


def fetch_first(c, u, after=()):
    rows, part = c.shape[0], u.shape[0] // 2

    def body(at_ref, c_ref, cv_ref, c_sem, fetch):
        first_c = copy(c_ref.at[:, at_block(2 * at_ref[0], part)], cv_ref, c_sem.at[0])
        fetch()
        first_c.start()
        first_c.wait()

    return call(
        body, "fetch_first", [(c, "h")], [((rows, part), BF, "v")], [dma(1)], ahead=[(u, 0, part // 2)], after=after, us=2.8
    )


def hidden(c, x):
    return (c.astype(F32) * x.astype(F32)).astype(BF)


def back_project(s, x, x_o, c, c_o, u, u_first, so_far, c_all=None, after=()):
    rows, (half, rank) = x.shape[0], u.shape
    part = half // 2
    tk = u_first.shape[0]
    n = part // tk
    first = so_far is None
    n_outs = 2 if first else 3

    def body(at_ref, x_ref, xo_ref, c_ref, co_ref, u_ref, uf_ref, *refs, fetch=nothing):
        if first:
            all_ref, acc_ref, b_ref, next_ref, uv, h, u_sem, c_sem = refs
            src = all_ref.at[:, pl.ds(pl.multiple_of(at_ref[0] * half + part, part), part)]
            next_c = copy(src, next_ref, c_sem.at[0])
        else:
            so_ref, own_ref, oth_ref, b_ref, uv, h, u_sem = refs

        def u_copy(k):
            return copy(u_ref.at[pl.ds(s * part + k * tk, tk), :], uv.at[k - 1], u_sem.at[k - 1])

        for k in range(1, n):
            u_copy(k).start()
        if first:
            next_c.start()
        fetch()
        for k in range(n):
            here = pl.ds(k * tk, tk)
            there = pl.ds(s * part + k * tk, tk)
            own = hidden(c_ref[:, here], x_ref[:, there])
            oth = hidden(co_ref[:, there], xo_ref[:, there])
            h[k, :rows, :] = own
            h[k, rows:, :] = oth
            b_ref[:, here] = jnp.sum(own.astype(F32), axis=0, keepdims=True) + jnp.sum(oth.astype(F32), axis=0, keepdims=True)
        for k in range(1, n):
            u_copy(k).wait()

        @pl.loop(0, 2)
        def _(i):
            at_rows = at_block(i, rows)
            total = None if first else so_ref[at_rows, :]
            for k in range(n):
                term = jnp.dot(h[k, at_rows, :], uv[k - 1] if k else uf_ref[...], preferred_element_type=F32)
                total = term if total is None else total + term
            if first:
                acc_ref[at_rows, :] = total
            else:

                @pl.when(i == 0)
                def _():
                    own_ref[...] = total.astype(BF)

                @pl.when(i == 1)
                def _():
                    oth_ref[...] = total

        if first:
            next_c.wait()

    outs = [((2 * rows, rank), F32, "v")] if first else [((rows, rank), BF, "v"), ((rows, rank), F32, "v")]
    outs += [((1, part), F32, "v")] + ([((rows, part), BF, "v")] if first else [])
    return call(
        body,
        "back_project",
        [(x, "v"), (x_o, "v"), (c, "v"), (c_o, "v"), (u, "h"), (u_first, "v"), (c_all, "h") if first else (so_far, "v")],
        outs,
        [pltpu.VMEM((max(1, n - 1), tk, rank), BF), pltpu.VMEM((n, 2 * rows, tk), BF), dma(max(1, n - 1))]
        + ([dma(1)] if first else []),
        flops=2 * rows * half * rank,
        mib=16,
        after=after,
        ahead=[(u, part, tk)] if first else [],
    )


def turn_x(x, x_o, after=()):
    rows, half = x.shape
    tw = min(512, half)
    n = half // tw

    def body(at_ref, x_ref, xo_ref, o_ref, stage, sems):
        def out(k):
            slot = lax.rem(k, 2)
            return copy(stage.at[slot], o_ref.at[at_block(k, tw), :], sems.at[slot])

        @pl.loop(0, n)
        def _(k):
            here = at_block(k, tw)
            slot = lax.rem(k, 2)

            @pl.when(k >= 2)
            def _():
                out(k).wait()

            stage[slot, :, :rows] = x_ref[:, here].T
            stage[slot, :, rows:] = xo_ref[:, here].T
            out(k).start()

        for k in range(max(0, n - 2), n):
            out(k).wait()

    return call(
        body,
        "turn_x",
        [(x, "v"), (x_o, "v")],
        [((half, 2 * rows), BF, "h")],
        [pltpu.VMEM((2, tw, 2 * rows), BF), dma(2)],
        after=after,
        us=3.6,
    )[0]


def turn_hidden(s, x, x_o, c, c_o, after=(), carry=()):
    rows, half = x.shape
    part = half // 2
    tw = min(512, part)

    def body(at_ref, x_ref, xo_ref, c_ref, co_ref, o_ref):
        @pl.loop(0, part // tw)
        def _(k):
            here = at_block(k, tw)
            there = pl.ds(pl.multiple_of(s * part + k * tw, tw), tw)
            o_ref[here, :rows] = hidden(c_ref[:, here], x_ref[:, there]).T
            o_ref[here, rows:] = hidden(co_ref[:, there], xo_ref[:, there]).T

    return call(
        body,
        "turn_hidden",
        [(a, "v") for a in (x, x_o, c, c_o)],
        [((part, 2 * rows), BF, "v")],
        mib=6,
        after=after,
        us=1.8,
        carry=carry,
    )


def fill(at_ref, both, refs):
    if len(refs) == 2:
        rows = refs[0].shape[0]
        both[:rows, :] = refs[0][...]
        both[rows:, :] = refs[1][...]
        return
    each = refs[0].shape[0]
    bit = at_ref[1] & 1
    for i, (keep, other) in enumerate((refs[:2], refs[2:])):
        both[at_block(2 * i + bit, each), :] = keep[...]
        both[at_block(2 * i + 1 - bit, each), :] = other[...]


def factor_grad(name, s, half, turned, p, so_far, placed=None, after=(), ahead=()):
    rows2, rank = turned.shape[1], p[0].shape[1]
    part = half // 2
    tw = min(512, part // 2)
    n = part // tw
    far = turned.shape[0] == half
    np_ = len(p)
    recv, full = placed or ((), None)
    nr = len(recv)
    ins = [(turned, "h" if far else "v")] + [(a, "v") for a in p]
    aliases = {}
    if so_far is not None:
        aliases[len(ins)] = 0
        ins.append((so_far, "h"))
    if placed:
        ins += [(a, "v") for a in recv]
        aliases[len(ins)] = 1
        ins.append((full, "h"))

    def body(at_ref, t_ref, *refs, fetch=nothing):
        p_refs, refs = refs[:np_], refs[np_ + (so_far is not None) :]
        r_refs, refs = refs[:nr], refs[nr + (nr > 0) :]
        o_ref, refs = refs[0], refs[1:]
        if nr:
            f_ref, refs = refs[0], refs[1:]
        stage, both, sems, put_sem, *refs = refs

        def left_copy(k):
            src = t_ref.at[pl.ds(pl.multiple_of(s * part + k * tw, tw), tw), :]
            return copy(src, refs[0].at[at_block(k, tw), :], refs[1].at[k])

        def put(i):
            w = recv[i].shape[1]
            there = pl.ds(pl.multiple_of((1 - at_ref[0]) * half + i * w, w), w)
            return copy(r_refs[i], f_ref.at[:, there], put_sem.at[i])

        def out(k, slot):
            there = pl.ds(pl.multiple_of(s * part + k * tw, tw), tw)
            return copy(stage.at[slot], o_ref.at[there, :], sems.at[slot])

        if far:
            for k in range(n):
                left_copy(k).start()
        for i in range(nr):
            put(i).start()
        fetch()
        fill(at_ref, both, p_refs)

        @pl.loop(0, n // 2)
        def _(kk):
            if far:
                left_copy(2 * kk).wait()
                left_copy(2 * kk + 1).wait()

            @pl.when(kk >= 1)
            def _():
                out(2 * kk - 2, 0).wait()
                out(2 * kk - 1, 1).wait()

            for i in range(2):
                k = 2 * kk + i
                left = refs[0][at_block(k, tw), :] if far else t_ref[at_block(k, tw), :]
                stage[i] = jnp.dot(left, both[...], preferred_element_type=F32).astype(BF)
                out(k, i).start()

        for i in range(2):
            out(n - 2 + i, i).wait()
        for i in range(nr):
            put(i).wait()

    outs = [((half, rank), BF, "h")] + ([(full.shape, BF, "h")] if placed else [])
    return call(
        body,
        name,
        ins,
        outs,
        [pltpu.VMEM((2, tw, rank), BF), pltpu.VMEM((rows2, rank), BF), dma(2), dma(max(1, nr))]
        + ([pltpu.VMEM((part, rows2), BF), dma(n)] if far else []),
        flops=rows2 * half * rank,
        aliases=aliases,
        mib=16 if far else 12,
        after=after,
        ahead=ahead,
    )


def expand(s, u, u_first, p, after=(), ahead=()):
    half, rank = u.shape
    rows2 = sum(a.shape[0] for a in p)
    part = half // 2
    tw = u_first.shape[0]
    n = part // tw

    def body(at_ref, u_ref, uf_ref, *refs, fetch=nothing):
        o_ref, uv, both, u_sem = refs[len(p) :]

        def u_copy(k):
            src = u_ref.at[pl.ds(pl.multiple_of(s * part + k * tw, tw), tw), :]
            return copy(src, uv.at[k - 1], u_sem.at[k - 1])

        for k in range(1, n):
            u_copy(k).start()
        fetch()
        fill(at_ref, both, refs[: len(p)])
        o_ref[:, :tw] = lax.dot_general(both[...], uf_ref[...], NT, preferred_element_type=F32)

        @pl.loop(1, n)
        def _(k):
            u_copy(k).wait()
            o_ref[:, at_block(k, tw)] = lax.dot_general(both[...], uv[k - 1], NT, preferred_element_type=F32)

    return call(
        body,
        "expand",
        [(u, "h"), (u_first, "v")] + [(a, "v") for a in p],
        [((rows2, part), F32, "v")],
        [pltpu.VMEM((max(1, n - 1), tw, rank), BF), pltpu.VMEM((rows2, rank), BF), dma(max(1, n - 1))],
        flops=rows2 * half * rank,
        mib=11,
        after=after,
        ahead=ahead,
    )


def input_grad(s, c, c_o, ex, v, v_first, bias, g, so_far, width, after=(), ahead=()):
    rows, half = c_o.shape
    rank = v.shape[1]
    part = half // 2
    tw = v_first.shape[0]
    n = part // tw
    slots = max(1, min(2, n - 1))
    ng = len(g)

    def body(at_ref, c_ref, co_ref, ex_ref, v_ref, vf_ref, b_ref, *refs, fetch=nothing):
        g_refs, refs = refs[:ng], refs[ng + (so_far is not None) :]
        own_ref, oth_ref, stage, vv, both, sems, v_sem = refs

        def v_copy(k):
            src = v_ref.at[pl.ds(pl.multiple_of(s * part + k * tw, tw), tw), :]
            slot = lax.rem(k - 1, slots)
            return copy(src, vv.at[slot], v_sem.at[slot])

        def columns(k):
            return pl.ds(pl.multiple_of(at_ref[0] * half + s * part + k * tw, tw), tw)

        def out(k):
            slot = lax.rem(k, 2)
            return copy(stage.at[slot], own_ref.at[:, columns(k)], sems.at[slot])

        def block(k, v_block):
            here = at_block(k, tw)
            there = pl.ds(pl.multiple_of(s * part + k * tw, tw), tw)
            bk = lax.dot_general(both[...], v_block, NT, preferred_element_type=F32)
            b = b_ref[:, columns(k)].astype(F32)
            cf, cof = c_ref[:, here].astype(F32), co_ref[:, there].astype(F32)
            stage[lax.rem(k, 2)] = (cf * (ex_ref[:rows, here] + b) + cf + bk[:rows]).astype(BF)
            oth_ref[:, here] = (cof * (ex_ref[rows:, here] + b) + cof + bk[rows:]).astype(BF)
            out(k).start()

        for k in range(1, min(n, slots + 1)):
            v_copy(k).start()
        fetch()
        fill(at_ref, both, g_refs)
        block(0, vf_ref[...])

        @pl.loop(1, n)
        def _(k):
            v_copy(k).wait()

            @pl.when(k >= 2)
            def _():
                out(k - 2).wait()

            block(k, vv[lax.rem(k - 1, slots)])

            @pl.when(k + slots < n)
            def _():
                v_copy(k + slots).start()

        for k in range(max(0, n - 2), n):
            out(k).wait()

    ins = [(c, "v"), (c_o, "v"), (ex, "v"), (v, "h"), (v_first, "v"), (bias, "v")] + [(a, "v") for a in g]
    aliases = {}
    if so_far is not None:
        aliases = {len(ins): 0}
        ins.append((so_far, "h"))
    return call(
        body,
        "input_grad",
        ins,
        [((rows, width), BF, "h"), ((rows, part), BF, "v")],
        [
            pltpu.VMEM((2, rows, tw), BF),
            pltpu.VMEM((slots, tw, rank), BF),
            pltpu.VMEM((2 * rows, rank), BF),
            dma(2),
            dma(slots),
        ],
        flops=2 * rows * half * rank,
        aliases=aliases,
        mib=14,
        after=after,
        ahead=ahead,
    )


def plus(a, b):
    return a.astype(F32) + b.astype(F32)


def pair_halves(a, b, direct, after=()):
    rows, rank = a.shape

    def body(at_ref, a_ref, b_ref, *outs):
        write_halves(at_ref, lambda here: plus(a_ref[here, :], b_ref[here, :]), outs)

    return call(body, "pair_halves", [(a, "v"), (b, "v")], halves_of(rows, rank, direct), after=after)


def pieces_of(a, b, m, after=(), carry=()):
    rows, rank = a.shape
    each = rows // m

    def body(at_ref, a_ref, b_ref, *outs):
        for d in range(m):
            here = at_block((at_ref[1] >> 1) ^ d, each)
            outs[d][...] = plus(a_ref[here, :], b_ref[here, :]).astype(BF)

    return call(body, "pieces_of", [(a, "v"), (b, "v")], [((each, rank), BF, "v")] * m, after=after, carry=carry)


def add_pieces(parts, after=(), carry=()):
    def body(at_ref, *refs):
        total = refs[0][...].astype(F32)
        for r in refs[1:-1]:
            total += r[...].astype(F32)
        refs[-1][...] = total.astype(BF)

    return call(body, "add_pieces", [(a, "v") for a in parts], [(parts[0].shape, BF, "v")], after=after, carry=carry)


def join_pieces(parts, after=()):
    m = len(parts)
    each, rank = parts[0].shape

    def body(at_ref, *refs):
        for d in range(m):
            refs[-1][at_block((at_ref[1] >> 1) ^ d, each), :] = refs[d][...]

    return call(body, "join_pieces", [(a, "v") for a in parts], [((m * each, rank), BF, "v")], after=after)[0]


def hold(a, after):
    def body(at_ref, a_ref, o_ref):
        pass

    return call(body, "hold", [(a, "v")], [(a.shape, a.dtype, "v")], aliases={0: 0}, after=after, mib=9)[0]


def solution(mesh):
    n = mesh.shape["col"]
    m = n // 2
    swap = [(0, 1), (1, 0)]

    def trade(a):
        return lax.ppermute(a, "batch", swap)

    def to(a, d):
        return lax.ppermute(a, "col", [(i, i ^ d) for i in range(n)])

    def spread(parts):
        return [parts[0]] + [to(parts[d], 2 * d) for d in range(1, m)]

    def local(x, c, u, v, bias):
        half, width = u.shape[0], x.shape[1]
        direct = x.shape[0] % (16 * n) == 0 and n & (n - 1) == 0 and n > 2

        def plain(total):
            total = lax.psum(total, "col").astype(BF)
            return [trade(total), total]

        part = half // 2
        tw = min(1024, part)
        x_s = cut_half(x, half)
        x_o = trade(x_s)
        own, x_own, c_s, *v_in = project_own(x, v, c, [x_s])
        theirs = trade(own)
        c_o = trade(hold(c_s, [theirs]))
        sums = project_other(x_o, v_in, theirs, direct)
        c0, u0 = fetch_first(c, u, [sums[0]])
        acc, b0, c1, u1 = back_project(0, x_own, x_o, c0, c_o, u, u0, None, c)
        if direct:
            parts = pieces_of(sums[0], to(sums[1], 1), m, [acc])
            own_g, mine_g, b1 = back_project(1, x_own, x_o, c1, c_o, u, u1, acc, after=[parts[0]])
            total, own_g = add_pieces(spread(parts), carry=[own_g])
            (h_t0,) = turn_hidden(0, x_own, x_o, c0, c_o, [total])
            sums_g = pair_halves(mine_g, trade(own_g), direct, [h_t0])
            (h_t1,) = turn_hidden(1, x_own, x_o, c1, c_o, [sums_g[0]])
            half_p = join_pieces(spread([total] * m), [h_t1])
            other_p = to(half_p, 1)
            x_t = turn_x(x_own, x_o, [half_p])
            other_p = hold(other_p, [(x_t, "h")])
            p = [trade(half_p), trade(other_p), half_p, other_p]
            (grad_u,) = factor_grad("u_grad", 0, half, h_t0, p, None, after=[(x_t, "h")])
            parts_g = pieces_of(sums_g[0], to(sums_g[1], 1), m, [(grad_u, "h")])
            grad_u, u0 = factor_grad("u_grad", 1, half, h_t1, p, grad_u, after=[parts_g[0]], ahead=[(u, 0, tw)])
            (total_g,) = add_pieces(spread(parts_g), [(grad_u, "h")])
            ex0, u1 = expand(0, u, u0, p, [total_g], [(u, part, tw)])
            half_g = join_pieces(spread([total_g] * m), [ex0])
            other_g = to(half_g, 1)
            ex1, v0 = expand(1, u, u1, p, [half_g], [(v, 0, tw)])
            other_g = hold(other_g, [ex1])
            g = [trade(half_g), trade(other_g), half_g, other_g]
        else:
            own_g, mine_g, b1 = back_project(1, x_own, x_o, c1, c_o, u, u1, acc)
            (sums_g,) = pair_halves(mine_g, trade(own_g), direct)
            p, g = plain(sums[0]), plain(sums_g)
            x_t = turn_x(x_own, x_o)
            (h_t0,) = turn_hidden(0, x_own, x_o, c0, c_o)
            (h_t1,) = turn_hidden(1, x_own, x_o, c1, c_o)
            (grad_u,) = factor_grad("u_grad", 0, half, h_t0, p, None)
            grad_u, u0 = factor_grad("u_grad", 1, half, h_t1, p, grad_u, ahead=[(u, 0, tw)])
            ex0, u1 = expand(0, u, u0, p, ahead=[(u, part, tw)])
            ex1, v0 = expand(1, u, u1, p, ahead=[(v, 0, tw)])
        bias = bias[None, :]
        out, oth0, v1 = input_grad(0, c0, c_o, ex0, v, v0, bias, g, None, width, [ex1], [(v, part, tw)])
        out, oth1 = input_grad(1, c1, c_o, ex1, v, v1, bias, g, out, width)
        back = [trade(oth0), trade(oth1)]
        (grad_v,) = factor_grad("v_grad", 0, half, x_t, g, None, after=[oth1])
        grad_v, out = factor_grad("v_grad", 1, half, x_t, g, grad_v, (back, out))
        return out, grad_u, grad_v, jnp.concatenate([b0[0], b1[0]])

    return jax.shard_map(
        local,
        mesh=mesh,
        in_specs=(
            P(("group", "batch"), "col"),
            P(("group", "batch"), "col"),
            P(("col", "batch"), None),
            P(("col", "batch"), None),
            P("col"),
        ),
        out_specs=(
            P(("group", "batch"), "col"),
            P(("group", "col", "batch"), None),
            P(("group", "col", "batch"), None),
            P(("group", "col", "batch")),
        ),
        check_vma=False,
    )
```

profile of v0, /device:TPU:0, one launch (start us, length us, event | category | flops | bytes accessed | tf_op | source)
XLA Modules:
  0.0 144.5 jit_solution(8974774155559932122)
XLA Ops:
  0.6 2.2 %cut_half.1.refs_3_ = bf16[256,8192]{1,0:T(8,128)(2,1)S(1)} custom-call(bf16[256,16384]{1,0:T(8,128)(2,1)} %refs_0_.6), custom_call_target="tpu_custom_call" | custom-call | flops 2529999872 | tf_op jit(solution)/shard_map/cut_half/pallas_call | solution.py:41
  2.9 0.5 collective-permute-start
  3.4 9.1 %project_own.1 = (bf16[256,1024]{1,0:T(8,128)(2,1)S(1)}, bf16[256,8192]{1,0:T(8,128)(2,1)S(1)}, bf16[256,8192]{1,0:T(8,128)(2,1)S(1)}, bf16[2048,1024]{1,0:T(8,1...) custom-call(bf16[256,16384]{1,0:T(8,128)(2,1)} %refs_0_.6, ...), custom_call_target="tpu_custom_call" | custom-call | flops 7646444544 | tf_op jit(solution)/shard_map/project_own/pallas_call | solution.py:41
  12.5 0.1 collective-permute-start.1
  12.6 1.9 %collective-permute-done.1.refs_1_ = bf16[256,1024]{1,0:T(8,128)(2,1)S(1)} collective-permute-done((bf16[256,1024]{1,0:T(8,128)(2,1)S(1)}, bf16[256,1024]{1,0:T(8,128)(2,1)S(1)}, u32[]{:S(2)}, u32[]{:S(2)}) %collective-permute-start.1) | collective-permute-done | bytes 524320 | tf_op jit(solution)/shard_map/ppermute | solution.py:619
  14.5 0.1 collective-permute-start.3
  14.6 5.8 %project_other.1 = (bf16[128,1024]{1,0:T(8,128)(2,1)S(1)}, bf16[128,1024]{1,0:T(8,128)(2,1)S(1)}) custom-call(bf16[256,8192]{1,0:T(8,128)(2,1)S(1)} %collective-permute-done.refs_0_.refs_1_, bf16[256,1024]{1,0:T(8,128)(2,1)S(1)} %collective-permute-done.1.refs_1_, bf16[2048,1024]{1,0:T(8,128)(2,1)S(1)} %get-tuple-element.49.refs_2_, ...), custom_call_target="tpu_custom_call" | custom-call | flops 7646444544 | tf_op jit(solution)/shard_map/project_other/pallas_call | solution.py:41
  20.4 2.9 %collective-permute-start.2 = (bf16[128,1024]{1,0:T(8,128)(2,1)S(1)}, bf16[128,1024]{1,0:T(8,128)(2,1)S(1)}, u32[]{:S(2)}, u32[]{:S(2)}) collective-permute-start(bf16[128,1024]{1,0:T(8,128)(2,1)S(1)} %get-tuple-element.54), channel_id=1, source_target_pairs={{0,2},{2,0},{4,6},{6,4},{8,10},{10,8},{12,14},{14,12},{1,3},{3,1},... | collective-permute-start | bytes 786440 | tf_op jit(solution)/shard_map/ppermute | solution.py:622
  23.4 2.9 %fetch_first.1 = (bf16[256,4096]{1,0:T(8,128)(2,1)S(1)}, bf16[2048,1024]{1,0:T(8,128)(2,1)S(1)}) custom-call(bf16[256,16384]{1,0:T(8,128)(2,1)} %refs_6_.4, bf16[8192,1024]{1,0:T(8,128)(2,1)} %refs_0_.9, bf16[128,1024]{1,0:T(8,128)(2,1)S(1)} %get-tuple-element.53.refs_2_.refs_0_), custom_call_target="tpu_custom_call" | custom-call | flops 3220000000 | tf_op jit(solution)/shard_map/fetch_first/pallas_call | solution.py:41
  26.3 6.9 %back_project.2 = (f32[512,1024]{1,0:T(8,128)S(1)}, f32[1,4096]{1,0:T(1,128)S(1)}, bf16[256,4096]{1,0:T(8,128)(2,1)S(1)}, bf16[2048,1024]{1,0:T(8,128)(2,1)S(1)}) custom-call(bf16[256,8192]{1,0:T(8,128)(2,1)S(1)} %get-tuple-element.47.refs_0_, bf16[256,8192]{1,0:T(8,128)(2,1)S(1)} %collective-permute-done.refs_0_.refs_1_, ...), custom_call_target="tpu_custom_call" | custom-call | flops 7646444544 | tf_op jit(solution)/shard_map/back_project/pallas_call | solution.py:41
  33.2 0.1 pieces_of.2
  33.2 1.7 %collective-permute-start.4 = (bf16[32,1024]{1,0:T(8,128)(2,1)S(1)}, bf16[32,1024]{1,0:T(8,128)(2,1)S(1)}, u32[]{:S(2)}, u32[]{:S(2)}) collective-permute-start(bf16[32,1024]{1,0:T(8,128)(2,1)S(1)} %get-tuple-element.60), channel_id=1, source_target_pairs={{0,4},{2,6},{4,0},{6,2},{8,12},{10,14},{12,8},{14,10},{1,5},{3,7},... | collective-permute-start | bytes 196616 | tf_op jit(solution)/shard_map/ppermute | solution.py:622
  34.9 2.6 %collective-permute-start.5 = (bf16[32,1024]{1,0:T(8,128)(2,1)S(1)}, bf16[32,1024]{1,0:T(8,128)(2,1)S(1)}, u32[]{:S(2)}, u32[]{:S(2)}) collective-permute-start(bf16[32,1024]{1,0:T(8,128)(2,1)S(1)} %get-tuple-element.61), channel_id=1, source_target_pairs={{0,8},{2,10},{4,12},{6,14},{8,0},{10,2},{12,4},{14,6},{1,9},{3,11}... | collective-permute-start | bytes 196616 | tf_op jit(solution)/shard_map/ppermute | solution.py:622
  37.5 0.2 collective-permute-start.6
  37.7 7.0 %back_project.3 = (bf16[256,1024]{1,0:T(8,128)(2,1)S(1)}, f32[256,1024]{1,0:T(8,128)S(1)}, f32[1,4096]{1,0:T(1,128)S(1)}) custom-call(bf16[256,8192]{1,0:T(8,128)(2,1)S(1)} %get-tuple-element.47.refs_0_, bf16[256,8192]{1,0:T(8,128)(2,1)S(1)} %collective-permute-done.refs_0_.refs_1_, bf16[256,4096]{1,0:T(8,128)(2,1)S(1)} %get-tuple-element.63.refs_2_.refs_0_, ...), custom_call_target="tpu_custom_call" | custom-call | flops 7646444544 | tf_op jit(solution)/shard_map/back_project/pallas_call | solution.py:41
  44.7 0.1 collective-permute-start.10
  44.8 3.7 %collective-permute-start.9 = (bf16[32,1024]{1,0:T(8,128)(2,1)S(1)}, bf16[32,1024]{1,0:T(8,128)(2,1)S(1)}, u32[]{:S(2)}, u32[]{:S(2)}) collective-permute-start(bf16[32,1024]{1,0:T(8,128)(2,1)S(1)} %get-tuple-element.66.refs_4_.refs_0_), channel_id=1, source_target_pairs={{0,12},{2,14},{4,8},{6,10},{8,4},{10,6},{12,0},{14,2},{1,13},{3,15... | collective-permute-start | bytes 196616 | tf_op jit(solution)/shard_map/ppermute | solution.py:622
  48.5 0.8 collective-permute-start.7
  49.3 1.6 %turn_hidden.2.refs_2_.refs_0_ = bf16[4096,512]{1,0:T(8,128)(2,1)S(1)} custom-call(bf16[256,8192]{1,0:T(8,128)(2,1)S(1)} %get-tuple-element.47.refs_0_, bf16[256,8192]{1,0:T(8,128)(2,1)S(1)} %collective-permute-done.refs_0_.refs_1_, bf16[256,4096]{1,0:T(8,128)(2,1)S(1)} %get-tuple-element.55.refs_2_.refs_0_, ...), custom_call_target="tpu_custom_call" | custom-call | flops 2070000000 | tf_op jit(solution)/shard_map/turn_hidden/pallas_call | solution.py:41
  50.9 0.1 pair_halves.1
  51.0 1.7 %turn_hidden.3.refs_4_.refs_0_ = bf16[4096,512]{1,0:T(8,128)(2,1)S(1)} custom-call(bf16[256,8192]{1,0:T(8,128)(2,1)S(1)} %get-tuple-element.47.refs_0_, bf16[256,8192]{1,0:T(8,128)(2,1)S(1)} %collective-permute-done.refs_0_.refs_1_, bf16[256,4096]{1,0:T(8,128)(2,1)S(1)} %get-tuple-element.63.refs_2_.refs_0_, ...), custom_call_target="tpu_custom_call" | custom-call | flops 2070000000 | tf_op jit(solution)/shard_map/turn_hidden/pallas_call | solution.py:41
  52.7 1.4 collective-permute-done.8.refs_2_
  54.1 0.1 collective-permute-done.7.refs_1_
  54.3 0.5 collective-permute-start.13
  54.8 8.2 %turn_x.1.refs_1_.refs_5_.refs_0_ = bf16[8192,512]{1,0:T(8,128)(2,1)} custom-call(bf16[256,8192]{1,0:T(8,128)(2,1)S(1)} %get-tuple-element.47.refs_0_, bf16[256,8192]{1,0:T(8,128)(2,1)S(1)} %collective-permute-done.refs_0_.refs_1_, bf16[128,1024]{1,0:T(8,128)(2,1)S(1)} %join_pieces.2.refs_2_.refs_3_.refs_4_), custom_call_target="tpu_custom_call" | custom-call | flops 4140000000 | tf_op jit(solution)/shard_map/turn_x/pallas_call | solution.py:41
  63.1 0.6 collective-permute-start.14
  63.6 1.5 %collective-permute-start.11 = (bf16[128,1024]{1,0:T(8,128)(2,1)S(1)}, bf16[128,1024]{1,0:T(8,128)(2,1)S(1)}, u32[]{:S(2)}, u32[]{:S(2)}) collective-permute-start(bf16[128,1024]{1,0:T(8,128)(2,1)S(1)} %get-tuple-element.70), channel_id=1, source_target_pairs={{0,2},{2,0},{4,6},{6,4},{8,10},{10,8},{12,14},{14,12},{1,3},{3,1},... | collective-permute-start | bytes 786440 | tf_op jit(solution)/shard_map/ppermute | solution.py:622
  65.2 9.0 %u_grad.2.refs_2_.refs_5_ = bf16[8192,1024]{1,0:T(8,128)(2,1)} custom-call(bf16[4096,512]{1,0:T(8,128)(2,1)S(1)} %turn_hidden.2.refs_2_.refs_0_, bf16[128,1024]{1,0:T(8,128)(2,1)S(1)} %collective-permute-done.12.refs_1_.refs_2_, bf16[128,1024]{1,0:T(8,128)(2,1)S(1)} %collective-permute-done.14.refs_2_.refs_3_, ...), custom_call_target="tpu_custom_call" | custom-call | flops 7646444544 | tf_op jit(solution)/shard_map/u_grad/pallas_call | solution.py:41
  74.2 0.1 pieces_of.3
  74.3 1.6 %collective-permute-start.15 = (bf16[32,1024]{1,0:T(8,128)(2,1)S(1)}, bf16[32,1024]{1,0:T(8,128)(2,1)S(1)}, u32[]{:S(2)}, u32[]{:S(2)}) collective-permute-start(bf16[32,1024]{1,0:T(8,128)(2,1)S(1)} %get-tuple-element.72), channel_id=1, source_target_pairs={{0,4},{2,6},{4,0},{6,2},{8,12},{10,14},{12,8},{14,10},{1,5},{3,7},... | collective-permute-start | bytes 196616 | tf_op jit(solution)/shard_map/ppermute | solution.py:622
  75.9 1.5 %collective-permute-start.16 = (bf16[32,1024]{1,0:T(8,128)(2,1)S(1)}, bf16[32,1024]{1,0:T(8,128)(2,1)S(1)}, u32[]{:S(2)}, u32[]{:S(2)}) collective-permute-start(bf16[32,1024]{1,0:T(8,128)(2,1)S(1)} %get-tuple-element.73), channel_id=1, source_target_pairs={{0,8},{2,10},{4,12},{6,14},{8,0},{10,2},{12,4},{14,6},{1,9},{3,11}... | collective-permute-start | bytes 196616 | tf_op jit(solution)/shard_map/ppermute | solution.py:622
  77.4 1.4 collective-permute-start.17
  78.8 9.0 %u_grad.3 = (bf16[8192,1024]{1,0:T(8,128)(2,1)}, bf16[1024,1024]{1,0:T(8,128)(2,1)S(1)}) custom-call(bf16[4096,512]{1,0:T(8,128)(2,1)S(1)} %turn_hidden.3.refs_4_.refs_0_, bf16[128,1024]{1,0:T(8,128)(2,1)S(1)} %collective-permute-done.12.refs_1_.refs_2_, ...), custom_call_target="tpu_custom_call", output_to_operand_aliasing={{0}: (5, {})} | custom-call | flops 7646444544 | tf_op jit(solution)/shard_map/u_grad/pallas_call | solution.py:41
  87.9 2.5 %collective-permute-start.20 = (bf16[32,1024]{1,0:T(8,128)(2,1)S(1)}, bf16[32,1024]{1,0:T(8,128)(2,1)S(1)}, u32[]{:S(2)}, u32[]{:S(2)}) collective-permute-start(bf16[32,1024]{1,0:T(8,128)(2,1)S(1)} %add_pieces.3.refs_7_.refs_0_), channel_id=1, source_target_pairs={{0,12},{2,14},{4,8},{6,10},{8,4},{10,6},{12,0},{14,2},{1,13},{3,15... | collective-permute-start | bytes 196616 | tf_op jit(solution)/shard_map/ppermute | solution.py:622
  90.4 1.9 %collective-permute-start.18 = (bf16[32,1024]{1,0:T(8,128)(2,1)S(1)}, bf16[32,1024]{1,0:T(8,128)(2,1)S(1)}, u32[]{:S(2)}, u32[]{:S(2)}) collective-permute-start(bf16[32,1024]{1,0:T(8,128)(2,1)S(1)} %add_pieces.3.refs_7_.refs_0_), channel_id=1, source_target_pairs={{0,4},{2,6},{4,0},{6,2},{8,12},{10,14},{12,8},{14,10},{1,5},{3,7},... | collective-permute-start | bytes 196616 | tf_op jit(solution)/shard_map/ppermute | solution.py:622
  92.3 6.4 %expand.2 = (f32[512,4096]{1,0:T(8,128)S(1)}, bf16[1024,1024]{1,0:T(8,128)(2,1)S(1)}) custom-call(bf16[8192,1024]{1,0:T(8,128)(2,1)} %refs_0_.9, bf16[1024,1024]{1,0:T(8,128)(2,1)S(1)} %get-tuple-element.76.refs_1_, bf16[128,1024]{1,0:T(8,128)(2,1)S(1)} %collective-permute-done.12.refs_1_.refs_2_, ...), custom_call_target="tpu_custom_call" | custom-call | flops 7646444544 | tf_op jit(solution)/shard_map/expand/pallas_call | solution.py:41
  98.8 1.2 collective-permute-start.22
  100.1 6.6 %expand.3 = (f32[512,4096]{1,0:T(8,128)S(1)}, bf16[1024,1024]{1,0:T(8,128)(2,1)S(1)}) custom-call(bf16[8192,1024]{1,0:T(8,128)(2,1)} %refs_0_.9, bf16[1024,1024]{1,0:T(8,128)(2,1)S(1)} %get-tuple-element.78.refs_1_, bf16[128,1024]{1,0:T(8,128)(2,1)S(1)} %collective-permute-done.12.refs_1_.refs_2_, ...), custom_call_target="tpu_custom_call" | custom-call | flops 7646444544 | tf_op jit(solution)/shard_map/expand/pallas_call | solution.py:41
  106.7 0.6 collective-permute-start.23
  107.3 0.2 copy-done
  107.5 0.9 collective-permute-done.23.refs_7_.refs_2_
  108.4 6.8 %input_grad.2 = (bf16[256,16384]{1,0:T(8,128)(2,1)}, bf16[256,4096]{1,0:T(8,128)(2,1)S(1)}, bf16[1024,1024]{1,0:T(8,128)(2,1)S(1)}) custom-call(bf16[256,4096]{1,0:T(8,128)(2,1)S(1)} %get-tuple-element.55.refs_2_.refs_0_, bf16[256,8192]{1,0:T(8,128)(2,1)S(1)} %collective-permute-done.3.refs_3_.refs_1_, f32[512,4096]{1,0:T(8,128)S(1)} %get-tuple-element.77.refs_4_.refs_2_, ...), custom_call_target="tpu_custom_call" | custom-call | flops 7646444544 | tf_op jit(solution)/shard_map/input_grad/pallas_call | solution.py:41
  115.2 6.7 %input_grad.3 = (bf16[256,16384]{1,0:T(8,128)(2,1)}, bf16[256,4096]{1,0:T(8,128)(2,1)S(1)}) custom-call(bf16[256,4096]{1,0:T(8,128)(2,1)S(1)} %get-tuple-element.63.refs_2_.refs_0_, bf16[256,8192]{1,0:T(8,128)(2,1)S(1)} %collective-permute-done.3.refs_3_.refs_1_, ...), custom_call_target="tpu_custom_call", output_to_operand_aliasing={{0}: (10, {})} | custom-call | flops 7646444544 | tf_op jit(solution)/shard_map/input_grad/pallas_call | solution.py:41
  121.9 0.4 collective-permute-start.25
  122.4 0.1 collective-permute-start.24
  122.5 0.6 pad_maximum_fusion
  123.1 10.2 %v_grad.2.refs_5_ = bf16[8192,1024]{1,0:T(8,128)(2,1)} custom-call(bf16[8192,512]{1,0:T(8,128)(2,1)} %turn_x.1.refs_1_.refs_5_.refs_0_, bf16[128,1024]{1,0:T(8,128)(2,1)S(1)} %collective-permute-done.21.refs_6_.refs_1_, bf16[128,1024]{1,0:T(8,128)(2,1)S(1)} %collective-permute-done.23.refs_7_.refs_2_, ...), custom_call_target="tpu_custom_call" | custom-call | flops 7646444544 | tf_op jit(solution)/shard_map/v_grad/pallas_call | solution.py:41
  133.4 10.9 %v_grad.3 = (bf16[8192,1024]{1,0:T(8,128)(2,1)}, bf16[256,16384]{1,0:T(8,128)(2,1)}) custom-call(bf16[8192,512]{1,0:T(8,128)(2,1)} %turn_x.1.refs_1_.refs_5_.refs_0_, bf16[128,1024]{1,0:T(8,128)(2,1)S(1)} %collective-permute-done.21.refs_6_.refs_1_, ...), custom_call_target="tpu_custom_call", output_to_operand_aliasing={{0}: (5, {}), {1}: (8, {})} | custom-call | flops 7646444544 | tf_op jit(solution)/shard_map/v_grad/pallas_call | solution.py:41
  (35 shorter events, 0.2 us)
Async XLA Ops:
  2.9 11.8 %collective-permute-start = (bf16[256,8192]{1,0:T(8,128)(2,1)S(1)}, bf16[256,8192]{1,0:T(8,128)(2,1)S(1)}, u32[]{:S(2)}, u32[]{:S(2)}) collective-permute-start(bf16[256,8192]{1,0:T(8,128)(2,1)S(1)} %cut_half.1.refs_3_), channel_id=1, source_target_pairs={{0,1},{1,0},{2,3},{3,2},{4,5},{5,4},{6,7},{7,6},{8,9},{9,8},{10,11... | collective-permute-start | bytes 12582920 | tf_op jit(solution)/shard_map/ppermute | solution.py:619
  12.5 2.0 %collective-permute-start.1 = (bf16[256,1024]{1,0:T(8,128)(2,1)S(1)}, bf16[256,1024]{1,0:T(8,128)(2,1)S(1)}, u32[]{:S(2)}, u32[]{:S(2)}) collective-permute-start(bf16[256,1024]{1,0:T(8,128)(2,1)S(1)} %get-tuple-element.48), channel_id=1, source_target_pairs={{0,1},{1,0},{2,3},{3,2},{4,5},{5,4},{6,7},{7,6},{8,9},{9,8},{10,11... | collective-permute-start | bytes 1572872 | tf_op jit(solution)/shard_map/ppermute | solution.py:619
  14.5 11.8 %collective-permute-start.3 = (bf16[256,8192]{1,0:T(8,128)(2,1)S(1)}, bf16[256,8192]{1,0:T(8,128)(2,1)S(1)}, u32[]{:S(2)}, u32[]{:S(2)}) collective-permute-start(bf16[256,8192]{1,0:T(8,128)(2,1)S(1)} %hold.3), channel_id=1, source_target_pairs={{0,1},{1,0},{2,3},{3,2},{4,5},{5,4},{6,7},{7,6},{8,9},{9,8},{10,11... | collective-permute-start | bytes 12582920 | tf_op jit(solution)/shard_map/ppermute | solution.py:619
  20.4 12.7 %collective-permute-start.2 = (bf16[128,1024]{1,0:T(8,128)(2,1)S(1)}, bf16[128,1024]{1,0:T(8,128)(2,1)S(1)}, u32[]{:S(2)}, u32[]{:S(2)}) collective-permute-start(bf16[128,1024]{1,0:T(8,128)(2,1)S(1)} %get-tuple-element.54), channel_id=1, source_target_pairs={{0,2},{2,0},{4,6},{6,4},{8,10},{10,8},{12,14},{14,12},{1,3},{3,1},... | collective-permute-start | bytes 786440 | tf_op jit(solution)/shard_map/ppermute | solution.py:622
  33.2 11.4 %collective-permute-start.4 = (bf16[32,1024]{1,0:T(8,128)(2,1)S(1)}, bf16[32,1024]{1,0:T(8,128)(2,1)S(1)}, u32[]{:S(2)}, u32[]{:S(2)}) collective-permute-start(bf16[32,1024]{1,0:T(8,128)(2,1)S(1)} %get-tuple-element.60), channel_id=1, source_target_pairs={{0,4},{2,6},{4,0},{6,2},{8,12},{10,14},{12,8},{14,10},{1,5},{3,7},... | collective-permute-start | bytes 196616 | tf_op jit(solution)/shard_map/ppermute | solution.py:622
  34.9 9.8 %collective-permute-start.5 = (bf16[32,1024]{1,0:T(8,128)(2,1)S(1)}, bf16[32,1024]{1,0:T(8,128)(2,1)S(1)}, u32[]{:S(2)}, u32[]{:S(2)}) collective-permute-start(bf16[32,1024]{1,0:T(8,128)(2,1)S(1)} %get-tuple-element.61), channel_id=1, source_target_pairs={{0,8},{2,10},{4,12},{6,14},{8,0},{10,2},{12,4},{14,6},{1,9},{3,11}... | collective-permute-start | bytes 196616 | tf_op jit(solution)/shard_map/ppermute | solution.py:622
  37.5 7.2 %collective-permute-start.6 = (bf16[32,1024]{1,0:T(8,128)(2,1)S(1)}, bf16[32,1024]{1,0:T(8,128)(2,1)S(1)}, u32[]{:S(2)}, u32[]{:S(2)}) collective-permute-start(bf16[32,1024]{1,0:T(8,128)(2,1)S(1)} %get-tuple-element.62), channel_id=1, source_target_pairs={{0,12},{2,14},{4,8},{6,10},{8,4},{10,6},{12,0},{14,2},{1,13},{3,15... | collective-permute-start | bytes 196616 | tf_op jit(solution)/shard_map/ppermute | solution.py:622
  44.7 6.1 %collective-permute-start.10 = (bf16[256,1024]{1,0:T(8,128)(2,1)S(1)}, bf16[256,1024]{1,0:T(8,128)(2,1)S(1)}, u32[]{:S(2)}, u32[]{:S(2)}) collective-permute-start(bf16[256,1024]{1,0:T(8,128)(2,1)S(1)} %get-tuple-element.68), channel_id=1, source_target_pairs={{0,1},{1,0},{2,3},{3,2},{4,5},{5,4},{6,7},{7,6},{8,9},{9,8},{10,11... | collective-permute-start | bytes 1572872 | tf_op jit(solution)/shard_map/ppermute | solution.py:619
  44.8 7.9 %collective-permute-start.9 = (bf16[32,1024]{1,0:T(8,128)(2,1)S(1)}, bf16[32,1024]{1,0:T(8,128)(2,1)S(1)}, u32[]{:S(2)}, u32[]{:S(2)}) collective-permute-start(bf16[32,1024]{1,0:T(8,128)(2,1)S(1)} %get-tuple-element.66.refs_4_.refs_0_), channel_id=1, source_target_pairs={{0,12},{2,14},{4,8},{6,10},{8,4},{10,6},{12,0},{14,2},{1,13},{3,15... | collective-permute-start | bytes 196616 | tf_op jit(solution)/shard_map/ppermute | solution.py:622
  48.5 5.6 %collective-permute-start.8 = (bf16[32,1024]{1,0:T(8,128)(2,1)S(1)}, bf16[32,1024]{1,0:T(8,128)(2,1)S(1)}, u32[]{:S(2)}, u32[]{:S(2)}) collective-permute-start(bf16[32,1024]{1,0:T(8,128)(2,1)S(1)} %get-tuple-element.66.refs_4_.refs_0_), channel_id=1, source_target_pairs={{0,8},{2,10},{4,12},{6,14},{8,0},{10,2},{12,4},{14,6},{1,9},{3,11}... | collective-permute-start | bytes 196616 | tf_op jit(solution)/shard_map/ppermute | solution.py:622
  48.5 5.7 %collective-permute-start.7 = (bf16[32,1024]{1,0:T(8,128)(2,1)S(1)}, bf16[32,1024]{1,0:T(8,128)(2,1)S(1)}, u32[]{:S(2)}, u32[]{:S(2)}) collective-permute-start(bf16[32,1024]{1,0:T(8,128)(2,1)S(1)} %get-tuple-element.66.refs_4_.refs_0_), channel_id=1, source_target_pairs={{0,4},{2,6},{4,0},{6,2},{8,12},{10,14},{12,8},{14,10},{1,5},{3,7},... | collective-permute-start | bytes 196616 | tf_op jit(solution)/shard_map/ppermute | solution.py:622
  54.3 8.8 %collective-permute-start.13 = (bf16[128,1024]{1,0:T(8,128)(2,1)S(1)}, bf16[128,1024]{1,0:T(8,128)(2,1)S(1)}, u32[]{:S(2)}, u32[]{:S(2)}) collective-permute-start(bf16[128,1024]{1,0:T(8,128)(2,1)S(1)} %join_pieces.2.refs_2_.refs_3_.refs_4_), channel_id=1, source_target_pairs={{0,2},{2,0},{4,6},{6,4},{8,10},{10,8},{12,14},{14,12},{1,3},{3,1},... | collective-permute-start | bytes 786440 | tf_op jit(solution)/shard_map/ppermute | solution.py:622
  54.8 10.4 %collective-permute-start.12 = (bf16[128,1024]{1,0:T(8,128)(2,1)S(1)}, bf16[128,1024]{1,0:T(8,128)(2,1)S(1)}, u32[]{:S(2)}, u32[]{:S(2)}) collective-permute-start(bf16[128,1024]{1,0:T(8,128)(2,1)S(1)} %join_pieces.2.refs_2_.refs_3_.refs_4_), channel_id=1, source_target_pairs={{0,1},{1,0},{2,3},{3,2},{4,5},{5,4},{6,7},{7,6},{8,9},{9,8},{10,11... | collective-permute-start | bytes 786440 | tf_op jit(solution)/shard_map/ppermute | solution.py:619
  63.1 2.1 %collective-permute-start.14 = (bf16[128,1024]{1,0:T(8,128)(2,1)S(1)}, bf16[128,1024]{1,0:T(8,128)(2,1)S(1)}, u32[]{:S(2)}, u32[]{:S(2)}) collective-permute-start(bf16[128,1024]{1,0:T(8,128)(2,1)S(1)} %hold.4.refs_4_.refs_5_), channel_id=1, source_target_pairs={{0,1},{1,0},{2,3},{3,2},{4,5},{5,4},{6,7},{7,6},{8,9},{9,8},{10,11... | collective-permute-start | bytes 786440 | tf_op jit(solution)/shard_map/ppermute | solution.py:619
  63.6 10.6 %collective-permute-start.11 = (bf16[128,1024]{1,0:T(8,128)(2,1)S(1)}, bf16[128,1024]{1,0:T(8,128)(2,1)S(1)}, u32[]{:S(2)}, u32[]{:S(2)}) collective-permute-start(bf16[128,1024]{1,0:T(8,128)(2,1)S(1)} %get-tuple-element.70), channel_id=1, source_target_pairs={{0,2},{2,0},{4,6},{6,4},{8,10},{10,8},{12,14},{14,12},{1,3},{3,1},... | collective-permute-start | bytes 786440 | tf_op jit(solution)/shard_map/ppermute | solution.py:622
  74.3 13.5 %collective-permute-start.15 = (bf16[32,1024]{1,0:T(8,128)(2,1)S(1)}, bf16[32,1024]{1,0:T(8,128)(2,1)S(1)}, u32[]{:S(2)}, u32[]{:S(2)}) collective-permute-start(bf16[32,1024]{1,0:T(8,128)(2,1)S(1)} %get-tuple-element.72), channel_id=1, source_target_pairs={{0,4},{2,6},{4,0},{6,2},{8,12},{10,14},{12,8},{14,10},{1,5},{3,7},... | collective-permute-start | bytes 196616 | tf_op jit(solution)/shard_map/ppermute | solution.py:622
  75.9 11.9 %collective-permute-start.16 = (bf16[32,1024]{1,0:T(8,128)(2,1)S(1)}, bf16[32,1024]{1,0:T(8,128)(2,1)S(1)}, u32[]{:S(2)}, u32[]{:S(2)}) collective-permute-start(bf16[32,1024]{1,0:T(8,128)(2,1)S(1)} %get-tuple-element.73), channel_id=1, source_target_pairs={{0,8},{2,10},{4,12},{6,14},{8,0},{10,2},{12,4},{14,6},{1,9},{3,11}... | collective-permute-start | bytes 196616 | tf_op jit(solution)/shard_map/ppermute | solution.py:622
  77.4 10.4 %collective-permute-start.17 = (bf16[32,1024]{1,0:T(8,128)(2,1)S(1)}, bf16[32,1024]{1,0:T(8,128)(2,1)S(1)}, u32[]{:S(2)}, u32[]{:S(2)}) collective-permute-start(bf16[32,1024]{1,0:T(8,128)(2,1)S(1)} %get-tuple-element.74), channel_id=1, source_target_pairs={{0,12},{2,14},{4,8},{6,10},{8,4},{10,6},{12,0},{14,2},{1,13},{3,15... | collective-permute-start | bytes 196616 | tf_op jit(solution)/shard_map/ppermute | solution.py:622
  87.9 10.9 %collective-permute-start.20 = (bf16[32,1024]{1,0:T(8,128)(2,1)S(1)}, bf16[32,1024]{1,0:T(8,128)(2,1)S(1)}, u32[]{:S(2)}, u32[]{:S(2)}) collective-permute-start(bf16[32,1024]{1,0:T(8,128)(2,1)S(1)} %add_pieces.3.refs_7_.refs_0_), channel_id=1, source_target_pairs={{0,12},{2,14},{4,8},{6,10},{8,4},{10,6},{12,0},{14,2},{1,13},{3,15... | collective-permute-start | bytes 196616 | tf_op jit(solution)/shard_map/ppermute | solution.py:622
  90.4 8.4 %collective-permute-start.19 = (bf16[32,1024]{1,0:T(8,128)(2,1)S(1)}, bf16[32,1024]{1,0:T(8,128)(2,1)S(1)}, u32[]{:S(2)}, u32[]{:S(2)}) collective-permute-start(bf16[32,1024]{1,0:T(8,128)(2,1)S(1)} %add_pieces.3.refs_7_.refs_0_), channel_id=1, source_target_pairs={{0,8},{2,10},{4,12},{6,14},{8,0},{10,2},{12,4},{14,6},{1,9},{3,11}... | collective-permute-start | bytes 196616 | tf_op jit(solution)/shard_map/ppermute | solution.py:622
  90.4 8.4 %collective-permute-start.18 = (bf16[32,1024]{1,0:T(8,128)(2,1)S(1)}, bf16[32,1024]{1,0:T(8,128)(2,1)S(1)}, u32[]{:S(2)}, u32[]{:S(2)}) collective-permute-start(bf16[32,1024]{1,0:T(8,128)(2,1)S(1)} %add_pieces.3.refs_7_.refs_0_), channel_id=1, source_target_pairs={{0,4},{2,6},{4,0},{6,2},{8,12},{10,14},{12,8},{14,10},{1,5},{3,7},... | collective-permute-start | bytes 196616 | tf_op jit(solution)/shard_map/ppermute | solution.py:622
  98.8 7.8 %collective-permute-start.22 = (bf16[128,1024]{1,0:T(8,128)(2,1)S(1)}, bf16[128,1024]{1,0:T(8,128)(2,1)S(1)}, u32[]{:S(2)}, u32[]{:S(2)}) collective-permute-start(bf16[128,1024]{1,0:T(8,128)(2,1)S(1)} %join_pieces.3.refs_7_.refs_8_.refs_3_), channel_id=1, source_target_pairs={{0,2},{2,0},{4,6},{6,4},{8,10},{10,8},{12,14},{14,12},{1,3},{3,1},... | collective-permute-start | bytes 786440 | tf_op jit(solution)/shard_map/ppermute | solution.py:622
  100.1 7.4 %collective-permute-start.21 = (bf16[128,1024]{1,0:T(8,128)(2,1)S(1)}, bf16[128,1024]{1,0:T(8,128)(2,1)S(1)}, u32[]{:S(2)}, u32[]{:S(2)}) collective-permute-start(bf16[128,1024]{1,0:T(8,128)(2,1)S(1)} %join_pieces.3.refs_7_.refs_8_.refs_3_), channel_id=1, source_target_pairs={{0,1},{1,0},{2,3},{3,2},{4,5},{5,4},{6,7},{7,6},{8,9},{9,8},{10,11... | collective-permute-start | bytes 786440 | tf_op jit(solution)/shard_map/ppermute | solution.py:619
  106.7 0.8 copy-start
  106.7 1.7 %collective-permute-start.23 = (bf16[128,1024]{1,0:T(8,128)(2,1)S(1)}, bf16[128,1024]{1,0:T(8,128)(2,1)S(1)}, u32[]{:S(2)}, u32[]{:S(2)}) collective-permute-start(bf16[128,1024]{1,0:T(8,128)(2,1)S(1)} %hold.5.refs_9_.refs_4_), channel_id=1, source_target_pairs={{0,1},{1,0},{2,3},{3,2},{4,5},{5,4},{6,7},{7,6},{8,9},{9,8},{10,11... | collective-permute-start | bytes 786440 | tf_op jit(solution)/shard_map/ppermute | solution.py:619
  121.9 11.4 %collective-permute-start.25 = (bf16[256,4096]{1,0:T(8,128)(2,1)S(1)}, bf16[256,4096]{1,0:T(8,128)(2,1)S(1)}, u32[]{:S(2)}, u32[]{:S(2)}) collective-permute-start(bf16[256,4096]{1,0:T(8,128)(2,1)S(1)} %get-tuple-element.83.refs_5_), channel_id=1, source_target_pairs={{0,1},{1,0},{2,3},{3,2},{4,5},{5,4},{6,7},{7,6},{8,9},{9,8},{10,11... | collective-permute-start | bytes 6291464 | tf_op jit(solution)/shard_map/ppermute | solution.py:619
  122.4 11.0 %collective-permute-start.24 = (bf16[256,4096]{1,0:T(8,128)(2,1)S(1)}, bf16[256,4096]{1,0:T(8,128)(2,1)S(1)}, u32[]{:S(2)}, u32[]{:S(2)}) collective-permute-start(bf16[256,4096]{1,0:T(8,128)(2,1)S(1)} %get-tuple-element.84), channel_id=1, source_target_pairs={{0,1},{1,0},{2,3},{3,2},{4,5},{5,4},{6,7},{7,6},{8,9},{9,8},{10,11... | collective-permute-start | bytes 6291464 | tf_op jit(solution)/shard_map/ppermute | solution.py:619
where the time goes:
time: 145 us; the launch traced here: 144 us
  Pallas kernels  111 us (77%)
  starting transfers between devices  26.6 us (18%)
  waiting for transfers between devices  4.35 us (3%)
    pallas_call x27, Pallas kernels, call(): pl.pallas_call(whole if n_ahead else lambda *refs: body(Place(), *refs[:n...  111 us
    ppermute x16, starting transfers between devices, to(): return lax.ppermute(a, 'col', [(i, i ^ d) for i in range(n)])  24.1 us
  transfers between devices with their start and end apart: 26, of which 4 were waited for; matrix products, arithmetic and copies ran while one was open for 0% of the time, Pallas kernels for 59%

commit v1 on v0

--- a/solution.py
+++ b/solution.py
@@ -158,19 +158,13 @@
 
 def project_other(x_o, vs, theirs, direct):
     rows, half = x_o.shape
-    part, rank = vs[0].shape
-    tk = min(1024, part)
-    each = part // tk
+    tk, rank = vs[0].shape
 
     def body(at_ref, x_ref, t_ref, *refs):
         vv, outs, acc = refs[:VPARTS], refs[VPARTS:-1], refs[-1]
-        acc[...] = t_ref[...].astype(F32)
-        for i in range(VPARTS):
-
-            @pl.loop(0, each)
-            def _(j):
-                acc[...] += jnp.dot(x_ref[:, at_block(i * each + j, tk)], vv[i][at_block(j, tk), :], preferred_element_type=F32)
-
+        for k in range(VPARTS):
+            part = jnp.dot(x_ref[:, k * tk : (k + 1) * tk], vv[k][...], preferred_element_type=F32)
+            acc[...] = part + (acc[...] if k else t_ref[...].astype(F32))
         write_halves(at_ref, lambda here: acc[here, :], outs)
 
     return call(
@@ -180,7 +174,7 @@
         halves_of(rows, rank, direct),
         [pltpu.VMEM((rows, rank), F32)],
         flops=2 * rows * half * rank,
-        mib=8,
+        mib=6,
     )
 
 
@@ -282,23 +276,18 @@
 
     def body(at_ref, x_ref, xo_ref, o_ref, stage, sems):
         def out(k):
-            slot = lax.rem(k, 2)
-            return copy(stage.at[slot], o_ref.at[at_block(k, tw), :], sems.at[slot])
+            here = at_block(k, tw)
+            return copy(stage.at[here, :], o_ref.at[here, :], sems.at[k])
 
         @pl.loop(0, n)
         def _(k):
             here = at_block(k, tw)
-            slot = lax.rem(k, 2)
-
-            @pl.when(k >= 2)
-            def _():
-                out(k).wait()
-
-            stage[slot, :, :rows] = x_ref[:, here].T
-            stage[slot, :, rows:] = xo_ref[:, here].T
+            stage[here, :rows] = x_ref[:, here].T
+            stage[here, rows:] = xo_ref[:, here].T
             out(k).start()
 
-        for k in range(max(0, n - 2), n):
+        @pl.loop(0, n)
+        def _(k):
             out(k).wait()
 
     return call(
@@ -306,9 +295,10 @@
         "turn_x",
         [(x, "v"), (x_o, "v")],
         [((half, 2 * rows), BF, "h")],
-        [pltpu.VMEM((2, tw, 2 * rows), BF), dma(2)],
+        [pltpu.VMEM((half, 2 * rows), BF), dma(n)],
         after=after,
         us=3.6,
+        mib=12,
     )[0]
 
 
@@ -350,14 +340,14 @@
         both[at_block(2 * i + 1 - bit, each), :] = other[...]
 
 
-def factor_grad(name, s, half, turned, p, so_far, placed=None, after=(), ahead=()):
+def factor_grad(name, s, half, turned, p, so_far, placed=None, after=(), ahead=(), work=1):
     rows2, rank = turned.shape[1], p[0].shape[1]
     part = half // 2
     tw = min(512, part // 2)
     n = part // tw
     far = turned.shape[0] == half
     np_ = len(p)
-    recv, full = placed or ((), None)
+    recv, full = ([placed[0]], placed[1]) if placed else ((), None)
     nr = len(recv)
     ins = [(turned, "h" if far else "v")] + [(a, "v") for a in p]
     aliases = {}
@@ -383,10 +373,11 @@
 
         def put(i):
             w = recv[i].shape[1]
-            there = pl.ds(pl.multiple_of((1 - at_ref[0]) * half + i * w, w), w)
+            there = pl.ds(pl.multiple_of((1 - at_ref[0]) * half + s * w, w), w)
             return copy(r_refs[i], f_ref.at[:, there], put_sem.at[i])
 
-        def out(k, slot):
+        def out(k):
+            slot = lax.rem(k, 4)
             there = pl.ds(pl.multiple_of(s * part + k * tw, tw), tw)
             return copy(stage.at[slot], o_ref.at[there, :], sems.at[slot])
 
@@ -404,19 +395,19 @@
                 left_copy(2 * kk).wait()
                 left_copy(2 * kk + 1).wait()
 
-            @pl.when(kk >= 1)
+            @pl.when(kk >= 2)
             def _():
-                out(2 * kk - 2, 0).wait()
-                out(2 * kk - 1, 1).wait()
+                out(2 * kk - 4).wait()
+                out(2 * kk - 3).wait()
 
             for i in range(2):
                 k = 2 * kk + i
                 left = refs[0][at_block(k, tw), :] if far else t_ref[at_block(k, tw), :]
-                stage[i] = jnp.dot(left, both[...], preferred_element_type=F32).astype(BF)
-                out(k, i).start()
-
-        for i in range(2):
-            out(n - 2 + i, i).wait()
+                stage[lax.rem(k, 4)] = jnp.dot(left, both[...], preferred_element_type=F32).astype(BF)
+                out(k).start()
+
+        for k in range(max(0, n - 4), n):
+            out(k).wait()
         for i in range(nr):
             put(i).wait()
 
@@ -426,11 +417,11 @@
         name,
         ins,
         outs,
-        [pltpu.VMEM((2, tw, rank), BF), pltpu.VMEM((rows2, rank), BF), dma(2), dma(max(1, nr))]
+        [pltpu.VMEM((4, tw, rank), BF), pltpu.VMEM((rows2, rank), BF), dma(4), dma(max(1, nr))]
         + ([pltpu.VMEM((part, rows2), BF), dma(n)] if far else []),
-        flops=rows2 * half * rank,
+        flops=work * rows2 * half * rank,
         aliases=aliases,
-        mib=16 if far else 12,
+        mib=18 if far else 12,
         after=after,
         ahead=ahead,
     )
@@ -678,9 +669,9 @@
         bias = bias[None, :]
         out, oth0, v1 = input_grad(0, c0, c_o, ex0, v, v0, bias, g, None, width, [ex1], [(v, part, tw)])
         out, oth1 = input_grad(1, c1, c_o, ex1, v, v1, bias, g, out, width)
-        back = [trade(oth0), trade(oth1)]
-        (grad_v,) = factor_grad("v_grad", 0, half, x_t, g, None, after=[oth1])
-        grad_v, out = factor_grad("v_grad", 1, half, x_t, g, grad_v, (back, out))
+        back0, back1 = trade(oth0), trade(oth1)
+        grad_v, out = factor_grad("v_grad", 0, half, x_t, g, None, (back0, out), work=0)
+        grad_v, out = factor_grad("v_grad", 1, half, x_t, g, grad_v, (back1, out))
         return out, grad_u, grad_v, jnp.concatenate([b0[0], b1[0]])
 
     return jax.shard_map(

time: 145 us -> 132 us (0.910)
  Pallas kernels: 111 us -> 95 us
  waiting for transfers between devices: 4.35 us -> 9.75 us
  starting transfers between devices: 26.6 us -> 24.5 us
    pallas_call x27, Pallas kernels: 111 us -> 95 us  [call(): pl.pallas_call(whole if n_ahead else lambda *refs: body(Place(), *refs[:n...]
    ppermute x16, waiting for transfers between devices: 1.53 us -> 5.94 us  [to(): return lax.ppermute(a, 'col', [(i, i ^ d) for i in range(n)])]
    ppermute x16, starting transfers between devices: 24.1 us -> 22.4 us  [to(): return lax.ppermute(a, 'col', [(i, i ^ d) for i in range(n)])]
  transfers between devices with their start and end apart: 26 -> 26, of which waited for: 4 -> 7; matrix products, arithmetic and copies ran while one was open for 0% -> 0% of each run, Pallas kernels for 59% -> 59%
where the time goes in v1:
time: 132 us; the launch traced here: 131 us
  Pallas kernels  95 us (72%)
  starting transfers between devices  24.5 us (19%)
  waiting for transfers between devices  9.75 us (7%)
    pallas_call x27, Pallas kernels, call(): pl.pallas_call(whole if n_ahead else lambda *refs: body(Place(), *refs[:n...  95 us
    ppermute x16, starting transfers between devices, to(): return lax.ppermute(a, 'col', [(i, i ^ d) for i in range(n)])  22.4 us
    ppermute x16, waiting for transfers between devices, to(): return lax.ppermute(a, 'col', [(i, i ^ d) for i in range(n)])  5.94 us
    ppermute x10, waiting for transfers between devices, trade(): return lax.ppermute(a, 'batch', swap)  3.81 us
  transfers between devices with their start and end apart: 26, of which 7 were waited for; matrix products, arithmetic and copies ran while one was open for 0% of the time, Pallas kernels for 59%

profile of v1, /device:TPU:0, one launch (start us, length us, event | category | flops | bytes accessed | tf_op | source)
XLA Modules:
  0.0 131.2 jit_solution(14983081031537769469)
XLA Ops:
  0.6 2.2 %cut_half.1.refs_3_ = bf16[256,8192]{1,0:T(8,128)(2,1)S(1)} custom-call(bf16[256,16384]{1,0:T(8,128)(2,1)} %refs_0_.6), custom_call_target="tpu_custom_call" | custom-call | flops 2529999872 | tf_op jit(solution)/shard_map/cut_half/pallas_call | solution.py:41
  2.9 0.5 collective-permute-start
  3.4 9.1 %project_own.1 = (bf16[256,1024]{1,0:T(8,128)(2,1)S(1)}, bf16[256,8192]{1,0:T(8,128)(2,1)S(1)}, bf16[256,8192]{1,0:T(8,128)(2,1)S(1)}, bf16[2048,1024]{1,0:T(8,1...) custom-call(bf16[256,16384]{1,0:T(8,128)(2,1)} %refs_0_.6, ...), custom_call_target="tpu_custom_call" | custom-call | flops 7646444544 | tf_op jit(solution)/shard_map/project_own/pallas_call | solution.py:41
  12.5 0.1 collective-permute-start.1
  12.6 1.9 %collective-permute-done.1.refs_1_ = bf16[256,1024]{1,0:T(8,128)(2,1)S(1)} collective-permute-done((bf16[256,1024]{1,0:T(8,128)(2,1)S(1)}, bf16[256,1024]{1,0:T(8,128)(2,1)S(1)}, u32[]{:S(2)}, u32[]{:S(2)}) %collective-permute-start.1) | collective-permute-done | bytes 524320 | tf_op jit(solution)/shard_map/ppermute | solution.py:610
  14.5 0.1 collective-permute-start.3
  14.6 4.6 %project_other.1 = (bf16[128,1024]{1,0:T(8,128)(2,1)S(1)}, bf16[128,1024]{1,0:T(8,128)(2,1)S(1)}) custom-call(bf16[256,8192]{1,0:T(8,128)(2,1)S(1)} %collective-permute-done.refs_0_.refs_1_, bf16[256,1024]{1,0:T(8,128)(2,1)S(1)} %collective-permute-done.1.refs_1_, bf16[2048,1024]{1,0:T(8,128)(2,1)S(1)} %get-tuple-element.51.refs_2_, ...), custom_call_target="tpu_custom_call" | custom-call | flops 7646444544 | tf_op jit(solution)/shard_map/project_other/pallas_call | solution.py:41
  19.3 2.9 %collective-permute-start.2 = (bf16[128,1024]{1,0:T(8,128)(2,1)S(1)}, bf16[128,1024]{1,0:T(8,128)(2,1)S(1)}, u32[]{:S(2)}, u32[]{:S(2)}) collective-permute-start(bf16[128,1024]{1,0:T(8,128)(2,1)S(1)} %get-tuple-element.56), channel_id=1, source_target_pairs={{0,2},{2,0},{4,6},{6,4},{8,10},{10,8},{12,14},{14,12},{1,3},{3,1},... | collective-permute-start | bytes 786440 | tf_op jit(solution)/shard_map/ppermute | solution.py:613
  22.2 2.9 %fetch_first.1 = (bf16[256,4096]{1,0:T(8,128)(2,1)S(1)}, bf16[2048,1024]{1,0:T(8,128)(2,1)S(1)}) custom-call(bf16[256,16384]{1,0:T(8,128)(2,1)} %refs_6_.4, bf16[8192,1024]{1,0:T(8,128)(2,1)} %refs_0_.9, bf16[128,1024]{1,0:T(8,128)(2,1)S(1)} %get-tuple-element.55.refs_2_.refs_0_), custom_call_target="tpu_custom_call" | custom-call | flops 3220000000 | tf_op jit(solution)/shard_map/fetch_first/pallas_call | solution.py:41
  25.1 6.9 %back_project.2 = (f32[512,1024]{1,0:T(8,128)S(1)}, f32[1,4096]{1,0:T(1,128)S(1)}, bf16[256,4096]{1,0:T(8,128)(2,1)S(1)}, bf16[2048,1024]{1,0:T(8,128)(2,1)S(1)}) custom-call(bf16[256,8192]{1,0:T(8,128)(2,1)S(1)} %get-tuple-element.49.refs_0_, bf16[256,8192]{1,0:T(8,128)(2,1)S(1)} %collective-permute-done.refs_0_.refs_1_, ...), custom_call_target="tpu_custom_call" | custom-call | flops 7646444544 | tf_op jit(solution)/shard_map/back_project/pallas_call | solution.py:41
  32.0 0.1 pieces_of.2
  32.1 1.6 %collective-permute-start.4 = (bf16[32,1024]{1,0:T(8,128)(2,1)S(1)}, bf16[32,1024]{1,0:T(8,128)(2,1)S(1)}, u32[]{:S(2)}, u32[]{:S(2)}) collective-permute-start(bf16[32,1024]{1,0:T(8,128)(2,1)S(1)} %get-tuple-element.62), channel_id=1, source_target_pairs={{0,4},{2,6},{4,0},{6,2},{8,12},{10,14},{12,8},{14,10},{1,5},{3,7},... | collective-permute-start | bytes 196616 | tf_op jit(solution)/shard_map/ppermute | solution.py:613
  33.7 2.6 %collective-permute-start.5 = (bf16[32,1024]{1,0:T(8,128)(2,1)S(1)}, bf16[32,1024]{1,0:T(8,128)(2,1)S(1)}, u32[]{:S(2)}, u32[]{:S(2)}) collective-permute-start(bf16[32,1024]{1,0:T(8,128)(2,1)S(1)} %get-tuple-element.63), channel_id=1, source_target_pairs={{0,8},{2,10},{4,12},{6,14},{8,0},{10,2},{12,4},{14,6},{1,9},{3,11}... | collective-permute-start | bytes 196616 | tf_op jit(solution)/shard_map/ppermute | solution.py:613
  36.3 0.2 collective-permute-start.6
  36.5 7.0 %back_project.3 = (bf16[256,1024]{1,0:T(8,128)(2,1)S(1)}, f32[256,1024]{1,0:T(8,128)S(1)}, f32[1,4096]{1,0:T(1,128)S(1)}) custom-call(bf16[256,8192]{1,0:T(8,128)(2,1)S(1)} %get-tuple-element.49.refs_0_, bf16[256,8192]{1,0:T(8,128)(2,1)S(1)} %collective-permute-done.refs_0_.refs_1_, bf16[256,4096]{1,0:T(8,128)(2,1)S(1)} %get-tuple-element.65.refs_2_.refs_0_, ...), custom_call_target="tpu_custom_call" | custom-call | flops 7646444544 | tf_op jit(solution)/shard_map/back_project/pallas_call | solution.py:41
  43.7 3.7 %collective-permute-start.9 = (bf16[32,1024]{1,0:T(8,128)(2,1)S(1)}, bf16[32,1024]{1,0:T(8,128)(2,1)S(1)}, u32[]{:S(2)}, u32[]{:S(2)}) collective-permute-start(bf16[32,1024]{1,0:T(8,128)(2,1)S(1)} %get-tuple-element.68.refs_4_.refs_0_), channel_id=1, source_target_pairs={{0,12},{2,14},{4,8},{6,10},{8,4},{10,6},{12,0},{14,2},{1,13},{3,15... | collective-permute-start | bytes 196616 | tf_op jit(solution)/shard_map/ppermute | solution.py:613
  47.3 0.8 collective-permute-start.7
  48.1 1.6 %turn_hidden.2.refs_2_.refs_0_ = bf16[4096,512]{1,0:T(8,128)(2,1)S(1)} custom-call(bf16[256,8192]{1,0:T(8,128)(2,1)S(1)} %get-tuple-element.49.refs_0_, bf16[256,8192]{1,0:T(8,128)(2,1)S(1)} %collective-permute-done.refs_0_.refs_1_, bf16[256,4096]{1,0:T(8,128)(2,1)S(1)} %get-tuple-element.57.refs_2_.refs_0_, ...), custom_call_target="tpu_custom_call" | custom-call | flops 2070000000 | tf_op jit(solution)/shard_map/turn_hidden/pallas_call | solution.py:41
  49.7 0.1 pair_halves.1
  49.8 1.6 %turn_hidden.3.refs_4_.refs_0_ = bf16[4096,512]{1,0:T(8,128)(2,1)S(1)} custom-call(bf16[256,8192]{1,0:T(8,128)(2,1)S(1)} %get-tuple-element.49.refs_0_, bf16[256,8192]{1,0:T(8,128)(2,1)S(1)} %collective-permute-done.refs_0_.refs_1_, bf16[256,4096]{1,0:T(8,128)(2,1)S(1)} %get-tuple-element.65.refs_2_.refs_0_, ...), custom_call_target="tpu_custom_call" | custom-call | flops 2070000000 | tf_op jit(solution)/shard_map/turn_hidden/pallas_call | solution.py:41
  51.4 1.5 %collective-permute-done.8.refs_2_ = bf16[32,1024]{1,0:T(8,128)(2,1)S(1)} collective-permute-done((bf16[32,1024]{1,0:T(8,128)(2,1)S(1)}, bf16[32,1024]{1,0:T(8,128)(2,1)S(1)}, u32[]{:S(2)}, u32[]{:S(2)}) %collective-permute-start.8) | collective-permute-done | bytes 65568 | tf_op jit(solution)/shard_map/ppermute | solution.py:613
  52.9 0.1 collective-permute-done.7.refs_1_
  53.1 0.5 collective-permute-start.13
  53.6 4.1 %turn_x.1.refs_1_.refs_5_.refs_0_ = bf16[8192,512]{1,0:T(8,128)(2,1)} custom-call(bf16[256,8192]{1,0:T(8,128)(2,1)S(1)} %get-tuple-element.49.refs_0_, bf16[256,8192]{1,0:T(8,128)(2,1)S(1)} %collective-permute-done.refs_0_.refs_1_, bf16[128,1024]{1,0:T(8,128)(2,1)S(1)} %join_pieces.2.refs_2_.refs_3_.refs_4_), custom_call_target="tpu_custom_call" | custom-call | flops 4140000000 | tf_op jit(solution)/shard_map/turn_x/pallas_call | solution.py:41
  57.7 3.2 %collective-permute-done.13.refs_0_ = bf16[128,1024]{1,0:T(8,128)(2,1)S(1)} collective-permute-done((bf16[128,1024]{1,0:T(8,128)(2,1)S(1)}, bf16[128,1024]{1,0:T(8,128)(2,1)S(1)}, u32[]{:S(2)}, u32[]{:S(2)}) %collective-permute-start.13) | collective-permute-done | bytes 262176 | tf_op jit(solution)/shard_map/ppermute | solution.py:613
  60.9 0.5 collective-permute-start.11
  61.5 1.0 collective-permute-done.14.refs_2_.refs_3_
  62.5 6.1 %u_grad.2.refs_2_.refs_5_ = bf16[8192,1024]{1,0:T(8,128)(2,1)} custom-call(bf16[4096,512]{1,0:T(8,128)(2,1)S(1)} %turn_hidden.2.refs_2_.refs_0_, bf16[128,1024]{1,0:T(8,128)(2,1)S(1)} %collective-permute-done.12.refs_1_.refs_2_, bf16[128,1024]{1,0:T(8,128)(2,1)S(1)} %collective-permute-done.14.refs_2_.refs_3_, ...), custom_call_target="tpu_custom_call" | custom-call | flops 7646444544 | tf_op jit(solution)/shard_map/u_grad/pallas_call | solution.py:41
  68.6 1.0 collective-permute-done.11.refs_1_
  69.7 1.7 %collective-permute-start.15 = (bf16[32,1024]{1,0:T(8,128)(2,1)S(1)}, bf16[32,1024]{1,0:T(8,128)(2,1)S(1)}, u32[]{:S(2)}, u32[]{:S(2)}) collective-permute-start(bf16[32,1024]{1,0:T(8,128)(2,1)S(1)} %get-tuple-element.74), channel_id=1, source_target_pairs={{0,4},{2,6},{4,0},{6,2},{8,12},{10,14},{12,8},{14,10},{1,5},{3,7},... | collective-permute-start | bytes 196616 | tf_op jit(solution)/shard_map/ppermute | solution.py:613
  71.4 1.7 %collective-permute-start.16 = (bf16[32,1024]{1,0:T(8,128)(2,1)S(1)}, bf16[32,1024]{1,0:T(8,128)(2,1)S(1)}, u32[]{:S(2)}, u32[]{:S(2)}) collective-permute-start(bf16[32,1024]{1,0:T(8,128)(2,1)S(1)} %get-tuple-element.75), channel_id=1, source_target_pairs={{0,8},{2,10},{4,12},{6,14},{8,0},{10,2},{12,4},{14,6},{1,9},{3,11}... | collective-permute-start | bytes 196616 | tf_op jit(solution)/shard_map/ppermute | solution.py:613
  73.1 1.0 collective-permute-start.17
  74.2 6.2 %u_grad.3 = (bf16[8192,1024]{1,0:T(8,128)(2,1)}, bf16[1024,1024]{1,0:T(8,128)(2,1)S(1)}) custom-call(bf16[4096,512]{1,0:T(8,128)(2,1)S(1)} %turn_hidden.3.refs_4_.refs_0_, bf16[128,1024]{1,0:T(8,128)(2,1)S(1)} %collective-permute-done.12.refs_1_.refs_2_, ...), custom_call_target="tpu_custom_call", output_to_operand_aliasing={{0}: (5, {})} | custom-call | flops 7646444544 | tf_op jit(solution)/shard_map/u_grad/pallas_call | solution.py:41
  80.4 2.9 %collective-permute-start.20 = (bf16[32,1024]{1,0:T(8,128)(2,1)S(1)}, bf16[32,1024]{1,0:T(8,128)(2,1)S(1)}, u32[]{:S(2)}, u32[]{:S(2)}) collective-permute-start(bf16[32,1024]{1,0:T(8,128)(2,1)S(1)} %add_pieces.3.refs_7_.refs_0_), channel_id=1, source_target_pairs={{0,12},{2,14},{4,8},{6,10},{8,4},{10,6},{12,0},{14,2},{1,13},{3,15... | collective-permute-start | bytes 196616 | tf_op jit(solution)/shard_map/ppermute | solution.py:613
  83.3 1.6 %collective-permute-start.18 = (bf16[32,1024]{1,0:T(8,128)(2,1)S(1)}, bf16[32,1024]{1,0:T(8,128)(2,1)S(1)}, u32[]{:S(2)}, u32[]{:S(2)}) collective-permute-start(bf16[32,1024]{1,0:T(8,128)(2,1)S(1)} %add_pieces.3.refs_7_.refs_0_), channel_id=1, source_target_pairs={{0,4},{2,6},{4,0},{6,2},{8,12},{10,14},{12,8},{14,10},{1,5},{3,7},... | collective-permute-start | bytes 196616 | tf_op jit(solution)/shard_map/ppermute | solution.py:613
  84.9 6.4 %expand.2 = (f32[512,4096]{1,0:T(8,128)S(1)}, bf16[1024,1024]{1,0:T(8,128)(2,1)S(1)}) custom-call(bf16[8192,1024]{1,0:T(8,128)(2,1)} %refs_0_.9, bf16[1024,1024]{1,0:T(8,128)(2,1)S(1)} %get-tuple-element.78.refs_1_, bf16[128,1024]{1,0:T(8,128)(2,1)S(1)} %collective-permute-done.12.refs_1_.refs_2_, ...), custom_call_target="tpu_custom_call" | custom-call | flops 7646444544 | tf_op jit(solution)/shard_map/expand/pallas_call | solution.py:41
  91.4 0.6 collective-permute-start.22
  92.0 6.6 %expand.3 = (f32[512,4096]{1,0:T(8,128)S(1)}, bf16[1024,1024]{1,0:T(8,128)(2,1)S(1)}) custom-call(bf16[8192,1024]{1,0:T(8,128)(2,1)} %refs_0_.9, bf16[1024,1024]{1,0:T(8,128)(2,1)S(1)} %get-tuple-element.80.refs_1_, bf16[128,1024]{1,0:T(8,128)(2,1)S(1)} %collective-permute-done.12.refs_1_.refs_2_, ...), custom_call_target="tpu_custom_call" | custom-call | flops 7646444544 | tf_op jit(solution)/shard_map/expand/pallas_call | solution.py:41
  98.6 0.6 collective-permute-start.23
  99.2 0.2 copy-done
  99.4 0.9 collective-permute-done.23.refs_7_.refs_2_
  100.3 6.8 %input_grad.2 = (bf16[256,16384]{1,0:T(8,128)(2,1)}, bf16[256,4096]{1,0:T(8,128)(2,1)S(1)}, bf16[1024,1024]{1,0:T(8,128)(2,1)S(1)}) custom-call(bf16[256,4096]{1,0:T(8,128)(2,1)S(1)} %get-tuple-element.57.refs_2_.refs_0_, bf16[256,8192]{1,0:T(8,128)(2,1)S(1)} %collective-permute-done.3.refs_3_.refs_1_, f32[512,4096]{1,0:T(8,128)S(1)} %get-tuple-element.79.refs_4_.refs_2_, ...), custom_call_target="tpu_custom_call" | custom-call | flops 7646444544 | tf_op jit(solution)/shard_map/input_grad/pallas_call | solution.py:41
  107.1 0.4 collective-permute-start.24
  107.6 6.7 %input_grad.3 = (bf16[256,16384]{1,0:T(8,128)(2,1)}, bf16[256,4096]{1,0:T(8,128)(2,1)S(1)}) custom-call(bf16[256,4096]{1,0:T(8,128)(2,1)S(1)} %get-tuple-element.65.refs_2_.refs_0_, bf16[256,8192]{1,0:T(8,128)(2,1)S(1)} %collective-permute-done.3.refs_3_.refs_1_, ...), custom_call_target="tpu_custom_call", output_to_operand_aliasing={{0}: (10, {})} | custom-call | flops 7646444544 | tf_op jit(solution)/shard_map/input_grad/pallas_call | solution.py:41
  114.3 0.2 collective-permute-start.25
  114.5 0.6 pad_maximum_fusion
  115.1 7.9 %v_grad.2 = (bf16[8192,1024]{1,0:T(8,128)(2,1)}, bf16[256,16384]{1,0:T(8,128)(2,1)}) custom-call(bf16[8192,512]{1,0:T(8,128)(2,1)} %turn_x.1.refs_1_.refs_5_.refs_0_, bf16[128,1024]{1,0:T(8,128)(2,1)S(1)} %collective-permute-done.21.refs_6_.refs_1_, bf16[128,1024]{1,0:T(8,128)(2,1)S(1)} %collective-permute-done.23.refs_7_.refs_2_, ...), custom_call_target="tpu_custom_call", output_to_operand_aliasing={{1}: (6, {})} | custom-call | flops 345000000 | tf_op jit(solution)/shard_map/v_grad/pallas_call | solution.py:41
  123.1 7.9 %v_grad.3 = (bf16[8192,1024]{1,0:T(8,128)(2,1)}, bf16[256,16384]{1,0:T(8,128)(2,1)}) custom-call(bf16[8192,512]{1,0:T(8,128)(2,1)} %turn_x.1.refs_1_.refs_5_.refs_0_, bf16[128,1024]{1,0:T(8,128)(2,1)S(1)} %collective-permute-done.21.refs_6_.refs_1_, ...), custom_call_target="tpu_custom_call", output_to_operand_aliasing={{0}: (5, {}), {1}: (7, {})} | custom-call | flops 7646444544 | tf_op jit(solution)/shard_map/v_grad/pallas_call | solution.py:41
  (35 shorter events, 0.4 us)
Async XLA Ops:
  2.9 11.8 %collective-permute-start = (bf16[256,8192]{1,0:T(8,128)(2,1)S(1)}, bf16[256,8192]{1,0:T(8,128)(2,1)S(1)}, u32[]{:S(2)}, u32[]{:S(2)}) collective-permute-start(bf16[256,8192]{1,0:T(8,128)(2,1)S(1)} %cut_half.1.refs_3_), channel_id=1, source_target_pairs={{0,1},{1,0},{2,3},{3,2},{4,5},{5,4},{6,7},{7,6},{8,9},{9,8},{10,11... | collective-permute-start | bytes 12582920 | tf_op jit(solution)/shard_map/ppermute | solution.py:610
  12.5 2.0 %collective-permute-start.1 = (bf16[256,1024]{1,0:T(8,128)(2,1)S(1)}, bf16[256,1024]{1,0:T(8,128)(2,1)S(1)}, u32[]{:S(2)}, u32[]{:S(2)}) collective-permute-start(bf16[256,1024]{1,0:T(8,128)(2,1)S(1)} %get-tuple-element.50), channel_id=1, source_target_pairs={{0,1},{1,0},{2,3},{3,2},{4,5},{5,4},{6,7},{7,6},{8,9},{9,8},{10,11... | collective-permute-start | bytes 1572872 | tf_op jit(solution)/shard_map/ppermute | solution.py:610
  14.5 10.6 %collective-permute-start.3 = (bf16[256,8192]{1,0:T(8,128)(2,1)S(1)}, bf16[256,8192]{1,0:T(8,128)(2,1)S(1)}, u32[]{:S(2)}, u32[]{:S(2)}) collective-permute-start(bf16[256,8192]{1,0:T(8,128)(2,1)S(1)} %hold.3), channel_id=1, source_target_pairs={{0,1},{1,0},{2,3},{3,2},{4,5},{5,4},{6,7},{7,6},{8,9},{9,8},{10,11... | collective-permute-start | bytes 12582920 | tf_op jit(solution)/shard_map/ppermute | solution.py:610
  19.3 12.7 %collective-permute-start.2 = (bf16[128,1024]{1,0:T(8,128)(2,1)S(1)}, bf16[128,1024]{1,0:T(8,128)(2,1)S(1)}, u32[]{:S(2)}, u32[]{:S(2)}) collective-permute-start(bf16[128,1024]{1,0:T(8,128)(2,1)S(1)} %get-tuple-element.56), channel_id=1, source_target_pairs={{0,2},{2,0},{4,6},{6,4},{8,10},{10,8},{12,14},{14,12},{1,3},{3,1},... | collective-permute-start | bytes 786440 | tf_op jit(solution)/shard_map/ppermute | solution.py:613
  32.1 11.4 %collective-permute-start.4 = (bf16[32,1024]{1,0:T(8,128)(2,1)S(1)}, bf16[32,1024]{1,0:T(8,128)(2,1)S(1)}, u32[]{:S(2)}, u32[]{:S(2)}) collective-permute-start(bf16[32,1024]{1,0:T(8,128)(2,1)S(1)} %get-tuple-element.62), channel_id=1, source_target_pairs={{0,4},{2,6},{4,0},{6,2},{8,12},{10,14},{12,8},{14,10},{1,5},{3,7},... | collective-permute-start | bytes 196616 | tf_op jit(solution)/shard_map/ppermute | solution.py:613
  33.7 9.8 %collective-permute-start.5 = (bf16[32,1024]{1,0:T(8,128)(2,1)S(1)}, bf16[32,1024]{1,0:T(8,128)(2,1)S(1)}, u32[]{:S(2)}, u32[]{:S(2)}) collective-permute-start(bf16[32,1024]{1,0:T(8,128)(2,1)S(1)} %get-tuple-element.63), channel_id=1, source_target_pairs={{0,8},{2,10},{4,12},{6,14},{8,0},{10,2},{12,4},{14,6},{1,9},{3,11}... | collective-permute-start | bytes 196616 | tf_op jit(solution)/shard_map/ppermute | solution.py:613
  36.3 7.2 %collective-permute-start.6 = (bf16[32,1024]{1,0:T(8,128)(2,1)S(1)}, bf16[32,1024]{1,0:T(8,128)(2,1)S(1)}, u32[]{:S(2)}, u32[]{:S(2)}) collective-permute-start(bf16[32,1024]{1,0:T(8,128)(2,1)S(1)} %get-tuple-element.64), channel_id=1, source_target_pairs={{0,12},{2,14},{4,8},{6,10},{8,4},{10,6},{12,0},{14,2},{1,13},{3,15... | collective-permute-start | bytes 196616 | tf_op jit(solution)/shard_map/ppermute | solution.py:613
  43.6 6.1 %collective-permute-start.10 = (bf16[256,1024]{1,0:T(8,128)(2,1)S(1)}, bf16[256,1024]{1,0:T(8,128)(2,1)S(1)}, u32[]{:S(2)}, u32[]{:S(2)}) collective-permute-start(bf16[256,1024]{1,0:T(8,128)(2,1)S(1)} %get-tuple-element.70), channel_id=1, source_target_pairs={{0,1},{1,0},{2,3},{3,2},{4,5},{5,4},{6,7},{7,6},{8,9},{9,8},{10,11... | collective-permute-start | bytes 1572872 | tf_op jit(solution)/shard_map/ppermute | solution.py:610
  43.7 7.7 %collective-permute-start.9 = (bf16[32,1024]{1,0:T(8,128)(2,1)S(1)}, bf16[32,1024]{1,0:T(8,128)(2,1)S(1)}, u32[]{:S(2)}, u32[]{:S(2)}) collective-permute-start(bf16[32,1024]{1,0:T(8,128)(2,1)S(1)} %get-tuple-element.68.refs_4_.refs_0_), channel_id=1, source_target_pairs={{0,12},{2,14},{4,8},{6,10},{8,4},{10,6},{12,0},{14,2},{1,13},{3,15... | collective-permute-start | bytes 196616 | tf_op jit(solution)/shard_map/ppermute | solution.py:613
  47.3 5.6 %collective-permute-start.8 = (bf16[32,1024]{1,0:T(8,128)(2,1)S(1)}, bf16[32,1024]{1,0:T(8,128)(2,1)S(1)}, u32[]{:S(2)}, u32[]{:S(2)}) collective-permute-start(bf16[32,1024]{1,0:T(8,128)(2,1)S(1)} %get-tuple-element.68.refs_4_.refs_0_), channel_id=1, source_target_pairs={{0,8},{2,10},{4,12},{6,14},{8,0},{10,2},{12,4},{14,6},{1,9},{3,11}... | collective-permute-start | bytes 196616 | tf_op jit(solution)/shard_map/ppermute | solution.py:613
  47.3 5.7 %collective-permute-start.7 = (bf16[32,1024]{1,0:T(8,128)(2,1)S(1)}, bf16[32,1024]{1,0:T(8,128)(2,1)S(1)}, u32[]{:S(2)}, u32[]{:S(2)}) collective-permute-start(bf16[32,1024]{1,0:T(8,128)(2,1)S(1)} %get-tuple-element.68.refs_4_.refs_0_), channel_id=1, source_target_pairs={{0,4},{2,6},{4,0},{6,2},{8,12},{10,14},{12,8},{14,10},{1,5},{3,7},... | collective-permute-start | bytes 196616 | tf_op jit(solution)/shard_map/ppermute | solution.py:613
  53.1 7.9 %collective-permute-start.13 = (bf16[128,1024]{1,0:T(8,128)(2,1)S(1)}, bf16[128,1024]{1,0:T(8,128)(2,1)S(1)}, u32[]{:S(2)}, u32[]{:S(2)}) collective-permute-start(bf16[128,1024]{1,0:T(8,128)(2,1)S(1)} %join_pieces.2.refs_2_.refs_3_.refs_4_), channel_id=1, source_target_pairs={{0,2},{2,0},{4,6},{6,4},{8,10},{10,8},{12,14},{14,12},{1,3},{3,1},... | collective-permute-start | bytes 786440 | tf_op jit(solution)/shard_map/ppermute | solution.py:613
  53.6 7.9 %collective-permute-start.12 = (bf16[128,1024]{1,0:T(8,128)(2,1)S(1)}, bf16[128,1024]{1,0:T(8,128)(2,1)S(1)}, u32[]{:S(2)}, u32[]{:S(2)}) collective-permute-start(bf16[128,1024]{1,0:T(8,128)(2,1)S(1)} %join_pieces.2.refs_2_.refs_3_.refs_4_), channel_id=1, source_target_pairs={{0,1},{1,0},{2,3},{3,2},{4,5},{5,4},{6,7},{7,6},{8,9},{9,8},{10,11... | collective-permute-start | bytes 786440 | tf_op jit(solution)/shard_map/ppermute | solution.py:610
  60.9 1.5 %collective-permute-start.14 = (bf16[128,1024]{1,0:T(8,128)(2,1)S(1)}, bf16[128,1024]{1,0:T(8,128)(2,1)S(1)}, u32[]{:S(2)}, u32[]{:S(2)}) collective-permute-start(bf16[128,1024]{1,0:T(8,128)(2,1)S(1)} %hold.4.refs_4_.refs_5_), channel_id=1, source_target_pairs={{0,1},{1,0},{2,3},{3,2},{4,5},{5,4},{6,7},{7,6},{8,9},{9,8},{10,11... | collective-permute-start | bytes 786440 | tf_op jit(solution)/shard_map/ppermute | solution.py:610
  60.9 8.7 %collective-permute-start.11 = (bf16[128,1024]{1,0:T(8,128)(2,1)S(1)}, bf16[128,1024]{1,0:T(8,128)(2,1)S(1)}, u32[]{:S(2)}, u32[]{:S(2)}) collective-permute-start(bf16[128,1024]{1,0:T(8,128)(2,1)S(1)} %get-tuple-element.72), channel_id=1, source_target_pairs={{0,2},{2,0},{4,6},{6,4},{8,10},{10,8},{12,14},{14,12},{1,3},{3,1},... | collective-permute-start | bytes 786440 | tf_op jit(solution)/shard_map/ppermute | solution.py:613
  69.7 10.6 %collective-permute-start.15 = (bf16[32,1024]{1,0:T(8,128)(2,1)S(1)}, bf16[32,1024]{1,0:T(8,128)(2,1)S(1)}, u32[]{:S(2)}, u32[]{:S(2)}) collective-permute-start(bf16[32,1024]{1,0:T(8,128)(2,1)S(1)} %get-tuple-element.74), channel_id=1, source_target_pairs={{0,4},{2,6},{4,0},{6,2},{8,12},{10,14},{12,8},{14,10},{1,5},{3,7},... | collective-permute-start | bytes 196616 | tf_op jit(solution)/shard_map/ppermute | solution.py:613
  71.4 8.9 %collective-permute-start.16 = (bf16[32,1024]{1,0:T(8,128)(2,1)S(1)}, bf16[32,1024]{1,0:T(8,128)(2,1)S(1)}, u32[]{:S(2)}, u32[]{:S(2)}) collective-permute-start(bf16[32,1024]{1,0:T(8,128)(2,1)S(1)} %get-tuple-element.75), channel_id=1, source_target_pairs={{0,8},{2,10},{4,12},{6,14},{8,0},{10,2},{12,4},{14,6},{1,9},{3,11}... | collective-permute-start | bytes 196616 | tf_op jit(solution)/shard_map/ppermute | solution.py:613
  73.1 7.2 %collective-permute-start.17 = (bf16[32,1024]{1,0:T(8,128)(2,1)S(1)}, bf16[32,1024]{1,0:T(8,128)(2,1)S(1)}, u32[]{:S(2)}, u32[]{:S(2)}) collective-permute-start(bf16[32,1024]{1,0:T(8,128)(2,1)S(1)} %get-tuple-element.76), channel_id=1, source_target_pairs={{0,12},{2,14},{4,8},{6,10},{8,4},{10,6},{12,0},{14,2},{1,13},{3,15... | collective-permute-start | bytes 196616 | tf_op jit(solution)/shard_map/ppermute | solution.py:613
  80.4 10.9 %collective-permute-start.20 = (bf16[32,1024]{1,0:T(8,128)(2,1)S(1)}, bf16[32,1024]{1,0:T(8,128)(2,1)S(1)}, u32[]{:S(2)}, u32[]{:S(2)}) collective-permute-start(bf16[32,1024]{1,0:T(8,128)(2,1)S(1)} %add_pieces.3.refs_7_.refs_0_), channel_id=1, source_target_pairs={{0,12},{2,14},{4,8},{6,10},{8,4},{10,6},{12,0},{14,2},{1,13},{3,15... | collective-permute-start | bytes 196616 | tf_op jit(solution)/shard_map/ppermute | solution.py:613
  83.3 8.0 %collective-permute-start.19 = (bf16[32,1024]{1,0:T(8,128)(2,1)S(1)}, bf16[32,1024]{1,0:T(8,128)(2,1)S(1)}, u32[]{:S(2)}, u32[]{:S(2)}) collective-permute-start(bf16[32,1024]{1,0:T(8,128)(2,1)S(1)} %add_pieces.3.refs_7_.refs_0_), channel_id=1, source_target_pairs={{0,8},{2,10},{4,12},{6,14},{8,0},{10,2},{12,4},{14,6},{1,9},{3,11}... | collective-permute-start | bytes 196616 | tf_op jit(solution)/shard_map/ppermute | solution.py:613
  83.3 8.0 %collective-permute-start.18 = (bf16[32,1024]{1,0:T(8,128)(2,1)S(1)}, bf16[32,1024]{1,0:T(8,128)(2,1)S(1)}, u32[]{:S(2)}, u32[]{:S(2)}) collective-permute-start(bf16[32,1024]{1,0:T(8,128)(2,1)S(1)} %add_pieces.3.refs_7_.refs_0_), channel_id=1, source_target_pairs={{0,4},{2,6},{4,0},{6,2},{8,12},{10,14},{12,8},{14,10},{1,5},{3,7},... | collective-permute-start | bytes 196616 | tf_op jit(solution)/shard_map/ppermute | solution.py:613
  91.4 7.2 %collective-permute-start.22 = (bf16[128,1024]{1,0:T(8,128)(2,1)S(1)}, bf16[128,1024]{1,0:T(8,128)(2,1)S(1)}, u32[]{:S(2)}, u32[]{:S(2)}) collective-permute-start(bf16[128,1024]{1,0:T(8,128)(2,1)S(1)} %join_pieces.3.refs_7_.refs_8_.refs_3_), channel_id=1, source_target_pairs={{0,2},{2,0},{4,6},{6,4},{8,10},{10,8},{12,14},{14,12},{1,3},{3,1},... | collective-permute-start | bytes 786440 | tf_op jit(solution)/shard_map/ppermute | solution.py:613
  92.0 7.4 %collective-permute-start.21 = (bf16[128,1024]{1,0:T(8,128)(2,1)S(1)}, bf16[128,1024]{1,0:T(8,128)(2,1)S(1)}, u32[]{:S(2)}, u32[]{:S(2)}) collective-permute-start(bf16[128,1024]{1,0:T(8,128)(2,1)S(1)} %join_pieces.3.refs_7_.refs_8_.refs_3_), channel_id=1, source_target_pairs={{0,1},{1,0},{2,3},{3,2},{4,5},{5,4},{6,7},{7,6},{8,9},{9,8},{10,11... | collective-permute-start | bytes 786440 | tf_op jit(solution)/shard_map/ppermute | solution.py:610
  98.6 0.8 copy-start
  98.6 1.7 %collective-permute-start.23 = (bf16[128,1024]{1,0:T(8,128)(2,1)S(1)}, bf16[128,1024]{1,0:T(8,128)(2,1)S(1)}, u32[]{:S(2)}, u32[]{:S(2)}) collective-permute-start(bf16[128,1024]{1,0:T(8,128)(2,1)S(1)} %hold.5.refs_9_.refs_4_), channel_id=1, source_target_pairs={{0,1},{1,0},{2,3},{3,2},{4,5},{5,4},{6,7},{7,6},{8,9},{9,8},{10,11... | collective-permute-start | bytes 786440 | tf_op jit(solution)/shard_map/ppermute | solution.py:610
  107.1 8.0 %collective-permute-start.24 = (bf16[256,4096]{1,0:T(8,128)(2,1)S(1)}, bf16[256,4096]{1,0:T(8,128)(2,1)S(1)}, u32[]{:S(2)}, u32[]{:S(2)}) collective-permute-start(bf16[256,4096]{1,0:T(8,128)(2,1)S(1)} %get-tuple-element.83), channel_id=1, source_target_pairs={{0,1},{1,0},{2,3},{3,2},{4,5},{5,4},{6,7},{7,6},{8,9},{9,8},{10,11... | collective-permute-start | bytes 6291464 | tf_op jit(solution)/shard_map/ppermute | solution.py:610
  114.3 8.8 %collective-permute-start.25 = (bf16[256,4096]{1,0:T(8,128)(2,1)S(1)}, bf16[256,4096]{1,0:T(8,128)(2,1)S(1)}, u32[]{:S(2)}, u32[]{:S(2)}) collective-permute-start(bf16[256,4096]{1,0:T(8,128)(2,1)S(1)} %get-tuple-element.88), channel_id=1, source_target_pairs={{0,1},{1,0},{2,3},{3,2},{4,5},{5,4},{6,7},{7,6},{8,9},{9,8},{10,11... | collective-permute-start | bytes 6291464 | tf_op jit(solution)/shard_map/ppermute | solution.py:610

commit v2 on v1

--- a/solution.py
+++ b/solution.py
@@ -156,39 +156,31 @@
     return [((rows // 2, rank), BF, "v")] * 2 if direct else [((rows, rank), F32, "v")]
 
 
-def project_other(x_o, vs, theirs, direct):
+def project_other(x_o, vs, theirs, c, u, direct):
     rows, half = x_o.shape
     tk, rank = vs[0].shape
-
-    def body(at_ref, x_ref, t_ref, *refs):
-        vv, outs, acc = refs[:VPARTS], refs[VPARTS:-1], refs[-1]
+    first = half // 2
+
+    def body(at_ref, x_ref, t_ref, c_ref, *refs, fetch):
+        vv, outs, cv_ref, acc, c_sem = refs[:VPARTS], refs[VPARTS:-3], refs[-3], refs[-2], refs[-1]
+        first_c = copy(c_ref.at[:, at_block(2 * at_ref[0], first)], cv_ref, c_sem.at[0])
+        fetch()
+        first_c.start()
         for k in range(VPARTS):
             part = jnp.dot(x_ref[:, k * tk : (k + 1) * tk], vv[k][...], preferred_element_type=F32)
             acc[...] = part + (acc[...] if k else t_ref[...].astype(F32))
         write_halves(at_ref, lambda here: acc[here, :], outs)
+        first_c.wait()
 
     return call(
         body,
         "project_other",
-        [(x_o, "v"), (theirs, "v")] + [(a, "v") for a in vs],
-        halves_of(rows, rank, direct),
-        [pltpu.VMEM((rows, rank), F32)],
+        [(x_o, "v"), (theirs, "v"), (c, "h")] + [(a, "v") for a in vs],
+        halves_of(rows, rank, direct) + [((rows, first), BF, "v")],
+        [pltpu.VMEM((rows, rank), F32), dma(1)],
         flops=2 * rows * half * rank,
         mib=6,
-    )
-
-
-def fetch_first(c, u, after=()):
-    rows, part = c.shape[0], u.shape[0] // 2
-
-    def body(at_ref, c_ref, cv_ref, c_sem, fetch):
-        first_c = copy(c_ref.at[:, at_block(2 * at_ref[0], part)], cv_ref, c_sem.at[0])
-        fetch()
-        first_c.start()
-        first_c.wait()
-
-    return call(
-        body, "fetch_first", [(c, "h")], [((rows, part), BF, "v")], [dma(1)], ahead=[(u, 0, part // 2)], after=after, us=2.8
+        ahead=[(u, 0, first // 4)],
     )
 
 
@@ -228,14 +220,17 @@
             h[k, :rows, :] = own
             h[k, rows:, :] = oth
             b_ref[:, here] = jnp.sum(own.astype(F32), axis=0, keepdims=True) + jnp.sum(oth.astype(F32), axis=0, keepdims=True)
-        for k in range(1, n):
-            u_copy(k).wait()
-
         @pl.loop(0, 2)
         def _(i):
             at_rows = at_block(i, rows)
             total = None if first else so_ref[at_rows, :]
             for k in range(n):
+                if k:
+
+                    @pl.when(i == 0)
+                    def _():
+                        u_copy(k).wait()
+
                 term = jnp.dot(h[k, at_rows, :], uv[k - 1] if k else uf_ref[...], preferred_element_type=F32)
                 total = term if total is None else total + term
             if first:
@@ -263,7 +258,7 @@
         [pltpu.VMEM((max(1, n - 1), tk, rank), BF), pltpu.VMEM((n, 2 * rows, tk), BF), dma(max(1, n - 1))]
         + ([dma(1)] if first else []),
         flops=2 * rows * half * rank,
-        mib=16,
+        mib=15,
         after=after,
         ahead=[(u, part, tk)] if first else [],
     )
@@ -345,11 +340,10 @@
     part = half // 2
     tw = min(512, part // 2)
     n = part // tw
-    far = turned.shape[0] == half
     np_ = len(p)
     recv, full = ([placed[0]], placed[1]) if placed else ((), None)
     nr = len(recv)
-    ins = [(turned, "h" if far else "v")] + [(a, "v") for a in p]
+    ins = [(turned, "v")] + [(a, "v") for a in p]
     aliases = {}
     if so_far is not None:
         aliases[len(ins)] = 0
@@ -365,11 +359,7 @@
         o_ref, refs = refs[0], refs[1:]
         if nr:
             f_ref, refs = refs[0], refs[1:]
-        stage, both, sems, put_sem, *refs = refs
-
-        def left_copy(k):
-            src = t_ref.at[pl.ds(pl.multiple_of(s * part + k * tw, tw), tw), :]
-            return copy(src, refs[0].at[at_block(k, tw), :], refs[1].at[k])
+        stage, both, sems, put_sem = refs
 
         def put(i):
             w = recv[i].shape[1]
@@ -381,20 +371,13 @@
             there = pl.ds(pl.multiple_of(s * part + k * tw, tw), tw)
             return copy(stage.at[slot], o_ref.at[there, :], sems.at[slot])
 
-        if far:
-            for k in range(n):
-                left_copy(k).start()
+        fetch()
         for i in range(nr):
             put(i).start()
-        fetch()
         fill(at_ref, both, p_refs)
 
         @pl.loop(0, n // 2)
         def _(kk):
-            if far:
-                left_copy(2 * kk).wait()
-                left_copy(2 * kk + 1).wait()
-
             @pl.when(kk >= 2)
             def _():
                 out(2 * kk - 4).wait()
@@ -402,8 +385,7 @@
 
             for i in range(2):
                 k = 2 * kk + i
-                left = refs[0][at_block(k, tw), :] if far else t_ref[at_block(k, tw), :]
-                stage[lax.rem(k, 4)] = jnp.dot(left, both[...], preferred_element_type=F32).astype(BF)
+                stage[lax.rem(k, 4)] = jnp.dot(t_ref[at_block(k, tw), :], both[...], preferred_element_type=F32).astype(BF)
                 out(k).start()
 
         for k in range(max(0, n - 4), n):
@@ -417,11 +399,10 @@
         name,
         ins,
         outs,
-        [pltpu.VMEM((4, tw, rank), BF), pltpu.VMEM((rows2, rank), BF), dma(4), dma(max(1, nr))]
-        + ([pltpu.VMEM((part, rows2), BF), dma(n)] if far else []),
+        [pltpu.VMEM((4, tw, rank), BF), pltpu.VMEM((rows2, rank), BF), dma(4), dma(max(1, nr))],
         flops=work * rows2 * half * rank,
         aliases=aliases,
-        mib=18 if far else 12,
+        mib=12,
         after=after,
         ahead=ahead,
     )
@@ -542,7 +523,7 @@
         ],
         flops=2 * rows * half * rank,
         aliases=aliases,
-        mib=14,
+        mib=13,
         after=after,
         ahead=ahead,
     )
@@ -598,7 +579,7 @@
     def body(at_ref, a_ref, o_ref):
         pass
 
-    return call(body, "hold", [(a, "v")], [(a.shape, a.dtype, "v")], aliases={0: 0}, after=after, mib=9)[0]
+    return call(body, "hold", [(a, "v")], [(a.shape, a.dtype, "v")], aliases={0: 0}, after=after)[0]
 
 
 def solution(mesh):
@@ -630,8 +611,7 @@
         own, x_own, c_s, *v_in = project_own(x, v, c, [x_s])
         theirs = trade(own)
         c_o = trade(hold(c_s, [theirs]))
-        sums = project_other(x_o, v_in, theirs, direct)
-        c0, u0 = fetch_first(c, u, [sums[0]])
+        *sums, c0, u0 = project_other(x_o, v_in, theirs, c, u, direct)
         acc, b0, c1, u1 = back_project(0, x_own, x_o, c0, c_o, u, u0, None, c)
         if direct:
             parts = pieces_of(sums[0], to(sums[1], 1), m, [acc])
@@ -644,8 +624,9 @@
             other_p = to(half_p, 1)
             x_t = turn_x(x_own, x_o, [half_p])
             other_p = hold(other_p, [(x_t, "h")])
+            grad_b = jnp.concatenate([b0[0], b1[0]])
             p = [trade(half_p), trade(other_p), half_p, other_p]
-            (grad_u,) = factor_grad("u_grad", 0, half, h_t0, p, None, after=[(x_t, "h")])
+            (grad_u,) = factor_grad("u_grad", 0, half, h_t0, p, None, after=[(x_t, "h"), (grad_b, "h")])
             parts_g = pieces_of(sums_g[0], to(sums_g[1], 1), m, [(grad_u, "h")])
             grad_u, u0 = factor_grad("u_grad", 1, half, h_t1, p, grad_u, after=[parts_g[0]], ahead=[(u, 0, tw)])
             (total_g,) = add_pieces(spread(parts_g), [(grad_u, "h")])
@@ -659,6 +640,7 @@
             own_g, mine_g, b1 = back_project(1, x_own, x_o, c1, c_o, u, u1, acc)
             (sums_g,) = pair_halves(mine_g, trade(own_g), direct)
             p, g = plain(sums[0]), plain(sums_g)
+            grad_b = jnp.concatenate([b0[0], b1[0]])
             x_t = turn_x(x_own, x_o)
             (h_t0,) = turn_hidden(0, x_own, x_o, c0, c_o)
             (h_t1,) = turn_hidden(1, x_own, x_o, c1, c_o)
@@ -668,11 +650,11 @@
             ex1, v0 = expand(1, u, u1, p, ahead=[(v, 0, tw)])
         bias = bias[None, :]
         out, oth0, v1 = input_grad(0, c0, c_o, ex0, v, v0, bias, g, None, width, [ex1], [(v, part, tw)])
-        out, oth1 = input_grad(1, c1, c_o, ex1, v, v1, bias, g, out, width)
+        out, oth1, x_t0 = input_grad(1, c1, c_o, ex1, v, v1, bias, g, out, width, ahead=[(x_t, 0, part)])
         back0, back1 = trade(oth0), trade(oth1)
-        grad_v, out = factor_grad("v_grad", 0, half, x_t, g, None, (back0, out), work=0)
-        grad_v, out = factor_grad("v_grad", 1, half, x_t, g, grad_v, (back1, out))
-        return out, grad_u, grad_v, jnp.concatenate([b0[0], b1[0]])
+        grad_v, out, x_t1 = factor_grad("v_grad", 0, half, x_t0, g, None, (back0, out), ahead=[(x_t, part, part)], work=0)
+        grad_v, out = factor_grad("v_grad", 1, half, x_t1, g, grad_v, (back1, out))
+        return out, grad_u, grad_v, grad_b
 
     return jax.shard_map(
         local,

time: 132 us -> 128 us (0.970)
  Pallas kernels: 95 us -> 90.3 us
  starting transfers between devices: 24.5 us -> 27 us
  waiting for transfers between devices: 9.75 us -> 8.04 us
    pallas_call x27 -> x26, Pallas kernels: 95 us -> 90.3 us  [call(): pl.pallas_call(whole if n_ahead else lambda *refs: body(Place(), *refs[:n...]
    ppermute x16, starting transfers between devices: 22.4 us -> 25 us  [to(): return lax.ppermute(a, 'col', [(i, i ^ d) for i in range(n)])]
  transfers between devices with their start and end apart: 26 -> 26, of which waited for: 7 -> 6; matrix products, arithmetic and copies ran while one was open for 0% -> 1% of each run, Pallas kernels for 59% -> 59%
where the time goes in v2:
time: 128 us; the launch traced here: 127 us
  Pallas kernels  90.3 us (71%)
  starting transfers between devices  27 us (21%)
  waiting for transfers between devices  8.04 us (6%)
    pallas_call x26, Pallas kernels, call(): pl.pallas_call(whole if n_ahead else lambda *refs: body(Place(), *refs[:n...  90.3 us
    ppermute x16, starting transfers between devices, to(): return lax.ppermute(a, 'col', [(i, i ^ d) for i in range(n)])  25 us
    ppermute x16, waiting for transfers between devices, to(): return lax.ppermute(a, 'col', [(i, i ^ d) for i in range(n)])  5.22 us
    ppermute x10, waiting for transfers between devices, trade(): return lax.ppermute(a, 'batch', swap)  2.82 us
  transfers between devices with their start and end apart: 26, of which 6 were waited for; matrix products, arithmetic and copies ran while one was open for 1% of the time, Pallas kernels for 59%

profile of v2, /device:TPU:0, one launch (start us, length us, event | category | flops | bytes accessed | tf_op | source)
XLA Modules:
  0.0 127.3 jit_solution(3192881438130506227)
XLA Ops:
  0.6 2.2 %cut_half.1.refs_3_ = bf16[256,8192]{1,0:T(8,128)(2,1)S(1)} custom-call(bf16[256,16384]{1,0:T(8,128)(2,1)} %refs_0_.5), custom_call_target="tpu_custom_call" | custom-call | flops 2529999872 | tf_op jit(solution)/shard_map/cut_half/pallas_call | solution.py:41
  2.9 0.5 collective-permute-start
  3.4 9.1 %project_own.1 = (bf16[256,1024]{1,0:T(8,128)(2,1)S(1)}, bf16[256,8192]{1,0:T(8,128)(2,1)S(1)}, bf16[256,8192]{1,0:T(8,128)(2,1)S(1)}, bf16[2048,1024]{1,0:T(8,1...) custom-call(bf16[256,16384]{1,0:T(8,128)(2,1)} %refs_0_.5, ...), custom_call_target="tpu_custom_call" | custom-call | flops 7646444544 | tf_op jit(solution)/shard_map/project_own/pallas_call | solution.py:41
  12.5 0.1 collective-permute-start.1
  12.6 1.9 %collective-permute-done.1.refs_1_ = bf16[256,1024]{1,0:T(8,128)(2,1)S(1)} collective-permute-done((bf16[256,1024]{1,0:T(8,128)(2,1)S(1)}, bf16[256,1024]{1,0:T(8,128)(2,1)S(1)}, u32[]{:S(2)}, u32[]{:S(2)}) %collective-permute-start.1) | collective-permute-done | bytes 524320 | tf_op jit(solution)/shard_map/ppermute | solution.py:591
  14.5 0.1 collective-permute-start.2
  14.6 5.6 %project_other.1 = (bf16[128,1024]{1,0:T(8,128)(2,1)S(1)}, bf16[128,1024]{1,0:T(8,128)(2,1)S(1)}, bf16[256,4096]{1,0:T(8,128)(2,1)S(1)}, bf16[1024,1024]{1,0:T(8,128)(2,1)S(1)}) custom-call(bf16[256,8192]{1,0:T(8,128)(2,1)S(1)} %collective-permute-done.refs_0_.refs_1_, bf16[256,1024]{1,0:T(8,128)(2,1)S(1)} %collective-permute-done.1.refs_1_, ...), custom_call_target="tpu_custom_call" | custom-call | flops 7646444544 | tf_op jit(solution)/shard_map/project_other/pallas_call | solution.py:41
  20.2 2.9 %collective-permute-start.3 = (bf16[128,1024]{1,0:T(8,128)(2,1)S(1)}, bf16[128,1024]{1,0:T(8,128)(2,1)S(1)}, u32[]{:S(2)}, u32[]{:S(2)}) collective-permute-start(bf16[128,1024]{1,0:T(8,128)(2,1)S(1)} %get-tuple-element.64), channel_id=1, source_target_pairs={{0,2},{2,0},{4,6},{6,4},{8,10},{10,8},{12,14},{14,12},{1,3},{3,1},... | collective-permute-start | bytes 786440 | tf_op jit(solution)/shard_map/ppermute | solution.py:594
  23.1 6.9 %back_project.2 = (f32[512,1024]{1,0:T(8,128)S(1)}, f32[1,4096]{1,0:T(1,128)S(1)}, bf16[256,4096]{1,0:T(8,128)(2,1)S(1)}, bf16[1024,1024]{1,0:T(8,128)(2,1)S(1)}) custom-call(bf16[256,8192]{1,0:T(8,128)(2,1)S(1)} %get-tuple-element.51.refs_0_, bf16[256,8192]{1,0:T(8,128)(2,1)S(1)} %collective-permute-done.refs_0_.refs_1_, ...), custom_call_target="tpu_custom_call" | custom-call | flops 7646444544 | tf_op jit(solution)/shard_map/back_project/pallas_call | solution.py:41
  30.1 0.1 pieces_of.2
  30.2 1.6 %collective-permute-start.4 = (bf16[32,1024]{1,0:T(8,128)(2,1)S(1)}, bf16[32,1024]{1,0:T(8,128)(2,1)S(1)}, u32[]{:S(2)}, u32[]{:S(2)}) collective-permute-start(bf16[32,1024]{1,0:T(8,128)(2,1)S(1)} %get-tuple-element.67), channel_id=1, source_target_pairs={{0,4},{2,6},{4,0},{6,2},{8,12},{10,14},{12,8},{14,10},{1,5},{3,7},... | collective-permute-start | bytes 196616 | tf_op jit(solution)/shard_map/ppermute | solution.py:594
  31.8 2.6 %collective-permute-start.5 = (bf16[32,1024]{1,0:T(8,128)(2,1)S(1)}, bf16[32,1024]{1,0:T(8,128)(2,1)S(1)}, u32[]{:S(2)}, u32[]{:S(2)}) collective-permute-start(bf16[32,1024]{1,0:T(8,128)(2,1)S(1)} %get-tuple-element.68), channel_id=1, source_target_pairs={{0,8},{2,10},{4,12},{6,14},{8,0},{10,2},{12,4},{14,6},{1,9},{3,11}... | collective-permute-start | bytes 196616 | tf_op jit(solution)/shard_map/ppermute | solution.py:594
  34.4 0.2 collective-permute-start.6
  34.6 7.1 %back_project.3 = (bf16[256,1024]{1,0:T(8,128)(2,1)S(1)}, f32[256,1024]{1,0:T(8,128)S(1)}, f32[1,4096]{1,0:T(1,128)S(1)}) custom-call(bf16[256,8192]{1,0:T(8,128)(2,1)S(1)} %get-tuple-element.51.refs_0_, bf16[256,8192]{1,0:T(8,128)(2,1)S(1)} %collective-permute-done.refs_0_.refs_1_, bf16[256,4096]{1,0:T(8,128)(2,1)S(1)} %get-tuple-element.60.refs_2_.refs_0_, ...), custom_call_target="tpu_custom_call" | custom-call | flops 7646444544 | tf_op jit(solution)/shard_map/back_project/pallas_call | solution.py:41
  41.8 0.1 collective-permute-start.7
  41.9 3.7 %collective-permute-start.10 = (bf16[32,1024]{1,0:T(8,128)(2,1)S(1)}, bf16[32,1024]{1,0:T(8,128)(2,1)S(1)}, u32[]{:S(2)}, u32[]{:S(2)}) collective-permute-start(bf16[32,1024]{1,0:T(8,128)(2,1)S(1)} %get-tuple-element.72.refs_4_.refs_0_), channel_id=1, source_target_pairs={{0,12},{2,14},{4,8},{6,10},{8,4},{10,6},{12,0},{14,2},{1,13},{3,15... | collective-permute-start | bytes 196616 | tf_op jit(solution)/shard_map/ppermute | solution.py:594
  45.5 0.8 collective-permute-start.8
  46.3 1.6 %turn_hidden.2.refs_2_.refs_0_ = bf16[4096,512]{1,0:T(8,128)(2,1)S(1)} custom-call(bf16[256,8192]{1,0:T(8,128)(2,1)S(1)} %get-tuple-element.51.refs_0_, bf16[256,8192]{1,0:T(8,128)(2,1)S(1)} %collective-permute-done.refs_0_.refs_1_, bf16[256,4096]{1,0:T(8,128)(2,1)S(1)} %get-tuple-element.57.refs_2_.refs_0_, ...), custom_call_target="tpu_custom_call" | custom-call | flops 2070000000 | tf_op jit(solution)/shard_map/turn_hidden/pallas_call | solution.py:41
  47.9 0.1 pair_halves.1
  48.0 1.6 %turn_hidden.3.refs_4_.refs_0_ = bf16[4096,512]{1,0:T(8,128)(2,1)S(1)} custom-call(bf16[256,8192]{1,0:T(8,128)(2,1)S(1)} %get-tuple-element.51.refs_0_, bf16[256,8192]{1,0:T(8,128)(2,1)S(1)} %collective-permute-done.refs_0_.refs_1_, bf16[256,4096]{1,0:T(8,128)(2,1)S(1)} %get-tuple-element.60.refs_2_.refs_0_, ...), custom_call_target="tpu_custom_call" | custom-call | flops 2070000000 | tf_op jit(solution)/shard_map/turn_hidden/pallas_call | solution.py:41
  49.6 1.6 %collective-permute-done.9.refs_2_ = bf16[32,1024]{1,0:T(8,128)(2,1)S(1)} collective-permute-done((bf16[32,1024]{1,0:T(8,128)(2,1)S(1)}, bf16[32,1024]{1,0:T(8,128)(2,1)S(1)}, u32[]{:S(2)}, u32[]{:S(2)}) %collective-permute-start.9) | collective-permute-done | bytes 65568 | tf_op jit(solution)/shard_map/ppermute | solution.py:594
  51.1 0.1 collective-permute-done.8.refs_1_
  51.3 1.4 %collective-permute-start.12 = (bf16[128,1024]{1,0:T(8,128)(2,1)S(1)}, bf16[128,1024]{1,0:T(8,128)(2,1)S(1)}, u32[]{:S(2)}, u32[]{:S(2)}) collective-permute-start(bf16[128,1024]{1,0:T(8,128)(2,1)S(1)} %join_pieces.2.refs_2_.refs_3_.refs_4_), channel_id=1, source_target_pairs={{0,2},{2,0},{4,6},{6,4},{8,10},{10,8},{12,14},{14,12},{1,3},{3,1},... | collective-permute-start | bytes 786440 | tf_op jit(solution)/shard_map/ppermute | solution.py:594
  52.7 4.1 %turn_x.1.refs_1_.refs_5_.refs_11_.refs_7_ = bf16[8192,512]{1,0:T(8,128)(2,1)} custom-call(bf16[256,8192]{1,0:T(8,128)(2,1)S(1)} %get-tuple-element.51.refs_0_, bf16[256,8192]{1,0:T(8,128)(2,1)S(1)} %collective-permute-done.refs_0_.refs_1_, bf16[128,1024]{1,0:T(8,128)(2,1)S(1)} %join_pieces.2.refs_2_.refs_3_.refs_4_), custom_call_target="tpu_custom_call" | custom-call | flops 4140000000 | tf_op jit(solution)/shard_map/turn_x/pallas_call | solution.py:41
  56.8 2.3 %collective-permute-done.12.refs_0_ = bf16[128,1024]{1,0:T(8,128)(2,1)S(1)} collective-permute-done((bf16[128,1024]{1,0:T(8,128)(2,1)S(1)}, bf16[128,1024]{1,0:T(8,128)(2,1)S(1)}, u32[]{:S(2)}, u32[]{:S(2)}) %collective-permute-start.12) | collective-permute-done | bytes 262176 | tf_op jit(solution)/shard_map/ppermute | solution.py:594
  59.2 0.6 pad_maximum_fusion.refs_6_
  59.8 1.4 %collective-permute-start.14 = (bf16[128,1024]{1,0:T(8,128)(2,1)S(1)}, bf16[128,1024]{1,0:T(8,128)(2,1)S(1)}, u32[]{:S(2)}, u32[]{:S(2)}) collective-permute-start(bf16[128,1024]{1,0:T(8,128)(2,1)S(1)} %get-tuple-element.76), channel_id=1, source_target_pairs={{0,2},{2,0},{4,6},{6,4},{8,10},{10,8},{12,14},{14,12},{1,3},{3,1},... | collective-permute-start | bytes 786440 | tf_op jit(solution)/shard_map/ppermute | solution.py:594
  61.1 6.1 %u_grad.2.refs_2_.refs_5_ = bf16[8192,1024]{1,0:T(8,128)(2,1)} custom-call(bf16[4096,512]{1,0:T(8,128)(2,1)S(1)} %turn_hidden.2.refs_2_.refs_0_, bf16[128,1024]{1,0:T(8,128)(2,1)S(1)} %collective-permute-done.11.refs_1_.refs_2_, bf16[128,1024]{1,0:T(8,128)(2,1)S(1)} %collective-permute-done.13.refs_2_.refs_3_, ...), custom_call_target="tpu_custom_call" | custom-call | flops 7646444544 | tf_op jit(solution)/shard_map/u_grad/pallas_call | solution.py:41
  67.3 1.2 collective-permute-done.14.refs_1_
  68.5 0.1 pieces_of.3
  68.6 1.7 %collective-permute-start.15 = (bf16[32,1024]{1,0:T(8,128)(2,1)S(1)}, bf16[32,1024]{1,0:T(8,128)(2,1)S(1)}, u32[]{:S(2)}, u32[]{:S(2)}) collective-permute-start(bf16[32,1024]{1,0:T(8,128)(2,1)S(1)} %get-tuple-element.79), channel_id=1, source_target_pairs={{0,4},{2,6},{4,0},{6,2},{8,12},{10,14},{12,8},{14,10},{1,5},{3,7},... | collective-permute-start | bytes 196616 | tf_op jit(solution)/shard_map/ppermute | solution.py:594
  70.3 1.7 %collective-permute-start.16 = (bf16[32,1024]{1,0:T(8,128)(2,1)S(1)}, bf16[32,1024]{1,0:T(8,128)(2,1)S(1)}, u32[]{:S(2)}, u32[]{:S(2)}) collective-permute-start(bf16[32,1024]{1,0:T(8,128)(2,1)S(1)} %get-tuple-element.80), channel_id=1, source_target_pairs={{0,8},{2,10},{4,12},{6,14},{8,0},{10,2},{12,4},{14,6},{1,9},{3,11}... | collective-permute-start | bytes 196616 | tf_op jit(solution)/shard_map/ppermute | solution.py:594
  72.0 1.0 collective-permute-start.17
  73.0 6.2 %u_grad.3 = (bf16[8192,1024]{1,0:T(8,128)(2,1)}, bf16[1024,1024]{1,0:T(8,128)(2,1)S(1)}) custom-call(bf16[4096,512]{1,0:T(8,128)(2,1)S(1)} %turn_hidden.3.refs_4_.refs_0_, bf16[128,1024]{1,0:T(8,128)(2,1)S(1)} %collective-permute-done.11.refs_1_.refs_2_, ...), custom_call_target="tpu_custom_call", output_to_operand_aliasing={{0}: (5, {})} | custom-call | flops 7646444544 | tf_op jit(solution)/shard_map/u_grad/pallas_call | solution.py:41
  79.2 2.9 %collective-permute-start.20 = (bf16[32,1024]{1,0:T(8,128)(2,1)S(1)}, bf16[32,1024]{1,0:T(8,128)(2,1)S(1)}, u32[]{:S(2)}, u32[]{:S(2)}) collective-permute-start(bf16[32,1024]{1,0:T(8,128)(2,1)S(1)} %add_pieces.3.refs_7_.refs_0_), channel_id=1, source_target_pairs={{0,12},{2,14},{4,8},{6,10},{8,4},{10,6},{12,0},{14,2},{1,13},{3,15... | collective-permute-start | bytes 196616 | tf_op jit(solution)/shard_map/ppermute | solution.py:594
  82.1 1.6 %collective-permute-start.18 = (bf16[32,1024]{1,0:T(8,128)(2,1)S(1)}, bf16[32,1024]{1,0:T(8,128)(2,1)S(1)}, u32[]{:S(2)}, u32[]{:S(2)}) collective-permute-start(bf16[32,1024]{1,0:T(8,128)(2,1)S(1)} %add_pieces.3.refs_7_.refs_0_), channel_id=1, source_target_pairs={{0,4},{2,6},{4,0},{6,2},{8,12},{10,14},{12,8},{14,10},{1,5},{3,7},... | collective-permute-start | bytes 196616 | tf_op jit(solution)/shard_map/ppermute | solution.py:594
  83.7 6.4 %expand.2 = (f32[512,4096]{1,0:T(8,128)S(1)}, bf16[1024,1024]{1,0:T(8,128)(2,1)S(1)}) custom-call(bf16[8192,1024]{1,0:T(8,128)(2,1)} %refs_0_.7, bf16[1024,1024]{1,0:T(8,128)(2,1)S(1)} %get-tuple-element.78.refs_1_, bf16[128,1024]{1,0:T(8,128)(2,1)S(1)} %collective-permute-done.11.refs_1_.refs_2_, ...), custom_call_target="tpu_custom_call" | custom-call | flops 7646444544 | tf_op jit(solution)/shard_map/expand/pallas_call | solution.py:41
  90.2 1.4 %collective-permute-start.22 = (bf16[128,1024]{1,0:T(8,128)(2,1)S(1)}, bf16[128,1024]{1,0:T(8,128)(2,1)S(1)}, u32[]{:S(2)}, u32[]{:S(2)}) collective-permute-start(bf16[128,1024]{1,0:T(8,128)(2,1)S(1)} %join_pieces.3.refs_7_.refs_8_.refs_3_), channel_id=1, source_target_pairs={{0,2},{2,0},{4,6},{6,4},{8,10},{10,8},{12,14},{14,12},{1,3},{3,1},... | collective-permute-start | bytes 786440 | tf_op jit(solution)/shard_map/ppermute | solution.py:594
  91.6 6.6 %expand.3 = (f32[512,4096]{1,0:T(8,128)S(1)}, bf16[1024,1024]{1,0:T(8,128)(2,1)S(1)}) custom-call(bf16[8192,1024]{1,0:T(8,128)(2,1)} %refs_0_.7, bf16[1024,1024]{1,0:T(8,128)(2,1)S(1)} %get-tuple-element.83.refs_1_, bf16[128,1024]{1,0:T(8,128)(2,1)S(1)} %collective-permute-done.11.refs_1_.refs_2_, ...), custom_call_target="tpu_custom_call" | custom-call | flops 7646444544 | tf_op jit(solution)/shard_map/expand/pallas_call | solution.py:41
  98.3 0.6 collective-permute-start.23
  98.8 0.2 copy-done
  99.0 0.9 collective-permute-done.23.refs_7_.refs_2_
  100.0 6.8 %input_grad.2 = (bf16[256,16384]{1,0:T(8,128)(2,1)}, bf16[256,4096]{1,0:T(8,128)(2,1)S(1)}, bf16[1024,1024]{1,0:T(8,128)(2,1)S(1)}) custom-call(bf16[256,4096]{1,0:T(8,128)(2,1)S(1)} %get-tuple-element.57.refs_2_.refs_0_, bf16[256,8192]{1,0:T(8,128)(2,1)S(1)} %collective-permute-done.2.refs_3_.refs_1_, f32[512,4096]{1,0:T(8,128)S(1)} %get-tuple-element.84.refs_4_.refs_2_, ...), custom_call_target="tpu_custom_call" | custom-call | flops 7646444544 | tf_op jit(solution)/shard_map/input_grad/pallas_call | solution.py:41
  106.8 0.4 collective-permute-start.24
  107.2 7.4 %input_grad.3 = (bf16[256,16384]{1,0:T(8,128)(2,1)}, bf16[256,4096]{1,0:T(8,128)(2,1)S(1)}, bf16[4096,512]{1,0:T(8,128)(2,1)S(1)}) custom-call(bf16[256,4096]{1,0:T(8,128)(2,1)S(1)} %get-tuple-element.60.refs_2_.refs_0_, bf16[256,8192]{1,0:T(8,128)(2,1)S(1)} %collective-permute-done.2.refs_3_.refs_1_, ...), custom_call_target="tpu_custom_call", output_to_operand_aliasing={{0}: (10, {})} | custom-call | flops 7646444544 | tf_op jit(solution)/shard_map/input_grad/pallas_call | solution.py:41
  114.6 0.2 collective-permute-start.25
  114.8 6.2 %v_grad.2 = (bf16[8192,1024]{1,0:T(8,128)(2,1)}, bf16[256,16384]{1,0:T(8,128)(2,1)}, bf16[4096,512]{1,0:T(8,128)(2,1)S(1)}) custom-call(bf16[4096,512]{1,0:T(8,128)(2,1)S(1)} %get-tuple-element.89.refs_0_, bf16[128,1024]{1,0:T(8,128)(2,1)S(1)} %collective-permute-done.21.refs_6_.refs_1_, ...), custom_call_target="tpu_custom_call", output_to_operand_aliasing={{1}: (6, {})} | custom-call | flops 345000000 | tf_op jit(solution)/shard_map/v_grad/pallas_call | solution.py:41
  121.0 6.2 %v_grad.3 = (bf16[8192,1024]{1,0:T(8,128)(2,1)}, bf16[256,16384]{1,0:T(8,128)(2,1)}) custom-call(bf16[4096,512]{1,0:T(8,128)(2,1)S(1)} %get-tuple-element.92.refs_0_, bf16[128,1024]{1,0:T(8,128)(2,1)S(1)} %collective-permute-done.21.refs_6_.refs_1_, ...), custom_call_target="tpu_custom_call", output_to_operand_aliasing={{0}: (5, {}), {1}: (7, {})} | custom-call | flops 7646444544 | tf_op jit(solution)/shard_map/v_grad/pallas_call | solution.py:41
  (34 shorter events, 0.2 us)
Async XLA Ops:
  2.9 11.8 %collective-permute-start = (bf16[256,8192]{1,0:T(8,128)(2,1)S(1)}, bf16[256,8192]{1,0:T(8,128)(2,1)S(1)}, u32[]{:S(2)}, u32[]{:S(2)}) collective-permute-start(bf16[256,8192]{1,0:T(8,128)(2,1)S(1)} %cut_half.1.refs_3_), channel_id=1, source_target_pairs={{0,1},{1,0},{2,3},{3,2},{4,5},{5,4},{6,7},{7,6},{8,9},{9,8},{10,11... | collective-permute-start | bytes 12582920 | tf_op jit(solution)/shard_map/ppermute | solution.py:591
  12.5 2.0 %collective-permute-start.1 = (bf16[256,1024]{1,0:T(8,128)(2,1)S(1)}, bf16[256,1024]{1,0:T(8,128)(2,1)S(1)}, u32[]{:S(2)}, u32[]{:S(2)}) collective-permute-start(bf16[256,1024]{1,0:T(8,128)(2,1)S(1)} %get-tuple-element.52), channel_id=1, source_target_pairs={{0,1},{1,0},{2,3},{3,2},{4,5},{5,4},{6,7},{7,6},{8,9},{9,8},{10,11... | collective-permute-start | bytes 1572872 | tf_op jit(solution)/shard_map/ppermute | solution.py:591
  14.5 8.6 %collective-permute-start.2 = (bf16[256,8192]{1,0:T(8,128)(2,1)S(1)}, bf16[256,8192]{1,0:T(8,128)(2,1)S(1)}, u32[]{:S(2)}, u32[]{:S(2)}) collective-permute-start(bf16[256,8192]{1,0:T(8,128)(2,1)S(1)} %hold.3), channel_id=1, source_target_pairs={{0,1},{1,0},{2,3},{3,2},{4,5},{5,4},{6,7},{7,6},{8,9},{9,8},{10,11... | collective-permute-start | bytes 12582920 | tf_op jit(solution)/shard_map/ppermute | solution.py:591
  20.2 9.9 %collective-permute-start.3 = (bf16[128,1024]{1,0:T(8,128)(2,1)S(1)}, bf16[128,1024]{1,0:T(8,128)(2,1)S(1)}, u32[]{:S(2)}, u32[]{:S(2)}) collective-permute-start(bf16[128,1024]{1,0:T(8,128)(2,1)S(1)} %get-tuple-element.64), channel_id=1, source_target_pairs={{0,2},{2,0},{4,6},{6,4},{8,10},{10,8},{12,14},{14,12},{1,3},{3,1},... | collective-permute-start | bytes 786440 | tf_op jit(solution)/shard_map/ppermute | solution.py:594
  30.2 11.5 %collective-permute-start.4 = (bf16[32,1024]{1,0:T(8,128)(2,1)S(1)}, bf16[32,1024]{1,0:T(8,128)(2,1)S(1)}, u32[]{:S(2)}, u32[]{:S(2)}) collective-permute-start(bf16[32,1024]{1,0:T(8,128)(2,1)S(1)} %get-tuple-element.67), channel_id=1, source_target_pairs={{0,4},{2,6},{4,0},{6,2},{8,12},{10,14},{12,8},{14,10},{1,5},{3,7},... | collective-permute-start | bytes 196616 | tf_op jit(solution)/shard_map/ppermute | solution.py:594
  31.8 9.9 %collective-permute-start.5 = (bf16[32,1024]{1,0:T(8,128)(2,1)S(1)}, bf16[32,1024]{1,0:T(8,128)(2,1)S(1)}, u32[]{:S(2)}, u32[]{:S(2)}) collective-permute-start(bf16[32,1024]{1,0:T(8,128)(2,1)S(1)} %get-tuple-element.68), channel_id=1, source_target_pairs={{0,8},{2,10},{4,12},{6,14},{8,0},{10,2},{12,4},{14,6},{1,9},{3,11}... | collective-permute-start | bytes 196616 | tf_op jit(solution)/shard_map/ppermute | solution.py:594
  34.4 7.3 %collective-permute-start.6 = (bf16[32,1024]{1,0:T(8,128)(2,1)S(1)}, bf16[32,1024]{1,0:T(8,128)(2,1)S(1)}, u32[]{:S(2)}, u32[]{:S(2)}) collective-permute-start(bf16[32,1024]{1,0:T(8,128)(2,1)S(1)} %get-tuple-element.69), channel_id=1, source_target_pairs={{0,12},{2,14},{4,8},{6,10},{8,4},{10,6},{12,0},{14,2},{1,13},{3,15... | collective-permute-start | bytes 196616 | tf_op jit(solution)/shard_map/ppermute | solution.py:594
  41.8 6.1 %collective-permute-start.7 = (bf16[256,1024]{1,0:T(8,128)(2,1)S(1)}, bf16[256,1024]{1,0:T(8,128)(2,1)S(1)}, u32[]{:S(2)}, u32[]{:S(2)}) collective-permute-start(bf16[256,1024]{1,0:T(8,128)(2,1)S(1)} %get-tuple-element.71), channel_id=1, source_target_pairs={{0,1},{1,0},{2,3},{3,2},{4,5},{5,4},{6,7},{7,6},{8,9},{9,8},{10,11... | collective-permute-start | bytes 1572872 | tf_op jit(solution)/shard_map/ppermute | solution.py:591
  41.9 7.7 %collective-permute-start.10 = (bf16[32,1024]{1,0:T(8,128)(2,1)S(1)}, bf16[32,1024]{1,0:T(8,128)(2,1)S(1)}, u32[]{:S(2)}, u32[]{:S(2)}) collective-permute-start(bf16[32,1024]{1,0:T(8,128)(2,1)S(1)} %get-tuple-element.72.refs_4_.refs_0_), channel_id=1, source_target_pairs={{0,12},{2,14},{4,8},{6,10},{8,4},{10,6},{12,0},{14,2},{1,13},{3,15... | collective-permute-start | bytes 196616 | tf_op jit(solution)/shard_map/ppermute | solution.py:594
  45.5 5.6 %collective-permute-start.9 = (bf16[32,1024]{1,0:T(8,128)(2,1)S(1)}, bf16[32,1024]{1,0:T(8,128)(2,1)S(1)}, u32[]{:S(2)}, u32[]{:S(2)}) collective-permute-start(bf16[32,1024]{1,0:T(8,128)(2,1)S(1)} %get-tuple-element.72.refs_4_.refs_0_), channel_id=1, source_target_pairs={{0,8},{2,10},{4,12},{6,14},{8,0},{10,2},{12,4},{14,6},{1,9},{3,11}... | collective-permute-start | bytes 196616 | tf_op jit(solution)/shard_map/ppermute | solution.py:594
  45.5 5.7 %collective-permute-start.8 = (bf16[32,1024]{1,0:T(8,128)(2,1)S(1)}, bf16[32,1024]{1,0:T(8,128)(2,1)S(1)}, u32[]{:S(2)}, u32[]{:S(2)}) collective-permute-start(bf16[32,1024]{1,0:T(8,128)(2,1)S(1)} %get-tuple-element.72.refs_4_.refs_0_), channel_id=1, source_target_pairs={{0,4},{2,6},{4,0},{6,2},{8,12},{10,14},{12,8},{14,10},{1,5},{3,7},... | collective-permute-start | bytes 196616 | tf_op jit(solution)/shard_map/ppermute | solution.py:594
  51.3 7.9 %collective-permute-start.12 = (bf16[128,1024]{1,0:T(8,128)(2,1)S(1)}, bf16[128,1024]{1,0:T(8,128)(2,1)S(1)}, u32[]{:S(2)}, u32[]{:S(2)}) collective-permute-start(bf16[128,1024]{1,0:T(8,128)(2,1)S(1)} %join_pieces.2.refs_2_.refs_3_.refs_4_), channel_id=1, source_target_pairs={{0,2},{2,0},{4,6},{6,4},{8,10},{10,8},{12,14},{14,12},{1,3},{3,1},... | collective-permute-start | bytes 786440 | tf_op jit(solution)/shard_map/ppermute | solution.py:594
  52.7 8.4 %collective-permute-start.11 = (bf16[128,1024]{1,0:T(8,128)(2,1)S(1)}, bf16[128,1024]{1,0:T(8,128)(2,1)S(1)}, u32[]{:S(2)}, u32[]{:S(2)}) collective-permute-start(bf16[128,1024]{1,0:T(8,128)(2,1)S(1)} %join_pieces.2.refs_2_.refs_3_.refs_4_), channel_id=1, source_target_pairs={{0,1},{1,0},{2,3},{3,2},{4,5},{5,4},{6,7},{7,6},{8,9},{9,8},{10,11... | collective-permute-start | bytes 786440 | tf_op jit(solution)/shard_map/ppermute | solution.py:591
  59.1 2.0 %collective-permute-start.13 = (bf16[128,1024]{1,0:T(8,128)(2,1)S(1)}, bf16[128,1024]{1,0:T(8,128)(2,1)S(1)}, u32[]{:S(2)}, u32[]{:S(2)}) collective-permute-start(bf16[128,1024]{1,0:T(8,128)(2,1)S(1)} %hold.4.refs_4_.refs_5_), channel_id=1, source_target_pairs={{0,1},{1,0},{2,3},{3,2},{4,5},{5,4},{6,7},{7,6},{8,9},{9,8},{10,11... | collective-permute-start | bytes 786440 | tf_op jit(solution)/shard_map/ppermute | solution.py:591
  59.8 8.7 %collective-permute-start.14 = (bf16[128,1024]{1,0:T(8,128)(2,1)S(1)}, bf16[128,1024]{1,0:T(8,128)(2,1)S(1)}, u32[]{:S(2)}, u32[]{:S(2)}) collective-permute-start(bf16[128,1024]{1,0:T(8,128)(2,1)S(1)} %get-tuple-element.76), channel_id=1, source_target_pairs={{0,2},{2,0},{4,6},{6,4},{8,10},{10,8},{12,14},{14,12},{1,3},{3,1},... | collective-permute-start | bytes 786440 | tf_op jit(solution)/shard_map/ppermute | solution.py:594
  68.6 10.6 %collective-permute-start.15 = (bf16[32,1024]{1,0:T(8,128)(2,1)S(1)}, bf16[32,1024]{1,0:T(8,128)(2,1)S(1)}, u32[]{:S(2)}, u32[]{:S(2)}) collective-permute-start(bf16[32,1024]{1,0:T(8,128)(2,1)S(1)} %get-tuple-element.79), channel_id=1, source_target_pairs={{0,4},{2,6},{4,0},{6,2},{8,12},{10,14},{12,8},{14,10},{1,5},{3,7},... | collective-permute-start | bytes 196616 | tf_op jit(solution)/shard_map/ppermute | solution.py:594
  70.3 8.9 %collective-permute-start.16 = (bf16[32,1024]{1,0:T(8,128)(2,1)S(1)}, bf16[32,1024]{1,0:T(8,128)(2,1)S(1)}, u32[]{:S(2)}, u32[]{:S(2)}) collective-permute-start(bf16[32,1024]{1,0:T(8,128)(2,1)S(1)} %get-tuple-element.80), channel_id=1, source_target_pairs={{0,8},{2,10},{4,12},{6,14},{8,0},{10,2},{12,4},{14,6},{1,9},{3,11}... | collective-permute-start | bytes 196616 | tf_op jit(solution)/shard_map/ppermute | solution.py:594
  72.0 7.2 %collective-permute-start.17 = (bf16[32,1024]{1,0:T(8,128)(2,1)S(1)}, bf16[32,1024]{1,0:T(8,128)(2,1)S(1)}, u32[]{:S(2)}, u32[]{:S(2)}) collective-permute-start(bf16[32,1024]{1,0:T(8,128)(2,1)S(1)} %get-tuple-element.81), channel_id=1, source_target_pairs={{0,12},{2,14},{4,8},{6,10},{8,4},{10,6},{12,0},{14,2},{1,13},{3,15... | collective-permute-start | bytes 196616 | tf_op jit(solution)/shard_map/ppermute | solution.py:594
  79.2 10.9 %collective-permute-start.20 = (bf16[32,1024]{1,0:T(8,128)(2,1)S(1)}, bf16[32,1024]{1,0:T(8,128)(2,1)S(1)}, u32[]{:S(2)}, u32[]{:S(2)}) collective-permute-start(bf16[32,1024]{1,0:T(8,128)(2,1)S(1)} %add_pieces.3.refs_7_.refs_0_), channel_id=1, source_target_pairs={{0,12},{2,14},{4,8},{6,10},{8,4},{10,6},{12,0},{14,2},{1,13},{3,15... | collective-permute-start | bytes 196616 | tf_op jit(solution)/shard_map/ppermute | solution.py:594
  82.1 8.0 %collective-permute-start.19 = (bf16[32,1024]{1,0:T(8,128)(2,1)S(1)}, bf16[32,1024]{1,0:T(8,128)(2,1)S(1)}, u32[]{:S(2)}, u32[]{:S(2)}) collective-permute-start(bf16[32,1024]{1,0:T(8,128)(2,1)S(1)} %add_pieces.3.refs_7_.refs_0_), channel_id=1, source_target_pairs={{0,8},{2,10},{4,12},{6,14},{8,0},{10,2},{12,4},{14,6},{1,9},{3,11}... | collective-permute-start | bytes 196616 | tf_op jit(solution)/shard_map/ppermute | solution.py:594
  82.1 8.1 %collective-permute-start.18 = (bf16[32,1024]{1,0:T(8,128)(2,1)S(1)}, bf16[32,1024]{1,0:T(8,128)(2,1)S(1)}, u32[]{:S(2)}, u32[]{:S(2)}) collective-permute-start(bf16[32,1024]{1,0:T(8,128)(2,1)S(1)} %add_pieces.3.refs_7_.refs_0_), channel_id=1, source_target_pairs={{0,4},{2,6},{4,0},{6,2},{8,12},{10,14},{12,8},{14,10},{1,5},{3,7},... | collective-permute-start | bytes 196616 | tf_op jit(solution)/shard_map/ppermute | solution.py:594
  90.2 8.0 %collective-permute-start.22 = (bf16[128,1024]{1,0:T(8,128)(2,1)S(1)}, bf16[128,1024]{1,0:T(8,128)(2,1)S(1)}, u32[]{:S(2)}, u32[]{:S(2)}) collective-permute-start(bf16[128,1024]{1,0:T(8,128)(2,1)S(1)} %join_pieces.3.refs_7_.refs_8_.refs_3_), channel_id=1, source_target_pairs={{0,2},{2,0},{4,6},{6,4},{8,10},{10,8},{12,14},{14,12},{1,3},{3,1},... | collective-permute-start | bytes 786440 | tf_op jit(solution)/shard_map/ppermute | solution.py:594
  91.6 7.4 %collective-permute-start.21 = (bf16[128,1024]{1,0:T(8,128)(2,1)S(1)}, bf16[128,1024]{1,0:T(8,128)(2,1)S(1)}, u32[]{:S(2)}, u32[]{:S(2)}) collective-permute-start(bf16[128,1024]{1,0:T(8,128)(2,1)S(1)} %join_pieces.3.refs_7_.refs_8_.refs_3_), channel_id=1, source_target_pairs={{0,1},{1,0},{2,3},{3,2},{4,5},{5,4},{6,7},{7,6},{8,9},{9,8},{10,11... | collective-permute-start | bytes 786440 | tf_op jit(solution)/shard_map/ppermute | solution.py:591
  98.2 0.8 copy-start
  98.3 1.7 %collective-permute-start.23 = (bf16[128,1024]{1,0:T(8,128)(2,1)S(1)}, bf16[128,1024]{1,0:T(8,128)(2,1)S(1)}, u32[]{:S(2)}, u32[]{:S(2)}) collective-permute-start(bf16[128,1024]{1,0:T(8,128)(2,1)S(1)} %hold.5.refs_9_.refs_4_), channel_id=1, source_target_pairs={{0,1},{1,0},{2,3},{3,2},{4,5},{5,4},{6,7},{7,6},{8,9},{9,8},{10,11... | collective-permute-start | bytes 786440 | tf_op jit(solution)/shard_map/ppermute | solution.py:591
  106.8 8.0 %collective-permute-start.24 = (bf16[256,4096]{1,0:T(8,128)(2,1)S(1)}, bf16[256,4096]{1,0:T(8,128)(2,1)S(1)}, u32[]{:S(2)}, u32[]{:S(2)}) collective-permute-start(bf16[256,4096]{1,0:T(8,128)(2,1)S(1)} %get-tuple-element.90), channel_id=1, source_target_pairs={{0,1},{1,0},{2,3},{3,2},{4,5},{5,4},{6,7},{7,6},{8,9},{9,8},{10,11... | collective-permute-start | bytes 6291464 | tf_op jit(solution)/shard_map/ppermute | solution.py:591
  114.6 6.4 %collective-permute-start.25 = (bf16[256,4096]{1,0:T(8,128)(2,1)S(1)}, bf16[256,4096]{1,0:T(8,128)(2,1)S(1)}, u32[]{:S(2)}, u32[]{:S(2)}) collective-permute-start(bf16[256,4096]{1,0:T(8,128)(2,1)S(1)} %get-tuple-element.94), channel_id=1, source_target_pairs={{0,1},{1,0},{2,3},{3,2},{4,5},{5,4},{6,7},{7,6},{8,9},{9,8},{10,11... | collective-permute-start | bytes 6291464 | tf_op jit(solution)/shard_map/ppermute | solution.py:591

commit v3 on v2

--- a/solution.py
+++ b/solution.py
@@ -88,25 +88,19 @@
 VPARTS = 4
 
 
-def project_own(x, v, c, after=()):
+def project_own(x, v, after=()):
     rows, (half, rank) = x.shape[0], v.shape
     part = half // VPARTS
     tk = min(1024, part)
     n = half // tk
     each = part // tk
 
-    def body(at_ref, x_ref, v_ref, c_ref, p_ref, xv_ref, cs_ref, *refs):
-        vv, (acc, x_sem, v_sem, c_sem) = refs[:VPARTS], refs[VPARTS:]
-
-        def cut(ref, dst, core, k, sem):
-            src = ref.at[:, pl.ds(pl.multiple_of(core * half + k * tk, tk), tk)]
-            return copy(src, dst.at[:, at_block(k, tk)], sem.at[k])
+    def body(at_ref, x_ref, v_ref, p_ref, xv_ref, *refs):
+        vv, (acc, x_sem, v_sem) = refs[:VPARTS], refs[VPARTS:]
 
         def x_copy(k):
-            return cut(x_ref, xv_ref, at_ref[0], k, x_sem)
-
-        def c_copy(k):
-            return cut(c_ref, cs_ref, 1 - at_ref[0], k, c_sem)
+            src = x_ref.at[:, pl.ds(pl.multiple_of(at_ref[0] * half + k * tk, tk), tk)]
+            return copy(src, xv_ref.at[:, at_block(k, tk)], x_sem.at[k])
 
         def v_copy(k, i, j):
             return copy(v_ref.at[at_block(k, tk), :], vv[i].at[at_block(j, tk), :], v_sem.at[k])
@@ -114,8 +108,6 @@
         for k in range(n):
             x_copy(k).start()
             v_copy(k, k // each, k % each).start()
-        for k in range(n):
-            c_copy(k).start()
         acc[...] = jnp.zeros_like(acc)
         for i in range(VPARTS):
 
@@ -127,15 +119,13 @@
                 acc[...] += jnp.dot(xv_ref[:, at_block(k, tk)], vv[i][at_block(j, tk), :], preferred_element_type=F32)
 
         p_ref[...] = acc[...].astype(BF)
-        for k in range(n):
-            c_copy(k).wait()
 
     return call(
         body,
         "project_own",
-        [(x, "h"), (v, "h"), (c, "h")],
-        [((rows, rank), BF, "v"), ((rows, half), BF, "v"), ((rows, half), BF, "v")] + [((part, rank), BF, "v")] * VPARTS,
-        [pltpu.VMEM((rows, rank), F32)] + [dma(n)] * 3,
+        [(x, "h"), (v, "h")],
+        [((rows, rank), BF, "v"), ((rows, half), BF, "v")] + [((part, rank), BF, "v")] * VPARTS,
+        [pltpu.VMEM((rows, rank), F32)] + [dma(n)] * 2,
         flops=2 * rows * half * rank,
         mib=8,
         after=after,
@@ -608,9 +598,9 @@
         tw = min(1024, part)
         x_s = cut_half(x, half)
         x_o = trade(x_s)
-        own, x_own, c_s, *v_in = project_own(x, v, c, [x_s])
+        own, x_own, *v_in = project_own(x, v, [x_s])
         theirs = trade(own)
-        c_o = trade(hold(c_s, [theirs]))
+        c_o = trade(hold(cut_half(c, half, [own]), [theirs]))
         *sums, c0, u0 = project_other(x_o, v_in, theirs, c, u, direct)
         acc, b0, c1, u1 = back_project(0, x_own, x_o, c0, c_o, u, u0, None, c)
         if direct:
@@ -626,7 +616,7 @@
             other_p = hold(other_p, [(x_t, "h")])
             grad_b = jnp.concatenate([b0[0], b1[0]])
             p = [trade(half_p), trade(other_p), half_p, other_p]
-            (grad_u,) = factor_grad("u_grad", 0, half, h_t0, p, None, after=[(x_t, "h"), (grad_b, "h")])
+            (grad_u,) = factor_grad("u_grad", 0, half, h_t0, p, None, after=[(x_t, "h")])
             parts_g = pieces_of(sums_g[0], to(sums_g[1], 1), m, [(grad_u, "h")])
             grad_u, u0 = factor_grad("u_grad", 1, half, h_t1, p, grad_u, after=[parts_g[0]], ahead=[(u, 0, tw)])
             (total_g,) = add_pieces(spread(parts_g), [(grad_u, "h")])
@@ -649,7 +639,7 @@
             ex0, u1 = expand(0, u, u0, p, ahead=[(u, part, tw)])
             ex1, v0 = expand(1, u, u1, p, ahead=[(v, 0, tw)])
         bias = bias[None, :]
-        out, oth0, v1 = input_grad(0, c0, c_o, ex0, v, v0, bias, g, None, width, [ex1], [(v, part, tw)])
+        out, oth0, v1 = input_grad(0, c0, c_o, ex0, v, v0, bias, g, None, width, [ex1, (grad_b, "h")], [(v, part, tw)])
         out, oth1, x_t0 = input_grad(1, c1, c_o, ex1, v, v1, bias, g, out, width, ahead=[(x_t, 0, part)])
         back0, back1 = trade(oth0), trade(oth1)
         grad_v, out, x_t1 = factor_grad("v_grad", 0, half, x_t0, g, None, (back0, out), ahead=[(x_t, part, part)], work=0)

time: 128 us -> 127 us (level)
  waiting for transfers between devices: 8.04 us -> 5.42 us
    ppermute x10, waiting for transfers between devices: 2.82 us -> 0.4 us  [trade(): return lax.ppermute(a, 'batch', swap)]
    pallas_call x26 -> x27, Pallas kernels: 90.3 us -> 91.4 us  [call(): pl.pallas_call(whole if n_ahead else lambda *refs: body(Place(), *refs[:n...]
  transfers between devices with their start and end apart: 26 -> 26, of which waited for: 6 -> 5; matrix products, arithmetic and copies ran while one was open for 1% -> 1% of each run, Pallas kernels for 59% -> 60%
where the time goes in v3:
time: 127 us; the launch traced here: 126 us
  Pallas kernels  91.4 us (72%)
  starting transfers between devices  27.6 us (22%)
  waiting for transfers between devices  5.42 us (4%)
    pallas_call x27, Pallas kernels, call(): pl.pallas_call(whole if n_ahead else lambda *refs: body(Place(), *refs[:n...  91.4 us
    ppermute x16, starting transfers between devices, to(): return lax.ppermute(a, 'col', [(i, i ^ d) for i in range(n)])  25.1 us
    ppermute x16, waiting for transfers between devices, to(): return lax.ppermute(a, 'col', [(i, i ^ d) for i in range(n)])  5.02 us
  transfers between devices with their start and end apart: 26, of which 5 were waited for; matrix products, arithmetic and copies ran while one was open for 1% of the time, Pallas kernels for 60%

profile of v3, /device:TPU:0, one launch (start us, length us, event | category | flops | bytes accessed | tf_op | source)
XLA Modules:
  0.0 126.3 jit_solution(15626223850773507957)
XLA Ops:
  0.6 2.2 %cut_half.2.refs_2_ = bf16[256,8192]{1,0:T(8,128)(2,1)S(1)} custom-call(bf16[256,16384]{1,0:T(8,128)(2,1)} %refs_0_.6), custom_call_target="tpu_custom_call" | custom-call | flops 2529999872 | tf_op jit(solution)/shard_map/cut_half/pallas_call | solution.py:41
  2.9 0.5 collective-permute-start
  3.4 8.0 %project_own.1 = (bf16[256,1024]{1,0:T(8,128)(2,1)S(1)}, bf16[256,8192]{1,0:T(8,128)(2,1)S(1)}, bf16[2048,1024]{1,0:T(8,128)(2,1)S(1)}, bf16[2048,1024]{1,0:T(8,...) custom-call(bf16[256,16384]{1,0:T(8,128)(2,1)} %refs_0_.6, bf16[8192,1024]{1,0:T(8,128)(2,1)} %refs_3_.3, ...), custom_call_target="tpu_custom_call" | custom-call | flops 7646444544 | tf_op jit(solution)/shard_map/project_own/pallas_call | solution.py:41
  11.4 0.1 collective-permute-start.1
  11.5 2.2 %cut_half.3.refs_0_ = bf16[256,8192]{1,0:T(8,128)(2,1)S(1)} custom-call(bf16[256,16384]{1,0:T(8,128)(2,1)} %refs_6_.4, bf16[256,1024]{1,0:T(8,128)(2,1)S(1)} %get-tuple-element.51.refs_1_), custom_call_target="tpu_custom_call" | custom-call | flops 2529999872 | tf_op jit(solution)/shard_map/cut_half/pallas_call | solution.py:41
  13.7 0.5 collective-permute-start.2
  14.2 5.6 %project_other.1 = (bf16[128,1024]{1,0:T(8,128)(2,1)S(1)}, bf16[128,1024]{1,0:T(8,128)(2,1)S(1)}, bf16[256,4096]{1,0:T(8,128)(2,1)S(1)}, bf16[1024,1024]{1,0:T(8,128)(2,1)S(1)}) custom-call(bf16[256,8192]{1,0:T(8,128)(2,1)S(1)} %collective-permute-done.refs_0_.refs_1_, bf16[256,1024]{1,0:T(8,128)(2,1)S(1)} %collective-permute-done.1.refs_1_, ...), custom_call_target="tpu_custom_call" | custom-call | flops 7646444544 | tf_op jit(solution)/shard_map/project_other/pallas_call | solution.py:41
  19.8 2.6 %collective-permute-start.3 = (bf16[128,1024]{1,0:T(8,128)(2,1)S(1)}, bf16[128,1024]{1,0:T(8,128)(2,1)S(1)}, u32[]{:S(2)}, u32[]{:S(2)}) collective-permute-start(bf16[128,1024]{1,0:T(8,128)(2,1)S(1)} %get-tuple-element.62), channel_id=1, source_target_pairs={{0,2},{2,0},{4,6},{6,4},{8,10},{10,8},{12,14},{14,12},{1,3},{3,1},... | collective-permute-start | bytes 786440 | tf_op jit(solution)/shard_map/ppermute | solution.py:584
  22.4 6.9 %back_project.2 = (f32[512,1024]{1,0:T(8,128)S(1)}, f32[1,4096]{1,0:T(1,128)S(1)}, bf16[256,4096]{1,0:T(8,128)(2,1)S(1)}, bf16[1024,1024]{1,0:T(8,128)(2,1)S(1)}) custom-call(bf16[256,8192]{1,0:T(8,128)(2,1)S(1)} %get-tuple-element.50.refs_0_, bf16[256,8192]{1,0:T(8,128)(2,1)S(1)} %collective-permute-done.refs_0_.refs_1_, ...), custom_call_target="tpu_custom_call" | custom-call | flops 7646444544 | tf_op jit(solution)/shard_map/back_project/pallas_call | solution.py:41
  29.4 0.1 pieces_of.2
  29.4 1.9 %collective-permute-start.4 = (bf16[32,1024]{1,0:T(8,128)(2,1)S(1)}, bf16[32,1024]{1,0:T(8,128)(2,1)S(1)}, u32[]{:S(2)}, u32[]{:S(2)}) collective-permute-start(bf16[32,1024]{1,0:T(8,128)(2,1)S(1)} %get-tuple-element.65), channel_id=1, source_target_pairs={{0,4},{2,6},{4,0},{6,2},{8,12},{10,14},{12,8},{14,10},{1,5},{3,7},... | collective-permute-start | bytes 196616 | tf_op jit(solution)/shard_map/ppermute | solution.py:584
  31.3 2.6 %collective-permute-start.5 = (bf16[32,1024]{1,0:T(8,128)(2,1)S(1)}, bf16[32,1024]{1,0:T(8,128)(2,1)S(1)}, u32[]{:S(2)}, u32[]{:S(2)}) collective-permute-start(bf16[32,1024]{1,0:T(8,128)(2,1)S(1)} %get-tuple-element.66), channel_id=1, source_target_pairs={{0,8},{2,10},{4,12},{6,14},{8,0},{10,2},{12,4},{14,6},{1,9},{3,11}... | collective-permute-start | bytes 196616 | tf_op jit(solution)/shard_map/ppermute | solution.py:584
  33.9 7.1 %back_project.3 = (bf16[256,1024]{1,0:T(8,128)(2,1)S(1)}, f32[256,1024]{1,0:T(8,128)S(1)}, f32[1,4096]{1,0:T(1,128)S(1)}) custom-call(bf16[256,8192]{1,0:T(8,128)(2,1)S(1)} %get-tuple-element.50.refs_0_, bf16[256,8192]{1,0:T(8,128)(2,1)S(1)} %collective-permute-done.refs_0_.refs_1_, bf16[256,4096]{1,0:T(8,128)(2,1)S(1)} %get-tuple-element.58.refs_2_.refs_0_, ...), custom_call_target="tpu_custom_call" | custom-call | flops 7646444544 | tf_op jit(solution)/shard_map/back_project/pallas_call | solution.py:41
  41.1 0.1 collective-permute-start.7
  41.1 3.9 %collective-permute-start.10 = (bf16[32,1024]{1,0:T(8,128)(2,1)S(1)}, bf16[32,1024]{1,0:T(8,128)(2,1)S(1)}, u32[]{:S(2)}, u32[]{:S(2)}) collective-permute-start(bf16[32,1024]{1,0:T(8,128)(2,1)S(1)} %get-tuple-element.70.refs_4_.refs_0_), channel_id=1, source_target_pairs={{0,12},{2,14},{4,8},{6,10},{8,4},{10,6},{12,0},{14,2},{1,13},{3,15... | collective-permute-start | bytes 196616 | tf_op jit(solution)/shard_map/ppermute | solution.py:584
  45.0 0.6 collective-permute-start.8
  45.7 1.6 %turn_hidden.2.refs_2_.refs_0_ = bf16[4096,512]{1,0:T(8,128)(2,1)S(1)} custom-call(bf16[256,8192]{1,0:T(8,128)(2,1)S(1)} %get-tuple-element.50.refs_0_, bf16[256,8192]{1,0:T(8,128)(2,1)S(1)} %collective-permute-done.refs_0_.refs_1_, bf16[256,4096]{1,0:T(8,128)(2,1)S(1)} %get-tuple-element.56.refs_2_.refs_0_, ...), custom_call_target="tpu_custom_call" | custom-call | flops 2070000000 | tf_op jit(solution)/shard_map/turn_hidden/pallas_call | solution.py:41
  47.2 0.1 pair_halves.1
  47.3 1.6 %turn_hidden.3.refs_4_.refs_0_ = bf16[4096,512]{1,0:T(8,128)(2,1)S(1)} custom-call(bf16[256,8192]{1,0:T(8,128)(2,1)S(1)} %get-tuple-element.50.refs_0_, bf16[256,8192]{1,0:T(8,128)(2,1)S(1)} %collective-permute-done.refs_0_.refs_1_, bf16[256,4096]{1,0:T(8,128)(2,1)S(1)} %get-tuple-element.58.refs_2_.refs_0_, ...), custom_call_target="tpu_custom_call" | custom-call | flops 2070000000 | tf_op jit(solution)/shard_map/turn_hidden/pallas_call | solution.py:41
  48.9 1.7 %collective-permute-done.9.refs_2_ = bf16[32,1024]{1,0:T(8,128)(2,1)S(1)} collective-permute-done((bf16[32,1024]{1,0:T(8,128)(2,1)S(1)}, bf16[32,1024]{1,0:T(8,128)(2,1)S(1)}, u32[]{:S(2)}, u32[]{:S(2)}) %collective-permute-start.9) | collective-permute-done | bytes 65568 | tf_op jit(solution)/shard_map/ppermute | solution.py:584
  50.6 0.1 collective-permute-done.8.refs_1_
  50.7 1.6 %collective-permute-start.12 = (bf16[128,1024]{1,0:T(8,128)(2,1)S(1)}, bf16[128,1024]{1,0:T(8,128)(2,1)S(1)}, u32[]{:S(2)}, u32[]{:S(2)}) collective-permute-start(bf16[128,1024]{1,0:T(8,128)(2,1)S(1)} %join_pieces.2.refs_2_.refs_3_.refs_4_), channel_id=1, source_target_pairs={{0,2},{2,0},{4,6},{6,4},{8,10},{10,8},{12,14},{14,12},{1,3},{3,1},... | collective-permute-start | bytes 786440 | tf_op jit(solution)/shard_map/ppermute | solution.py:584
  52.3 4.1 %turn_x.1.refs_1_.refs_5_.refs_11_.refs_7_ = bf16[8192,512]{1,0:T(8,128)(2,1)} custom-call(bf16[256,8192]{1,0:T(8,128)(2,1)S(1)} %get-tuple-element.50.refs_0_, bf16[256,8192]{1,0:T(8,128)(2,1)S(1)} %collective-permute-done.refs_0_.refs_1_, bf16[128,1024]{1,0:T(8,128)(2,1)S(1)} %join_pieces.2.refs_2_.refs_3_.refs_4_), custom_call_target="tpu_custom_call" | custom-call | flops 4140000000 | tf_op jit(solution)/shard_map/turn_x/pallas_call | solution.py:41
  56.5 2.2 %collective-permute-done.12.refs_0_ = bf16[128,1024]{1,0:T(8,128)(2,1)S(1)} collective-permute-done((bf16[128,1024]{1,0:T(8,128)(2,1)S(1)}, bf16[128,1024]{1,0:T(8,128)(2,1)S(1)}, u32[]{:S(2)}, u32[]{:S(2)}) %collective-permute-start.12) | collective-permute-done | bytes 262176 | tf_op jit(solution)/shard_map/ppermute | solution.py:584
  58.7 1.5 %collective-permute-start.14 = (bf16[128,1024]{1,0:T(8,128)(2,1)S(1)}, bf16[128,1024]{1,0:T(8,128)(2,1)S(1)}, u32[]{:S(2)}, u32[]{:S(2)}) collective-permute-start(bf16[128,1024]{1,0:T(8,128)(2,1)S(1)} %get-tuple-element.72), channel_id=1, source_target_pairs={{0,2},{2,0},{4,6},{6,4},{8,10},{10,8},{12,14},{14,12},{1,3},{3,1},... | collective-permute-start | bytes 786440 | tf_op jit(solution)/shard_map/ppermute | solution.py:584
  60.1 0.0 collective-permute-done.13.refs_2_.refs_3_
  60.2 6.1 %u_grad.2.refs_2_.refs_5_ = bf16[8192,1024]{1,0:T(8,128)(2,1)} custom-call(bf16[4096,512]{1,0:T(8,128)(2,1)S(1)} %turn_hidden.2.refs_2_.refs_0_, bf16[128,1024]{1,0:T(8,128)(2,1)S(1)} %collective-permute-done.11.refs_1_.refs_2_, bf16[128,1024]{1,0:T(8,128)(2,1)S(1)} %collective-permute-done.13.refs_2_.refs_3_, ...), custom_call_target="tpu_custom_call" | custom-call | flops 7646444544 | tf_op jit(solution)/shard_map/u_grad/pallas_call | solution.py:41
  66.3 1.0 collective-permute-done.14.refs_1_
  67.4 0.1 pieces_of.3
  67.4 1.7 %collective-permute-start.15 = (bf16[32,1024]{1,0:T(8,128)(2,1)S(1)}, bf16[32,1024]{1,0:T(8,128)(2,1)S(1)}, u32[]{:S(2)}, u32[]{:S(2)}) collective-permute-start(bf16[32,1024]{1,0:T(8,128)(2,1)S(1)} %get-tuple-element.75), channel_id=1, source_target_pairs={{0,4},{2,6},{4,0},{6,2},{8,12},{10,14},{12,8},{14,10},{1,5},{3,7},... | collective-permute-start | bytes 196616 | tf_op jit(solution)/shard_map/ppermute | solution.py:584
  69.1 1.7 %collective-permute-start.16 = (bf16[32,1024]{1,0:T(8,128)(2,1)S(1)}, bf16[32,1024]{1,0:T(8,128)(2,1)S(1)}, u32[]{:S(2)}, u32[]{:S(2)}) collective-permute-start(bf16[32,1024]{1,0:T(8,128)(2,1)S(1)} %get-tuple-element.76), channel_id=1, source_target_pairs={{0,8},{2,10},{4,12},{6,14},{8,0},{10,2},{12,4},{14,6},{1,9},{3,11}... | collective-permute-start | bytes 196616 | tf_op jit(solution)/shard_map/ppermute | solution.py:584
  70.9 1.0 collective-permute-start.17
  71.9 6.2 %u_grad.3 = (bf16[8192,1024]{1,0:T(8,128)(2,1)}, bf16[1024,1024]{1,0:T(8,128)(2,1)S(1)}) custom-call(bf16[4096,512]{1,0:T(8,128)(2,1)S(1)} %turn_hidden.3.refs_4_.refs_0_, bf16[128,1024]{1,0:T(8,128)(2,1)S(1)} %collective-permute-done.11.refs_1_.refs_2_, ...), custom_call_target="tpu_custom_call", output_to_operand_aliasing={{0}: (5, {})} | custom-call | flops 7646444544 | tf_op jit(solution)/shard_map/u_grad/pallas_call | solution.py:41
  78.1 2.9 %collective-permute-start.20 = (bf16[32,1024]{1,0:T(8,128)(2,1)S(1)}, bf16[32,1024]{1,0:T(8,128)(2,1)S(1)}, u32[]{:S(2)}, u32[]{:S(2)}) collective-permute-start(bf16[32,1024]{1,0:T(8,128)(2,1)S(1)} %add_pieces.3.refs_7_.refs_0_), channel_id=1, source_target_pairs={{0,12},{2,14},{4,8},{6,10},{8,4},{10,6},{12,0},{14,2},{1,13},{3,15... | collective-permute-start | bytes 196616 | tf_op jit(solution)/shard_map/ppermute | solution.py:584
  81.0 1.6 %collective-permute-start.18 = (bf16[32,1024]{1,0:T(8,128)(2,1)S(1)}, bf16[32,1024]{1,0:T(8,128)(2,1)S(1)}, u32[]{:S(2)}, u32[]{:S(2)}) collective-permute-start(bf16[32,1024]{1,0:T(8,128)(2,1)S(1)} %add_pieces.3.refs_7_.refs_0_), channel_id=1, source_target_pairs={{0,4},{2,6},{4,0},{6,2},{8,12},{10,14},{12,8},{14,10},{1,5},{3,7},... | collective-permute-start | bytes 196616 | tf_op jit(solution)/shard_map/ppermute | solution.py:584
  82.6 6.4 %expand.2 = (f32[512,4096]{1,0:T(8,128)S(1)}, bf16[1024,1024]{1,0:T(8,128)(2,1)S(1)}) custom-call(bf16[8192,1024]{1,0:T(8,128)(2,1)} %refs_0_.9, bf16[1024,1024]{1,0:T(8,128)(2,1)S(1)} %get-tuple-element.74.refs_1_, bf16[128,1024]{1,0:T(8,128)(2,1)S(1)} %collective-permute-done.11.refs_1_.refs_2_, ...), custom_call_target="tpu_custom_call" | custom-call | flops 7646444544 | tf_op jit(solution)/shard_map/expand/pallas_call | solution.py:41
  89.1 1.6 %collective-permute-start.22 = (bf16[128,1024]{1,0:T(8,128)(2,1)S(1)}, bf16[128,1024]{1,0:T(8,128)(2,1)S(1)}, u32[]{:S(2)}, u32[]{:S(2)}) collective-permute-start(bf16[128,1024]{1,0:T(8,128)(2,1)S(1)} %join_pieces.3.refs_7_.refs_8_.refs_3_), channel_id=1, source_target_pairs={{0,2},{2,0},{4,6},{6,4},{8,10},{10,8},{12,14},{14,12},{1,3},{3,1},... | collective-permute-start | bytes 786440 | tf_op jit(solution)/shard_map/ppermute | solution.py:584
  90.6 6.6 %expand.3 = (f32[512,4096]{1,0:T(8,128)S(1)}, bf16[1024,1024]{1,0:T(8,128)(2,1)S(1)}) custom-call(bf16[8192,1024]{1,0:T(8,128)(2,1)} %refs_0_.9, bf16[1024,1024]{1,0:T(8,128)(2,1)S(1)} %get-tuple-element.79.refs_1_, bf16[128,1024]{1,0:T(8,128)(2,1)S(1)} %collective-permute-done.11.refs_1_.refs_2_, ...), custom_call_target="tpu_custom_call" | custom-call | flops 7646444544 | tf_op jit(solution)/shard_map/expand/pallas_call | solution.py:41
  97.3 0.6 collective-permute-start.23
  97.8 0.2 copy-done
  98.0 0.6 pad_maximum_fusion.refs_12_
  98.7 0.3 collective-permute-done.23.refs_7_.refs_2_
  99.0 6.8 %input_grad.2 = (bf16[256,16384]{1,0:T(8,128)(2,1)}, bf16[256,4096]{1,0:T(8,128)(2,1)S(1)}, bf16[1024,1024]{1,0:T(8,128)(2,1)S(1)}) custom-call(bf16[256,4096]{1,0:T(8,128)(2,1)S(1)} %get-tuple-element.56.refs_2_.refs_0_, bf16[256,8192]{1,0:T(8,128)(2,1)S(1)} %collective-permute-done.2.refs_3_.refs_1_, f32[512,4096]{1,0:T(8,128)S(1)} %get-tuple-element.80.refs_4_.refs_2_, ...), custom_call_target="tpu_custom_call" | custom-call | flops 7646444544 | tf_op jit(solution)/shard_map/input_grad/pallas_call | solution.py:41
  105.8 0.4 collective-permute-start.24
  106.2 7.4 %input_grad.3 = (bf16[256,16384]{1,0:T(8,128)(2,1)}, bf16[256,4096]{1,0:T(8,128)(2,1)S(1)}, bf16[4096,512]{1,0:T(8,128)(2,1)S(1)}) custom-call(bf16[256,4096]{1,0:T(8,128)(2,1)S(1)} %get-tuple-element.58.refs_2_.refs_0_, bf16[256,8192]{1,0:T(8,128)(2,1)S(1)} %collective-permute-done.2.refs_3_.refs_1_, ...), custom_call_target="tpu_custom_call", output_to_operand_aliasing={{0}: (10, {})} | custom-call | flops 7646444544 | tf_op jit(solution)/shard_map/input_grad/pallas_call | solution.py:41
  113.6 0.2 collective-permute-start.25
  113.8 6.2 %v_grad.2 = (bf16[8192,1024]{1,0:T(8,128)(2,1)}, bf16[256,16384]{1,0:T(8,128)(2,1)}, bf16[4096,512]{1,0:T(8,128)(2,1)S(1)}) custom-call(bf16[4096,512]{1,0:T(8,128)(2,1)S(1)} %get-tuple-element.87.refs_0_, bf16[128,1024]{1,0:T(8,128)(2,1)S(1)} %collective-permute-done.21.refs_6_.refs_1_, ...), custom_call_target="tpu_custom_call", output_to_operand_aliasing={{1}: (6, {})} | custom-call | flops 345000000 | tf_op jit(solution)/shard_map/v_grad/pallas_call | solution.py:41
  120.0 6.2 %v_grad.3 = (bf16[8192,1024]{1,0:T(8,128)(2,1)}, bf16[256,16384]{1,0:T(8,128)(2,1)}) custom-call(bf16[4096,512]{1,0:T(8,128)(2,1)S(1)} %get-tuple-element.90.refs_0_, bf16[128,1024]{1,0:T(8,128)(2,1)S(1)} %collective-permute-done.21.refs_6_.refs_1_, ...), custom_call_target="tpu_custom_call", output_to_operand_aliasing={{0}: (5, {}), {1}: (7, {})} | custom-call | flops 7646444544 | tf_op jit(solution)/shard_map/v_grad/pallas_call | solution.py:41
  (35 shorter events, 0.3 us)
Async XLA Ops:
  2.9 11.4 %collective-permute-start = (bf16[256,8192]{1,0:T(8,128)(2,1)S(1)}, bf16[256,8192]{1,0:T(8,128)(2,1)S(1)}, u32[]{:S(2)}, u32[]{:S(2)}) collective-permute-start(bf16[256,8192]{1,0:T(8,128)(2,1)S(1)} %cut_half.2.refs_2_), channel_id=1, source_target_pairs={{0,1},{1,0},{2,3},{3,2},{4,5},{5,4},{6,7},{7,6},{8,9},{9,8},{10,11... | collective-permute-start | bytes 12582920 | tf_op jit(solution)/shard_map/ppermute | solution.py:581
  11.4 2.3 %collective-permute-start.1 = (bf16[256,1024]{1,0:T(8,128)(2,1)S(1)}, bf16[256,1024]{1,0:T(8,128)(2,1)S(1)}, u32[]{:S(2)}, u32[]{:S(2)}) collective-permute-start(bf16[256,1024]{1,0:T(8,128)(2,1)S(1)} %get-tuple-element.51.refs_1_), channel_id=1, source_target_pairs={{0,1},{1,0},{2,3},{3,2},{4,5},{5,4},{6,7},{7,6},{8,9},{9,8},{10,11... | collective-permute-start | bytes 1572872 | tf_op jit(solution)/shard_map/ppermute | solution.py:581
  13.7 8.7 %collective-permute-start.2 = (bf16[256,8192]{1,0:T(8,128)(2,1)S(1)}, bf16[256,8192]{1,0:T(8,128)(2,1)S(1)}, u32[]{:S(2)}, u32[]{:S(2)}) collective-permute-start(bf16[256,8192]{1,0:T(8,128)(2,1)S(1)} %hold.3), channel_id=1, source_target_pairs={{0,1},{1,0},{2,3},{3,2},{4,5},{5,4},{6,7},{7,6},{8,9},{9,8},{10,11... | collective-permute-start | bytes 12582920 | tf_op jit(solution)/shard_map/ppermute | solution.py:581
  19.8 9.5 %collective-permute-start.3 = (bf16[128,1024]{1,0:T(8,128)(2,1)S(1)}, bf16[128,1024]{1,0:T(8,128)(2,1)S(1)}, u32[]{:S(2)}, u32[]{:S(2)}) collective-permute-start(bf16[128,1024]{1,0:T(8,128)(2,1)S(1)} %get-tuple-element.62), channel_id=1, source_target_pairs={{0,2},{2,0},{4,6},{6,4},{8,10},{10,8},{12,14},{14,12},{1,3},{3,1},... | collective-permute-start | bytes 786440 | tf_op jit(solution)/shard_map/ppermute | solution.py:584
  29.4 11.5 %collective-permute-start.4 = (bf16[32,1024]{1,0:T(8,128)(2,1)S(1)}, bf16[32,1024]{1,0:T(8,128)(2,1)S(1)}, u32[]{:S(2)}, u32[]{:S(2)}) collective-permute-start(bf16[32,1024]{1,0:T(8,128)(2,1)S(1)} %get-tuple-element.65), channel_id=1, source_target_pairs={{0,4},{2,6},{4,0},{6,2},{8,12},{10,14},{12,8},{14,10},{1,5},{3,7},... | collective-permute-start | bytes 196616 | tf_op jit(solution)/shard_map/ppermute | solution.py:584
  31.3 9.7 %collective-permute-start.5 = (bf16[32,1024]{1,0:T(8,128)(2,1)S(1)}, bf16[32,1024]{1,0:T(8,128)(2,1)S(1)}, u32[]{:S(2)}, u32[]{:S(2)}) collective-permute-start(bf16[32,1024]{1,0:T(8,128)(2,1)S(1)} %get-tuple-element.66), channel_id=1, source_target_pairs={{0,8},{2,10},{4,12},{6,14},{8,0},{10,2},{12,4},{14,6},{1,9},{3,11}... | collective-permute-start | bytes 196616 | tf_op jit(solution)/shard_map/ppermute | solution.py:584
  33.9 7.1 %collective-permute-start.6 = (bf16[32,1024]{1,0:T(8,128)(2,1)S(1)}, bf16[32,1024]{1,0:T(8,128)(2,1)S(1)}, u32[]{:S(2)}, u32[]{:S(2)}) collective-permute-start(bf16[32,1024]{1,0:T(8,128)(2,1)S(1)} %get-tuple-element.67), channel_id=1, source_target_pairs={{0,12},{2,14},{4,8},{6,10},{8,4},{10,6},{12,0},{14,2},{1,13},{3,15... | collective-permute-start | bytes 196616 | tf_op jit(solution)/shard_map/ppermute | solution.py:584
  41.1 6.2 %collective-permute-start.7 = (bf16[256,1024]{1,0:T(8,128)(2,1)S(1)}, bf16[256,1024]{1,0:T(8,128)(2,1)S(1)}, u32[]{:S(2)}, u32[]{:S(2)}) collective-permute-start(bf16[256,1024]{1,0:T(8,128)(2,1)S(1)} %get-tuple-element.69), channel_id=1, source_target_pairs={{0,1},{1,0},{2,3},{3,2},{4,5},{5,4},{6,7},{7,6},{8,9},{9,8},{10,11... | collective-permute-start | bytes 1572872 | tf_op jit(solution)/shard_map/ppermute | solution.py:581
  41.1 7.8 %collective-permute-start.10 = (bf16[32,1024]{1,0:T(8,128)(2,1)S(1)}, bf16[32,1024]{1,0:T(8,128)(2,1)S(1)}, u32[]{:S(2)}, u32[]{:S(2)}) collective-permute-start(bf16[32,1024]{1,0:T(8,128)(2,1)S(1)} %get-tuple-element.70.refs_4_.refs_0_), channel_id=1, source_target_pairs={{0,12},{2,14},{4,8},{6,10},{8,4},{10,6},{12,0},{14,2},{1,13},{3,15... | collective-permute-start | bytes 196616 | tf_op jit(solution)/shard_map/ppermute | solution.py:584
  45.0 5.6 %collective-permute-start.9 = (bf16[32,1024]{1,0:T(8,128)(2,1)S(1)}, bf16[32,1024]{1,0:T(8,128)(2,1)S(1)}, u32[]{:S(2)}, u32[]{:S(2)}) collective-permute-start(bf16[32,1024]{1,0:T(8,128)(2,1)S(1)} %get-tuple-element.70.refs_4_.refs_0_), channel_id=1, source_target_pairs={{0,8},{2,10},{4,12},{6,14},{8,0},{10,2},{12,4},{14,6},{1,9},{3,11}... | collective-permute-start | bytes 196616 | tf_op jit(solution)/shard_map/ppermute | solution.py:584
  45.0 5.7 %collective-permute-start.8 = (bf16[32,1024]{1,0:T(8,128)(2,1)S(1)}, bf16[32,1024]{1,0:T(8,128)(2,1)S(1)}, u32[]{:S(2)}, u32[]{:S(2)}) collective-permute-start(bf16[32,1024]{1,0:T(8,128)(2,1)S(1)} %get-tuple-element.70.refs_4_.refs_0_), channel_id=1, source_target_pairs={{0,4},{2,6},{4,0},{6,2},{8,12},{10,14},{12,8},{14,10},{1,5},{3,7},... | collective-permute-start | bytes 196616 | tf_op jit(solution)/shard_map/ppermute | solution.py:584
  50.7 7.9 %collective-permute-start.12 = (bf16[128,1024]{1,0:T(8,128)(2,1)S(1)}, bf16[128,1024]{1,0:T(8,128)(2,1)S(1)}, u32[]{:S(2)}, u32[]{:S(2)}) collective-permute-start(bf16[128,1024]{1,0:T(8,128)(2,1)S(1)} %join_pieces.2.refs_2_.refs_3_.refs_4_), channel_id=1, source_target_pairs={{0,2},{2,0},{4,6},{6,4},{8,10},{10,8},{12,14},{14,12},{1,3},{3,1},... | collective-permute-start | bytes 786440 | tf_op jit(solution)/shard_map/ppermute | solution.py:584
  52.3 7.8 %collective-permute-start.11 = (bf16[128,1024]{1,0:T(8,128)(2,1)S(1)}, bf16[128,1024]{1,0:T(8,128)(2,1)S(1)}, u32[]{:S(2)}, u32[]{:S(2)}) collective-permute-start(bf16[128,1024]{1,0:T(8,128)(2,1)S(1)} %join_pieces.2.refs_2_.refs_3_.refs_4_), channel_id=1, source_target_pairs={{0,1},{1,0},{2,3},{3,2},{4,5},{5,4},{6,7},{7,6},{8,9},{9,8},{10,11... | collective-permute-start | bytes 786440 | tf_op jit(solution)/shard_map/ppermute | solution.py:581
  58.6 1.5 %collective-permute-start.13 = (bf16[128,1024]{1,0:T(8,128)(2,1)S(1)}, bf16[128,1024]{1,0:T(8,128)(2,1)S(1)}, u32[]{:S(2)}, u32[]{:S(2)}) collective-permute-start(bf16[128,1024]{1,0:T(8,128)(2,1)S(1)} %hold.4.refs_4_.refs_5_), channel_id=1, source_target_pairs={{0,1},{1,0},{2,3},{3,2},{4,5},{5,4},{6,7},{7,6},{8,9},{9,8},{10,11... | collective-permute-start | bytes 786440 | tf_op jit(solution)/shard_map/ppermute | solution.py:581
  58.7 8.7 %collective-permute-start.14 = (bf16[128,1024]{1,0:T(8,128)(2,1)S(1)}, bf16[128,1024]{1,0:T(8,128)(2,1)S(1)}, u32[]{:S(2)}, u32[]{:S(2)}) collective-permute-start(bf16[128,1024]{1,0:T(8,128)(2,1)S(1)} %get-tuple-element.72), channel_id=1, source_target_pairs={{0,2},{2,0},{4,6},{6,4},{8,10},{10,8},{12,14},{14,12},{1,3},{3,1},... | collective-permute-start | bytes 786440 | tf_op jit(solution)/shard_map/ppermute | solution.py:584
  67.4 10.6 %collective-permute-start.15 = (bf16[32,1024]{1,0:T(8,128)(2,1)S(1)}, bf16[32,1024]{1,0:T(8,128)(2,1)S(1)}, u32[]{:S(2)}, u32[]{:S(2)}) collective-permute-start(bf16[32,1024]{1,0:T(8,128)(2,1)S(1)} %get-tuple-element.75), channel_id=1, source_target_pairs={{0,4},{2,6},{4,0},{6,2},{8,12},{10,14},{12,8},{14,10},{1,5},{3,7},... | collective-permute-start | bytes 196616 | tf_op jit(solution)/shard_map/ppermute | solution.py:584
  69.1 8.9 %collective-permute-start.16 = (bf16[32,1024]{1,0:T(8,128)(2,1)S(1)}, bf16[32,1024]{1,0:T(8,128)(2,1)S(1)}, u32[]{:S(2)}, u32[]{:S(2)}) collective-permute-start(bf16[32,1024]{1,0:T(8,128)(2,1)S(1)} %get-tuple-element.76), channel_id=1, source_target_pairs={{0,8},{2,10},{4,12},{6,14},{8,0},{10,2},{12,4},{14,6},{1,9},{3,11}... | collective-permute-start | bytes 196616 | tf_op jit(solution)/shard_map/ppermute | solution.py:584
  70.9 7.2 %collective-permute-start.17 = (bf16[32,1024]{1,0:T(8,128)(2,1)S(1)}, bf16[32,1024]{1,0:T(8,128)(2,1)S(1)}, u32[]{:S(2)}, u32[]{:S(2)}) collective-permute-start(bf16[32,1024]{1,0:T(8,128)(2,1)S(1)} %get-tuple-element.77), channel_id=1, source_target_pairs={{0,12},{2,14},{4,8},{6,10},{8,4},{10,6},{12,0},{14,2},{1,13},{3,15... | collective-permute-start | bytes 196616 | tf_op jit(solution)/shard_map/ppermute | solution.py:584
  78.1 10.9 %collective-permute-start.20 = (bf16[32,1024]{1,0:T(8,128)(2,1)S(1)}, bf16[32,1024]{1,0:T(8,128)(2,1)S(1)}, u32[]{:S(2)}, u32[]{:S(2)}) collective-permute-start(bf16[32,1024]{1,0:T(8,128)(2,1)S(1)} %add_pieces.3.refs_7_.refs_0_), channel_id=1, source_target_pairs={{0,12},{2,14},{4,8},{6,10},{8,4},{10,6},{12,0},{14,2},{1,13},{3,15... | collective-permute-start | bytes 196616 | tf_op jit(solution)/shard_map/ppermute | solution.py:584
  81.0 8.0 %collective-permute-start.19 = (bf16[32,1024]{1,0:T(8,128)(2,1)S(1)}, bf16[32,1024]{1,0:T(8,128)(2,1)S(1)}, u32[]{:S(2)}, u32[]{:S(2)}) collective-permute-start(bf16[32,1024]{1,0:T(8,128)(2,1)S(1)} %add_pieces.3.refs_7_.refs_0_), channel_id=1, source_target_pairs={{0,8},{2,10},{4,12},{6,14},{8,0},{10,2},{12,4},{14,6},{1,9},{3,11}... | collective-permute-start | bytes 196616 | tf_op jit(solution)/shard_map/ppermute | solution.py:584
  81.0 8.0 %collective-permute-start.18 = (bf16[32,1024]{1,0:T(8,128)(2,1)S(1)}, bf16[32,1024]{1,0:T(8,128)(2,1)S(1)}, u32[]{:S(2)}, u32[]{:S(2)}) collective-permute-start(bf16[32,1024]{1,0:T(8,128)(2,1)S(1)} %add_pieces.3.refs_7_.refs_0_), channel_id=1, source_target_pairs={{0,4},{2,6},{4,0},{6,2},{8,12},{10,14},{12,8},{14,10},{1,5},{3,7},... | collective-permute-start | bytes 196616 | tf_op jit(solution)/shard_map/ppermute | solution.py:584
  89.1 8.1 %collective-permute-start.22 = (bf16[128,1024]{1,0:T(8,128)(2,1)S(1)}, bf16[128,1024]{1,0:T(8,128)(2,1)S(1)}, u32[]{:S(2)}, u32[]{:S(2)}) collective-permute-start(bf16[128,1024]{1,0:T(8,128)(2,1)S(1)} %join_pieces.3.refs_7_.refs_8_.refs_3_), channel_id=1, source_target_pairs={{0,2},{2,0},{4,6},{6,4},{8,10},{10,8},{12,14},{14,12},{1,3},{3,1},... | collective-permute-start | bytes 786440 | tf_op jit(solution)/shard_map/ppermute | solution.py:584
  90.6 8.0 %collective-permute-start.21 = (bf16[128,1024]{1,0:T(8,128)(2,1)S(1)}, bf16[128,1024]{1,0:T(8,128)(2,1)S(1)}, u32[]{:S(2)}, u32[]{:S(2)}) collective-permute-start(bf16[128,1024]{1,0:T(8,128)(2,1)S(1)} %join_pieces.3.refs_7_.refs_8_.refs_3_), channel_id=1, source_target_pairs={{0,1},{1,0},{2,3},{3,2},{4,5},{5,4},{6,7},{7,6},{8,9},{9,8},{10,11... | collective-permute-start | bytes 786440 | tf_op jit(solution)/shard_map/ppermute | solution.py:581
  97.2 0.8 copy-start
  97.3 1.7 %collective-permute-start.23 = (bf16[128,1024]{1,0:T(8,128)(2,1)S(1)}, bf16[128,1024]{1,0:T(8,128)(2,1)S(1)}, u32[]{:S(2)}, u32[]{:S(2)}) collective-permute-start(bf16[128,1024]{1,0:T(8,128)(2,1)S(1)} %hold.5.refs_9_.refs_4_), channel_id=1, source_target_pairs={{0,1},{1,0},{2,3},{3,2},{4,5},{5,4},{6,7},{7,6},{8,9},{9,8},{10,11... | collective-permute-start | bytes 786440 | tf_op jit(solution)/shard_map/ppermute | solution.py:581
  105.8 8.0 %collective-permute-start.24 = (bf16[256,4096]{1,0:T(8,128)(2,1)S(1)}, bf16[256,4096]{1,0:T(8,128)(2,1)S(1)}, u32[]{:S(2)}, u32[]{:S(2)}) collective-permute-start(bf16[256,4096]{1,0:T(8,128)(2,1)S(1)} %get-tuple-element.88), channel_id=1, source_target_pairs={{0,1},{1,0},{2,3},{3,2},{4,5},{5,4},{6,7},{7,6},{8,9},{9,8},{10,11... | collective-permute-start | bytes 6291464 | tf_op jit(solution)/shard_map/ppermute | solution.py:581
  113.6 6.4 %collective-permute-start.25 = (bf16[256,4096]{1,0:T(8,128)(2,1)S(1)}, bf16[256,4096]{1,0:T(8,128)(2,1)S(1)}, u32[]{:S(2)}, u32[]{:S(2)}) collective-permute-start(bf16[256,4096]{1,0:T(8,128)(2,1)S(1)} %get-tuple-element.92), channel_id=1, source_target_pairs={{0,1},{1,0},{2,3},{3,2},{4,5},{5,4},{6,7},{7,6},{8,9},{9,8},{10,11... | collective-permute-start | bytes 6291464 | tf_op jit(solution)/shard_map/ppermute | solution.py:581

commit v4 on v3

--- a/solution.py
+++ b/solution.py
@@ -178,24 +178,25 @@
     return (c.astype(F32) * x.astype(F32)).astype(BF)
 
 
-def back_project(s, x, x_o, c, c_o, u, u_first, so_far, c_all=None, after=()):
+def back_project(lo, n, x, x_o, c, c_o, u, u_first, so_far, c_all=None, after=()):
     rows, (half, rank) = x.shape[0], u.shape
-    part = half // 2
+    part = c.shape[1]
     tk = u_first.shape[0]
-    n = part // tk
-    first = so_far is None
-    n_outs = 2 if first else 3
+    shift = lo * tk % part
+    first, last = so_far is None, (lo + n) * tk == half
 
     def body(at_ref, x_ref, xo_ref, c_ref, co_ref, u_ref, uf_ref, *refs, fetch=nothing):
         if first:
             all_ref, acc_ref, b_ref, next_ref, uv, h, u_sem, c_sem = refs
             src = all_ref.at[:, pl.ds(pl.multiple_of(at_ref[0] * half + part, part), part)]
             next_c = copy(src, next_ref, c_sem.at[0])
+        elif last:
+            so_ref, own_ref, oth_ref, b_ref, uv, h, u_sem = refs
         else:
-            so_ref, own_ref, oth_ref, b_ref, uv, h, u_sem = refs
+            so_ref, acc_ref, b_ref, uv, h, u_sem = refs
 
         def u_copy(k):
-            return copy(u_ref.at[pl.ds(s * part + k * tk, tk), :], uv.at[k - 1], u_sem.at[k - 1])
+            return copy(u_ref.at[pl.ds((lo + k) * tk, tk), :], uv.at[k - 1], u_sem.at[k - 1])
 
         for k in range(1, n):
             u_copy(k).start()
@@ -204,12 +205,13 @@
         fetch()
         for k in range(n):
             here = pl.ds(k * tk, tk)
-            there = pl.ds(s * part + k * tk, tk)
-            own = hidden(c_ref[:, here], x_ref[:, there])
+            there = pl.ds((lo + k) * tk, tk)
+            own = hidden(c_ref[:, pl.ds(shift + k * tk, tk)], x_ref[:, there])
             oth = hidden(co_ref[:, there], xo_ref[:, there])
             h[k, :rows, :] = own
             h[k, rows:, :] = oth
             b_ref[:, here] = jnp.sum(own.astype(F32), axis=0, keepdims=True) + jnp.sum(oth.astype(F32), axis=0, keepdims=True)
+
         @pl.loop(0, 2)
         def _(i):
             at_rows = at_block(i, rows)
@@ -223,7 +225,7 @@
 
                 term = jnp.dot(h[k, at_rows, :], uv[k - 1] if k else uf_ref[...], preferred_element_type=F32)
                 total = term if total is None else total + term
-            if first:
+            if not last:
                 acc_ref[at_rows, :] = total
             else:
 
@@ -238,8 +240,8 @@
         if first:
             next_c.wait()
 
-    outs = [((2 * rows, rank), F32, "v")] if first else [((rows, rank), BF, "v"), ((rows, rank), F32, "v")]
-    outs += [((1, part), F32, "v")] + ([((rows, part), BF, "v")] if first else [])
+    outs = [((rows, rank), BF, "v"), ((rows, rank), F32, "v")] if last else [((2 * rows, rank), F32, "v")]
+    outs += [((1, n * tk), F32, "v")] + ([((rows, part), BF, "v")] if first else [])
     return call(
         body,
         "back_project",
@@ -247,10 +249,10 @@
         outs,
         [pltpu.VMEM((max(1, n - 1), tk, rank), BF), pltpu.VMEM((n, 2 * rows, tk), BF), dma(max(1, n - 1))]
         + ([dma(1)] if first else []),
-        flops=2 * rows * half * rank,
-        mib=15,
+        flops=4 * rows * n * tk * rank,
+        mib=15 if first else 12,
         after=after,
-        ahead=[(u, part, tk)] if first else [],
+        ahead=[] if last else [(u, (lo + n) * tk, tk)],
     )
 
 
@@ -554,7 +556,7 @@
     return call(body, "add_pieces", [(a, "v") for a in parts], [(parts[0].shape, BF, "v")], after=after, carry=carry)
 
 
-def join_pieces(parts, after=()):
+def join_pieces(parts, after=(), carry=()):
     m = len(parts)
     each, rank = parts[0].shape
 
@@ -562,7 +564,7 @@
         for d in range(m):
             refs[-1][at_block((at_ref[1] >> 1) ^ d, each), :] = refs[d][...]
 
-    return call(body, "join_pieces", [(a, "v") for a in parts], [((m * each, rank), BF, "v")], after=after)[0]
+    return call(body, "join_pieces", [(a, "v") for a in parts], [((m * each, rank), BF, "v")], after=after, carry=carry)
 
 
 def hold(a, after):
@@ -602,35 +604,37 @@
         theirs = trade(own)
         c_o = trade(hold(cut_half(c, half, [own]), [theirs]))
         *sums, c0, u0 = project_other(x_o, v_in, theirs, c, u, direct)
-        acc, b0, c1, u1 = back_project(0, x_own, x_o, c0, c_o, u, u0, None, c)
+        acc, b0, c1, u1 = back_project(0, 4, x_own, x_o, c0, c_o, u, u0, None, c)
         if direct:
             parts = pieces_of(sums[0], to(sums[1], 1), m, [acc])
-            own_g, mine_g, b1 = back_project(1, x_own, x_o, c1, c_o, u, u1, acc, after=[parts[0]])
-            total, own_g = add_pieces(spread(parts), carry=[own_g])
-            (h_t0,) = turn_hidden(0, x_own, x_o, c0, c_o, [total])
-            sums_g = pair_halves(mine_g, trade(own_g), direct, [h_t0])
-            (h_t1,) = turn_hidden(1, x_own, x_o, c1, c_o, [sums_g[0]])
-            half_p = join_pieces(spread([total] * m), [h_t1])
+            acc, b1, u1 = back_project(4, 2, x_own, x_o, c1, c_o, u, u1, acc, after=[parts[0]])
+            (h_t0,) = turn_hidden(0, x_own, x_o, c0, c_o, [acc])
+            (total,) = add_pieces(spread(parts), [h_t0])
+            own_g, mine_g, b2 = back_project(6, 2, x_own, x_o, c1, c_o, u, u1, acc, after=[total])
+            (h_t1,) = turn_hidden(1, x_own, x_o, c1, c_o, [mine_g])
+            half_p, own_g = join_pieces(spread([total] * m), [h_t1], [own_g])
             other_p = to(half_p, 1)
             x_t = turn_x(x_own, x_o, [half_p])
+            sums_g = pair_halves(mine_g, trade(own_g), direct, [(x_t, "h")])
             other_p = hold(other_p, [(x_t, "h")])
-            grad_b = jnp.concatenate([b0[0], b1[0]])
+            grad_b = jnp.concatenate([b0[0], b1[0], b2[0]])
             p = [trade(half_p), trade(other_p), half_p, other_p]
             (grad_u,) = factor_grad("u_grad", 0, half, h_t0, p, None, after=[(x_t, "h")])
             parts_g = pieces_of(sums_g[0], to(sums_g[1], 1), m, [(grad_u, "h")])
             grad_u, u0 = factor_grad("u_grad", 1, half, h_t1, p, grad_u, after=[parts_g[0]], ahead=[(u, 0, tw)])
             (total_g,) = add_pieces(spread(parts_g), [(grad_u, "h")])
             ex0, u1 = expand(0, u, u0, p, [total_g], [(u, part, tw)])
-            half_g = join_pieces(spread([total_g] * m), [ex0])
+            (half_g,) = join_pieces(spread([total_g] * m), [ex0])
             other_g = to(half_g, 1)
             ex1, v0 = expand(1, u, u1, p, [half_g], [(v, 0, tw)])
             other_g = hold(other_g, [ex1])
             g = [trade(half_g), trade(other_g), half_g, other_g]
         else:
-            own_g, mine_g, b1 = back_project(1, x_own, x_o, c1, c_o, u, u1, acc)
+            acc, b1, u1 = back_project(4, 2, x_own, x_o, c1, c_o, u, u1, acc)
+            own_g, mine_g, b2 = back_project(6, 2, x_own, x_o, c1, c_o, u, u1, acc)
             (sums_g,) = pair_halves(mine_g, trade(own_g), direct)
             p, g = plain(sums[0]), plain(sums_g)
-            grad_b = jnp.concatenate([b0[0], b1[0]])
+            grad_b = jnp.concatenate([b0[0], b1[0], b2[0]])
             x_t = turn_x(x_own, x_o)
             (h_t0,) = turn_hidden(0, x_own, x_o, c0, c_o)
             (h_t1,) = turn_hidden(1, x_own, x_o, c1, c_o)

time: 127 us -> 125 us (0.984)
  waiting for transfers between devices: 5.42 us -> 2.44 us
    ppermute x16, waiting for transfers between devices: 5.02 us -> 2.08 us  [to(): return lax.ppermute(a, 'col', [(i, i ^ d) for i in range(n)])]
    pallas_call x27 -> x28, Pallas kernels: 91.4 us -> 91.9 us  [call(): pl.pallas_call(whole if n_ahead else lambda *refs: body(Place(), *refs[:n...]
  transfers between devices with their start and end apart: 26 -> 26, of which waited for: 5 -> 4; matrix products, arithmetic and copies ran while one was open for 1% -> 1% of each run, Pallas kernels for 60% -> 62%
where the time goes in v4:
time: 125 us; the launch traced here: 124 us
  Pallas kernels  91.9 us (74%)
  starting transfers between devices  27.9 us (22%)
  waiting for transfers between devices  2.44 us (2%)
    pallas_call x28, Pallas kernels, call(): pl.pallas_call(whole if n_ahead else lambda *refs: body(Place(), *refs[:n...  91.9 us
    ppermute x16, starting transfers between devices, to(): return lax.ppermute(a, 'col', [(i, i ^ d) for i in range(n)])  25 us
    ppermute x10, starting transfers between devices, trade(): return lax.ppermute(a, 'batch', swap)  2.88 us
  transfers between devices with their start and end apart: 26, of which 4 were waited for; matrix products, arithmetic and copies ran while one was open for 1% of the time, Pallas kernels for 62%

profile of v4, /device:TPU:0, one launch (start us, length us, event | category | flops | bytes accessed | tf_op | source)
XLA Modules:
  0.0 124.3 jit_solution(414903317958032801)
XLA Ops:
  0.6 2.2 %cut_half.2.refs_2_ = bf16[256,8192]{1,0:T(8,128)(2,1)S(1)} custom-call(bf16[256,16384]{1,0:T(8,128)(2,1)} %refs_0_.6), custom_call_target="tpu_custom_call" | custom-call | flops 2529999872 | tf_op jit(solution)/shard_map/cut_half/pallas_call | solution.py:41
  2.9 0.5 collective-permute-start
  3.4 8.0 %project_own.1 = (bf16[256,1024]{1,0:T(8,128)(2,1)S(1)}, bf16[256,8192]{1,0:T(8,128)(2,1)S(1)}, bf16[2048,1024]{1,0:T(8,128)(2,1)S(1)}, bf16[2048,1024]{1,0:T(8,...) custom-call(bf16[256,16384]{1,0:T(8,128)(2,1)} %refs_0_.6, bf16[8192,1024]{1,0:T(8,128)(2,1)} %refs_3_.3, ...), custom_call_target="tpu_custom_call" | custom-call | flops 7646444544 | tf_op jit(solution)/shard_map/project_own/pallas_call | solution.py:41
  11.4 0.1 collective-permute-start.1
  11.5 2.2 %cut_half.3.refs_0_ = bf16[256,8192]{1,0:T(8,128)(2,1)S(1)} custom-call(bf16[256,16384]{1,0:T(8,128)(2,1)} %refs_6_.4, bf16[256,1024]{1,0:T(8,128)(2,1)S(1)} %get-tuple-element.54.refs_1_), custom_call_target="tpu_custom_call" | custom-call | flops 2529999872 | tf_op jit(solution)/shard_map/cut_half/pallas_call | solution.py:41
  13.7 0.5 collective-permute-start.2
  14.2 5.6 %project_other.1 = (bf16[128,1024]{1,0:T(8,128)(2,1)S(1)}, bf16[128,1024]{1,0:T(8,128)(2,1)S(1)}, bf16[256,4096]{1,0:T(8,128)(2,1)S(1)}, bf16[1024,1024]{1,0:T(8,128)(2,1)S(1)}) custom-call(bf16[256,8192]{1,0:T(8,128)(2,1)S(1)} %collective-permute-done.refs_0_.refs_1_, bf16[256,1024]{1,0:T(8,128)(2,1)S(1)} %collective-permute-done.1.refs_1_, ...), custom_call_target="tpu_custom_call" | custom-call | flops 7646444544 | tf_op jit(solution)/shard_map/project_other/pallas_call | solution.py:41
  19.8 2.6 %collective-permute-start.3 = (bf16[128,1024]{1,0:T(8,128)(2,1)S(1)}, bf16[128,1024]{1,0:T(8,128)(2,1)S(1)}, u32[]{:S(2)}, u32[]{:S(2)}) collective-permute-start(bf16[128,1024]{1,0:T(8,128)(2,1)S(1)} %get-tuple-element.65), channel_id=1, source_target_pairs={{0,2},{2,0},{4,6},{6,4},{8,10},{10,8},{12,14},{14,12},{1,3},{3,1},... | collective-permute-start | bytes 786440 | tf_op jit(solution)/shard_map/ppermute | solution.py:586
  22.4 6.9 %back_project.3 = (f32[512,1024]{1,0:T(8,128)S(1)}, f32[1,4096]{1,0:T(1,128)S(1)}, bf16[256,4096]{1,0:T(8,128)(2,1)S(1)}, bf16[1024,1024]{1,0:T(8,128)(2,1)S(1)}) custom-call(bf16[256,8192]{1,0:T(8,128)(2,1)S(1)} %get-tuple-element.53.refs_0_, bf16[256,8192]{1,0:T(8,128)(2,1)S(1)} %collective-permute-done.refs_0_.refs_1_, ...), custom_call_target="tpu_custom_call" | custom-call | flops 7646444544 | tf_op jit(solution)/shard_map/back_project/pallas_call | solution.py:41
  29.3 0.0 collective-permute-done.3.refs_1_
  29.4 0.1 pieces_of.2
  29.4 1.9 %collective-permute-start.4 = (bf16[32,1024]{1,0:T(8,128)(2,1)S(1)}, bf16[32,1024]{1,0:T(8,128)(2,1)S(1)}, u32[]{:S(2)}, u32[]{:S(2)}) collective-permute-start(bf16[32,1024]{1,0:T(8,128)(2,1)S(1)} %get-tuple-element.69), channel_id=1, source_target_pairs={{0,4},{2,6},{4,0},{6,2},{8,12},{10,14},{12,8},{14,10},{1,5},{3,7},... | collective-permute-start | bytes 196616 | tf_op jit(solution)/shard_map/ppermute | solution.py:586
  31.3 2.6 %collective-permute-start.5 = (bf16[32,1024]{1,0:T(8,128)(2,1)S(1)}, bf16[32,1024]{1,0:T(8,128)(2,1)S(1)}, u32[]{:S(2)}, u32[]{:S(2)}) collective-permute-start(bf16[32,1024]{1,0:T(8,128)(2,1)S(1)} %get-tuple-element.70), channel_id=1, source_target_pairs={{0,8},{2,10},{4,12},{6,14},{8,0},{10,2},{12,4},{14,6},{1,9},{3,11}... | collective-permute-start | bytes 196616 | tf_op jit(solution)/shard_map/ppermute | solution.py:586
  33.9 3.7 %back_project.4 = (f32[512,1024]{1,0:T(8,128)S(1)}, f32[1,2048]{1,0:T(1,128)S(1)}, bf16[1024,1024]{1,0:T(8,128)(2,1)S(1)}) custom-call(bf16[256,8192]{1,0:T(8,128)(2,1)S(1)} %get-tuple-element.53.refs_0_, bf16[256,8192]{1,0:T(8,128)(2,1)S(1)} %collective-permute-done.refs_0_.refs_1_, bf16[256,4096]{1,0:T(8,128)(2,1)S(1)} %get-tuple-element.61.refs_2_.refs_0_, ...), custom_call_target="tpu_custom_call" | custom-call | flops 3995722240 | tf_op jit(solution)/shard_map/back_project/pallas_call | solution.py:41
  37.6 1.7 %turn_hidden.2.refs_4_.refs_0_ = bf16[4096,512]{1,0:T(8,128)(2,1)S(1)} custom-call(bf16[256,8192]{1,0:T(8,128)(2,1)S(1)} %get-tuple-element.53.refs_0_, bf16[256,8192]{1,0:T(8,128)(2,1)S(1)} %collective-permute-done.refs_0_.refs_1_, bf16[256,4096]{1,0:T(8,128)(2,1)S(1)} %get-tuple-element.59.refs_2_.refs_0_, ...), custom_call_target="tpu_custom_call" | custom-call | flops 2070000000 | tf_op jit(solution)/shard_map/turn_hidden/pallas_call | solution.py:41
  39.3 0.7 collective-permute-done.6.refs_3_
  40.1 3.2 %collective-permute-start.9 = (bf16[32,1024]{1,0:T(8,128)(2,1)S(1)}, bf16[32,1024]{1,0:T(8,128)(2,1)S(1)}, u32[]{:S(2)}, u32[]{:S(2)}) collective-permute-start(bf16[32,1024]{1,0:T(8,128)(2,1)S(1)} %add_pieces.2.refs_7_.refs_0_), channel_id=1, source_target_pairs={{0,12},{2,14},{4,8},{6,10},{8,4},{10,6},{12,0},{14,2},{1,13},{3,15... | collective-permute-start | bytes 196616 | tf_op jit(solution)/shard_map/ppermute | solution.py:586
  43.3 1.3 %collective-permute-start.7 = (bf16[32,1024]{1,0:T(8,128)(2,1)S(1)}, bf16[32,1024]{1,0:T(8,128)(2,1)S(1)}, u32[]{:S(2)}, u32[]{:S(2)}) collective-permute-start(bf16[32,1024]{1,0:T(8,128)(2,1)S(1)} %add_pieces.2.refs_7_.refs_0_), channel_id=1, source_target_pairs={{0,4},{2,6},{4,0},{6,2},{8,12},{10,14},{12,8},{14,10},{1,5},{3,7},... | collective-permute-start | bytes 196616 | tf_op jit(solution)/shard_map/ppermute | solution.py:586
  44.6 3.8 %back_project.5 = (bf16[256,1024]{1,0:T(8,128)(2,1)S(1)}, f32[256,1024]{1,0:T(8,128)S(1)}, f32[1,2048]{1,0:T(1,128)S(1)}) custom-call(bf16[256,8192]{1,0:T(8,128)(2,1)S(1)} %get-tuple-element.53.refs_0_, bf16[256,8192]{1,0:T(8,128)(2,1)S(1)} %collective-permute-done.refs_0_.refs_1_, bf16[256,4096]{1,0:T(8,128)(2,1)S(1)} %get-tuple-element.61.refs_2_.refs_0_, ...), custom_call_target="tpu_custom_call" | custom-call | flops 3995722240 | tf_op jit(solution)/shard_map/back_project/pallas_call | solution.py:41
  48.3 1.6 %turn_hidden.3.refs_5_.refs_0_ = bf16[4096,512]{1,0:T(8,128)(2,1)S(1)} custom-call(bf16[256,8192]{1,0:T(8,128)(2,1)S(1)} %get-tuple-element.53.refs_0_, bf16[256,8192]{1,0:T(8,128)(2,1)S(1)} %collective-permute-done.refs_0_.refs_1_, bf16[256,4096]{1,0:T(8,128)(2,1)S(1)} %get-tuple-element.61.refs_2_.refs_0_, ...), custom_call_target="tpu_custom_call" | custom-call | flops 2070000000 | tf_op jit(solution)/shard_map/turn_hidden/pallas_call | solution.py:41
  50.0 1.6 %collective-permute-start.11 = (bf16[128,1024]{1,0:T(8,128)(2,1)S(1)}, bf16[128,1024]{1,0:T(8,128)(2,1)S(1)}, u32[]{:S(2)}, u32[]{:S(2)}) collective-permute-start(bf16[128,1024]{1,0:T(8,128)(2,1)S(1)} %get-tuple-element.74.refs_2_.refs_3_.refs_4_), channel_id=1, source_target_pairs={{0,2},{2,0},{4,6},{6,4},{8,10},{10,8},{12,14},{14,12},{1,3},{3,1},... | collective-permute-start | bytes 786440 | tf_op jit(solution)/shard_map/ppermute | solution.py:586
  51.5 0.5 collective-permute-start.13
  52.1 4.1 %turn_x.1.refs_1_.refs_5_.refs_2_.refs_11_.refs_7_ = bf16[8192,512]{1,0:T(8,128)(2,1)} custom-call(bf16[256,8192]{1,0:T(8,128)(2,1)S(1)} %get-tuple-element.53.refs_0_, bf16[256,8192]{1,0:T(8,128)(2,1)S(1)} %collective-permute-done.refs_0_.refs_1_, bf16[128,1024]{1,0:T(8,128)(2,1)S(1)} %get-tuple-element.74.refs_2_.refs_3_.refs_4_), custom_call_target="tpu_custom_call" | custom-call | flops 4140000000 | tf_op jit(solution)/shard_map/turn_x/pallas_call | solution.py:41
  56.2 0.3 collective-permute-done.11.refs_0_
  56.4 0.1 pair_halves.1
  56.5 1.6 %collective-permute-start.14 = (bf16[128,1024]{1,0:T(8,128)(2,1)S(1)}, bf16[128,1024]{1,0:T(8,128)(2,1)S(1)}, u32[]{:S(2)}, u32[]{:S(2)}) collective-permute-start(bf16[128,1024]{1,0:T(8,128)(2,1)S(1)} %get-tuple-element.77), channel_id=1, source_target_pairs={{0,2},{2,0},{4,6},{6,4},{8,10},{10,8},{12,14},{14,12},{1,3},{3,1},... | collective-permute-start | bytes 786440 | tf_op jit(solution)/shard_map/ppermute | solution.py:586
  58.1 6.2 %u_grad.2.refs_2_.refs_5_ = bf16[8192,1024]{1,0:T(8,128)(2,1)} custom-call(bf16[4096,512]{1,0:T(8,128)(2,1)S(1)} %turn_hidden.2.refs_4_.refs_0_, bf16[128,1024]{1,0:T(8,128)(2,1)S(1)} %collective-permute-done.10.refs_1_.refs_2_, bf16[128,1024]{1,0:T(8,128)(2,1)S(1)} %collective-permute-done.12.refs_2_.refs_3_, ...), custom_call_target="tpu_custom_call" | custom-call | flops 7646444544 | tf_op jit(solution)/shard_map/u_grad/pallas_call | solution.py:41
  64.3 1.1 collective-permute-done.14.refs_1_
  65.3 0.1 pieces_of.3
  65.4 1.2 collective-permute-start.15
  66.6 2.6 %collective-permute-start.16 = (bf16[32,1024]{1,0:T(8,128)(2,1)S(1)}, bf16[32,1024]{1,0:T(8,128)(2,1)S(1)}, u32[]{:S(2)}, u32[]{:S(2)}) collective-permute-start(bf16[32,1024]{1,0:T(8,128)(2,1)S(1)} %get-tuple-element.81), channel_id=1, source_target_pairs={{0,8},{2,10},{4,12},{6,14},{8,0},{10,2},{12,4},{14,6},{1,9},{3,11}... | collective-permute-start | bytes 196616 | tf_op jit(solution)/shard_map/ppermute | solution.py:586
  69.3 0.6 collective-permute-start.17
  69.8 6.2 %u_grad.3 = (bf16[8192,1024]{1,0:T(8,128)(2,1)}, bf16[1024,1024]{1,0:T(8,128)(2,1)S(1)}) custom-call(bf16[4096,512]{1,0:T(8,128)(2,1)S(1)} %turn_hidden.3.refs_5_.refs_0_, bf16[128,1024]{1,0:T(8,128)(2,1)S(1)} %collective-permute-done.10.refs_1_.refs_2_, ...), custom_call_target="tpu_custom_call", output_to_operand_aliasing={{0}: (5, {})} | custom-call | flops 7646444544 | tf_op jit(solution)/shard_map/u_grad/pallas_call | solution.py:41
  76.1 3.3 %collective-permute-start.20 = (bf16[32,1024]{1,0:T(8,128)(2,1)S(1)}, bf16[32,1024]{1,0:T(8,128)(2,1)S(1)}, u32[]{:S(2)}, u32[]{:S(2)}) collective-permute-start(bf16[32,1024]{1,0:T(8,128)(2,1)S(1)} %add_pieces.3.refs_7_.refs_0_), channel_id=1, source_target_pairs={{0,12},{2,14},{4,8},{6,10},{8,4},{10,6},{12,0},{14,2},{1,13},{3,15... | collective-permute-start | bytes 196616 | tf_op jit(solution)/shard_map/ppermute | solution.py:586
  79.4 1.1 collective-permute-start.18
  80.5 6.4 %expand.2 = (f32[512,4096]{1,0:T(8,128)S(1)}, bf16[1024,1024]{1,0:T(8,128)(2,1)S(1)}) custom-call(bf16[8192,1024]{1,0:T(8,128)(2,1)} %refs_0_.9, bf16[1024,1024]{1,0:T(8,128)(2,1)S(1)} %get-tuple-element.79.refs_1_, bf16[128,1024]{1,0:T(8,128)(2,1)S(1)} %collective-permute-done.10.refs_1_.refs_2_, ...), custom_call_target="tpu_custom_call" | custom-call | flops 7646444544 | tf_op jit(solution)/shard_map/expand/pallas_call | solution.py:41
  87.0 1.5 %collective-permute-start.22 = (bf16[128,1024]{1,0:T(8,128)(2,1)S(1)}, bf16[128,1024]{1,0:T(8,128)(2,1)S(1)}, u32[]{:S(2)}, u32[]{:S(2)}) collective-permute-start(bf16[128,1024]{1,0:T(8,128)(2,1)S(1)} %join_pieces.3.refs_7_.refs_8_.refs_3_), channel_id=1, source_target_pairs={{0,2},{2,0},{4,6},{6,4},{8,10},{10,8},{12,14},{14,12},{1,3},{3,1},... | collective-permute-start | bytes 786440 | tf_op jit(solution)/shard_map/ppermute | solution.py:586
  88.6 6.6 %expand.3 = (f32[512,4096]{1,0:T(8,128)S(1)}, bf16[1024,1024]{1,0:T(8,128)(2,1)S(1)}) custom-call(bf16[8192,1024]{1,0:T(8,128)(2,1)} %refs_0_.9, bf16[1024,1024]{1,0:T(8,128)(2,1)S(1)} %get-tuple-element.84.refs_1_, bf16[128,1024]{1,0:T(8,128)(2,1)S(1)} %collective-permute-done.10.refs_1_.refs_2_, ...), custom_call_target="tpu_custom_call" | custom-call | flops 7646444544 | tf_op jit(solution)/shard_map/expand/pallas_call | solution.py:41
  95.2 0.6 collective-permute-start.23
  95.8 0.2 copy-done
  96.0 0.6 pad_maximum_fusion.refs_12_
  96.6 0.3 collective-permute-done.23.refs_7_.refs_2_
  96.9 6.8 %input_grad.2 = (bf16[256,16384]{1,0:T(8,128)(2,1)}, bf16[256,4096]{1,0:T(8,128)(2,1)S(1)}, bf16[1024,1024]{1,0:T(8,128)(2,1)S(1)}) custom-call(bf16[256,4096]{1,0:T(8,128)(2,1)S(1)} %get-tuple-element.59.refs_2_.refs_0_, bf16[256,8192]{1,0:T(8,128)(2,1)S(1)} %collective-permute-done.2.refs_3_.refs_1_, f32[512,4096]{1,0:T(8,128)S(1)} %get-tuple-element.85.refs_4_.refs_2_, ...), custom_call_target="tpu_custom_call" | custom-call | flops 7646444544 | tf_op jit(solution)/shard_map/input_grad/pallas_call | solution.py:41
  103.7 0.4 collective-permute-start.24
  104.2 7.4 %input_grad.3 = (bf16[256,16384]{1,0:T(8,128)(2,1)}, bf16[256,4096]{1,0:T(8,128)(2,1)S(1)}, bf16[4096,512]{1,0:T(8,128)(2,1)S(1)}) custom-call(bf16[256,4096]{1,0:T(8,128)(2,1)S(1)} %get-tuple-element.61.refs_2_.refs_0_, bf16[256,8192]{1,0:T(8,128)(2,1)S(1)} %collective-permute-done.2.refs_3_.refs_1_, ...), custom_call_target="tpu_custom_call", output_to_operand_aliasing={{0}: (10, {})} | custom-call | flops 7646444544 | tf_op jit(solution)/shard_map/input_grad/pallas_call | solution.py:41
  111.5 0.2 collective-permute-start.25
  111.8 6.2 %v_grad.2 = (bf16[8192,1024]{1,0:T(8,128)(2,1)}, bf16[256,16384]{1,0:T(8,128)(2,1)}, bf16[4096,512]{1,0:T(8,128)(2,1)S(1)}) custom-call(bf16[4096,512]{1,0:T(8,128)(2,1)S(1)} %get-tuple-element.93.refs_0_, bf16[128,1024]{1,0:T(8,128)(2,1)S(1)} %collective-permute-done.21.refs_6_.refs_1_, ...), custom_call_target="tpu_custom_call", output_to_operand_aliasing={{1}: (6, {})} | custom-call | flops 345000000 | tf_op jit(solution)/shard_map/v_grad/pallas_call | solution.py:41
  117.9 6.2 %v_grad.3 = (bf16[8192,1024]{1,0:T(8,128)(2,1)}, bf16[256,16384]{1,0:T(8,128)(2,1)}) custom-call(bf16[4096,512]{1,0:T(8,128)(2,1)S(1)} %get-tuple-element.96.refs_0_, bf16[128,1024]{1,0:T(8,128)(2,1)S(1)} %collective-permute-done.21.refs_6_.refs_1_, ...), custom_call_target="tpu_custom_call", output_to_operand_aliasing={{0}: (5, {}), {1}: (7, {})} | custom-call | flops 7646444544 | tf_op jit(solution)/shard_map/v_grad/pallas_call | solution.py:41
  (36 shorter events, 0.3 us)
Async XLA Ops:
  2.9 11.4 %collective-permute-start = (bf16[256,8192]{1,0:T(8,128)(2,1)S(1)}, bf16[256,8192]{1,0:T(8,128)(2,1)S(1)}, u32[]{:S(2)}, u32[]{:S(2)}) collective-permute-start(bf16[256,8192]{1,0:T(8,128)(2,1)S(1)} %cut_half.2.refs_2_), channel_id=1, source_target_pairs={{0,1},{1,0},{2,3},{3,2},{4,5},{5,4},{6,7},{7,6},{8,9},{9,8},{10,11... | collective-permute-start | bytes 12582920 | tf_op jit(solution)/shard_map/ppermute | solution.py:583
  11.4 2.3 %collective-permute-start.1 = (bf16[256,1024]{1,0:T(8,128)(2,1)S(1)}, bf16[256,1024]{1,0:T(8,128)(2,1)S(1)}, u32[]{:S(2)}, u32[]{:S(2)}) collective-permute-start(bf16[256,1024]{1,0:T(8,128)(2,1)S(1)} %get-tuple-element.54.refs_1_), channel_id=1, source_target_pairs={{0,1},{1,0},{2,3},{3,2},{4,5},{5,4},{6,7},{7,6},{8,9},{9,8},{10,11... | collective-permute-start | bytes 1572872 | tf_op jit(solution)/shard_map/ppermute | solution.py:583
  13.7 8.7 %collective-permute-start.2 = (bf16[256,8192]{1,0:T(8,128)(2,1)S(1)}, bf16[256,8192]{1,0:T(8,128)(2,1)S(1)}, u32[]{:S(2)}, u32[]{:S(2)}) collective-permute-start(bf16[256,8192]{1,0:T(8,128)(2,1)S(1)} %hold.3), channel_id=1, source_target_pairs={{0,1},{1,0},{2,3},{3,2},{4,5},{5,4},{6,7},{7,6},{8,9},{9,8},{10,11... | collective-permute-start | bytes 12582920 | tf_op jit(solution)/shard_map/ppermute | solution.py:583
  19.8 9.5 %collective-permute-start.3 = (bf16[128,1024]{1,0:T(8,128)(2,1)S(1)}, bf16[128,1024]{1,0:T(8,128)(2,1)S(1)}, u32[]{:S(2)}, u32[]{:S(2)}) collective-permute-start(bf16[128,1024]{1,0:T(8,128)(2,1)S(1)} %get-tuple-element.65), channel_id=1, source_target_pairs={{0,2},{2,0},{4,6},{6,4},{8,10},{10,8},{12,14},{14,12},{1,3},{3,1},... | collective-permute-start | bytes 786440 | tf_op jit(solution)/shard_map/ppermute | solution.py:586
  29.4 9.9 %collective-permute-start.4 = (bf16[32,1024]{1,0:T(8,128)(2,1)S(1)}, bf16[32,1024]{1,0:T(8,128)(2,1)S(1)}, u32[]{:S(2)}, u32[]{:S(2)}) collective-permute-start(bf16[32,1024]{1,0:T(8,128)(2,1)S(1)} %get-tuple-element.69), channel_id=1, source_target_pairs={{0,4},{2,6},{4,0},{6,2},{8,12},{10,14},{12,8},{14,10},{1,5},{3,7},... | collective-permute-start | bytes 196616 | tf_op jit(solution)/shard_map/ppermute | solution.py:586
  31.3 8.0 %collective-permute-start.5 = (bf16[32,1024]{1,0:T(8,128)(2,1)S(1)}, bf16[32,1024]{1,0:T(8,128)(2,1)S(1)}, u32[]{:S(2)}, u32[]{:S(2)}) collective-permute-start(bf16[32,1024]{1,0:T(8,128)(2,1)S(1)} %get-tuple-element.70), channel_id=1, source_target_pairs={{0,8},{2,10},{4,12},{6,14},{8,0},{10,2},{12,4},{14,6},{1,9},{3,11}... | collective-permute-start | bytes 196616 | tf_op jit(solution)/shard_map/ppermute | solution.py:586
  33.9 6.2 %collective-permute-start.6 = (bf16[32,1024]{1,0:T(8,128)(2,1)S(1)}, bf16[32,1024]{1,0:T(8,128)(2,1)S(1)}, u32[]{:S(2)}, u32[]{:S(2)}) collective-permute-start(bf16[32,1024]{1,0:T(8,128)(2,1)S(1)} %get-tuple-element.71), channel_id=1, source_target_pairs={{0,12},{2,14},{4,8},{6,10},{8,4},{10,6},{12,0},{14,2},{1,13},{3,15... | collective-permute-start | bytes 196616 | tf_op jit(solution)/shard_map/ppermute | solution.py:586
  40.1 9.8 %collective-permute-start.9 = (bf16[32,1024]{1,0:T(8,128)(2,1)S(1)}, bf16[32,1024]{1,0:T(8,128)(2,1)S(1)}, u32[]{:S(2)}, u32[]{:S(2)}) collective-permute-start(bf16[32,1024]{1,0:T(8,128)(2,1)S(1)} %add_pieces.2.refs_7_.refs_0_), channel_id=1, source_target_pairs={{0,12},{2,14},{4,8},{6,10},{8,4},{10,6},{12,0},{14,2},{1,13},{3,15... | collective-permute-start | bytes 196616 | tf_op jit(solution)/shard_map/ppermute | solution.py:586
  43.3 6.6 %collective-permute-start.8 = (bf16[32,1024]{1,0:T(8,128)(2,1)S(1)}, bf16[32,1024]{1,0:T(8,128)(2,1)S(1)}, u32[]{:S(2)}, u32[]{:S(2)}) collective-permute-start(bf16[32,1024]{1,0:T(8,128)(2,1)S(1)} %add_pieces.2.refs_7_.refs_0_), channel_id=1, source_target_pairs={{0,8},{2,10},{4,12},{6,14},{8,0},{10,2},{12,4},{14,6},{1,9},{3,11}... | collective-permute-start | bytes 196616 | tf_op jit(solution)/shard_map/ppermute | solution.py:586
  43.3 6.6 %collective-permute-start.7 = (bf16[32,1024]{1,0:T(8,128)(2,1)S(1)}, bf16[32,1024]{1,0:T(8,128)(2,1)S(1)}, u32[]{:S(2)}, u32[]{:S(2)}) collective-permute-start(bf16[32,1024]{1,0:T(8,128)(2,1)S(1)} %add_pieces.2.refs_7_.refs_0_), channel_id=1, source_target_pairs={{0,4},{2,6},{4,0},{6,2},{8,12},{10,14},{12,8},{14,10},{1,5},{3,7},... | collective-permute-start | bytes 196616 | tf_op jit(solution)/shard_map/ppermute | solution.py:586
  50.0 6.4 %collective-permute-start.11 = (bf16[128,1024]{1,0:T(8,128)(2,1)S(1)}, bf16[128,1024]{1,0:T(8,128)(2,1)S(1)}, u32[]{:S(2)}, u32[]{:S(2)}) collective-permute-start(bf16[128,1024]{1,0:T(8,128)(2,1)S(1)} %get-tuple-element.74.refs_2_.refs_3_.refs_4_), channel_id=1, source_target_pairs={{0,2},{2,0},{4,6},{6,4},{8,10},{10,8},{12,14},{14,12},{1,3},{3,1},... | collective-permute-start | bytes 786440 | tf_op jit(solution)/shard_map/ppermute | solution.py:586
  51.5 6.6 %collective-permute-start.10 = (bf16[128,1024]{1,0:T(8,128)(2,1)S(1)}, bf16[128,1024]{1,0:T(8,128)(2,1)S(1)}, u32[]{:S(2)}, u32[]{:S(2)}) collective-permute-start(bf16[128,1024]{1,0:T(8,128)(2,1)S(1)} %get-tuple-element.74.refs_2_.refs_3_.refs_4_), channel_id=1, source_target_pairs={{0,1},{1,0},{2,3},{3,2},{4,5},{5,4},{6,7},{7,6},{8,9},{9,8},{10,11... | collective-permute-start | bytes 786440 | tf_op jit(solution)/shard_map/ppermute | solution.py:583
  51.5 4.9 %collective-permute-start.13 = (bf16[256,1024]{1,0:T(8,128)(2,1)S(1)}, bf16[256,1024]{1,0:T(8,128)(2,1)S(1)}, u32[]{:S(2)}, u32[]{:S(2)}) collective-permute-start(bf16[256,1024]{1,0:T(8,128)(2,1)S(1)} %get-tuple-element.75), channel_id=1, source_target_pairs={{0,1},{1,0},{2,3},{3,2},{4,5},{5,4},{6,7},{7,6},{8,9},{9,8},{10,11... | collective-permute-start | bytes 1572872 | tf_op jit(solution)/shard_map/ppermute | solution.py:583
  56.4 1.7 %collective-permute-start.12 = (bf16[128,1024]{1,0:T(8,128)(2,1)S(1)}, bf16[128,1024]{1,0:T(8,128)(2,1)S(1)}, u32[]{:S(2)}, u32[]{:S(2)}) collective-permute-start(bf16[128,1024]{1,0:T(8,128)(2,1)S(1)} %hold.4.refs_4_.refs_5_), channel_id=1, source_target_pairs={{0,1},{1,0},{2,3},{3,2},{4,5},{5,4},{6,7},{7,6},{8,9},{9,8},{10,11... | collective-permute-start | bytes 786440 | tf_op jit(solution)/shard_map/ppermute | solution.py:583
  56.5 8.8 %collective-permute-start.14 = (bf16[128,1024]{1,0:T(8,128)(2,1)S(1)}, bf16[128,1024]{1,0:T(8,128)(2,1)S(1)}, u32[]{:S(2)}, u32[]{:S(2)}) collective-permute-start(bf16[128,1024]{1,0:T(8,128)(2,1)S(1)} %get-tuple-element.77), channel_id=1, source_target_pairs={{0,2},{2,0},{4,6},{6,4},{8,10},{10,8},{12,14},{14,12},{1,3},{3,1},... | collective-permute-start | bytes 786440 | tf_op jit(solution)/shard_map/ppermute | solution.py:586
  65.4 10.6 %collective-permute-start.15 = (bf16[32,1024]{1,0:T(8,128)(2,1)S(1)}, bf16[32,1024]{1,0:T(8,128)(2,1)S(1)}, u32[]{:S(2)}, u32[]{:S(2)}) collective-permute-start(bf16[32,1024]{1,0:T(8,128)(2,1)S(1)} %get-tuple-element.80), channel_id=1, source_target_pairs={{0,4},{2,6},{4,0},{6,2},{8,12},{10,14},{12,8},{14,10},{1,5},{3,7},... | collective-permute-start | bytes 196616 | tf_op jit(solution)/shard_map/ppermute | solution.py:586
  66.6 9.4 %collective-permute-start.16 = (bf16[32,1024]{1,0:T(8,128)(2,1)S(1)}, bf16[32,1024]{1,0:T(8,128)(2,1)S(1)}, u32[]{:S(2)}, u32[]{:S(2)}) collective-permute-start(bf16[32,1024]{1,0:T(8,128)(2,1)S(1)} %get-tuple-element.81), channel_id=1, source_target_pairs={{0,8},{2,10},{4,12},{6,14},{8,0},{10,2},{12,4},{14,6},{1,9},{3,11}... | collective-permute-start | bytes 196616 | tf_op jit(solution)/shard_map/ppermute | solution.py:586
  69.3 6.8 %collective-permute-start.17 = (bf16[32,1024]{1,0:T(8,128)(2,1)S(1)}, bf16[32,1024]{1,0:T(8,128)(2,1)S(1)}, u32[]{:S(2)}, u32[]{:S(2)}) collective-permute-start(bf16[32,1024]{1,0:T(8,128)(2,1)S(1)} %get-tuple-element.82), channel_id=1, source_target_pairs={{0,12},{2,14},{4,8},{6,10},{8,4},{10,6},{12,0},{14,2},{1,13},{3,15... | collective-permute-start | bytes 196616 | tf_op jit(solution)/shard_map/ppermute | solution.py:586
  76.1 10.9 %collective-permute-start.20 = (bf16[32,1024]{1,0:T(8,128)(2,1)S(1)}, bf16[32,1024]{1,0:T(8,128)(2,1)S(1)}, u32[]{:S(2)}, u32[]{:S(2)}) collective-permute-start(bf16[32,1024]{1,0:T(8,128)(2,1)S(1)} %add_pieces.3.refs_7_.refs_0_), channel_id=1, source_target_pairs={{0,12},{2,14},{4,8},{6,10},{8,4},{10,6},{12,0},{14,2},{1,13},{3,15... | collective-permute-start | bytes 196616 | tf_op jit(solution)/shard_map/ppermute | solution.py:586
  79.4 7.6 %collective-permute-start.19 = (bf16[32,1024]{1,0:T(8,128)(2,1)S(1)}, bf16[32,1024]{1,0:T(8,128)(2,1)S(1)}, u32[]{:S(2)}, u32[]{:S(2)}) collective-permute-start(bf16[32,1024]{1,0:T(8,128)(2,1)S(1)} %add_pieces.3.refs_7_.refs_0_), channel_id=1, source_target_pairs={{0,8},{2,10},{4,12},{6,14},{8,0},{10,2},{12,4},{14,6},{1,9},{3,11}... | collective-permute-start | bytes 196616 | tf_op jit(solution)/shard_map/ppermute | solution.py:586
  79.4 7.6 %collective-permute-start.18 = (bf16[32,1024]{1,0:T(8,128)(2,1)S(1)}, bf16[32,1024]{1,0:T(8,128)(2,1)S(1)}, u32[]{:S(2)}, u32[]{:S(2)}) collective-permute-start(bf16[32,1024]{1,0:T(8,128)(2,1)S(1)} %add_pieces.3.refs_7_.refs_0_), channel_id=1, source_target_pairs={{0,4},{2,6},{4,0},{6,2},{8,12},{10,14},{12,8},{14,10},{1,5},{3,7},... | collective-permute-start | bytes 196616 | tf_op jit(solution)/shard_map/ppermute | solution.py:586
  87.0 8.1 %collective-permute-start.22 = (bf16[128,1024]{1,0:T(8,128)(2,1)S(1)}, bf16[128,1024]{1,0:T(8,128)(2,1)S(1)}, u32[]{:S(2)}, u32[]{:S(2)}) collective-permute-start(bf16[128,1024]{1,0:T(8,128)(2,1)S(1)} %join_pieces.3.refs_7_.refs_8_.refs_3_), channel_id=1, source_target_pairs={{0,2},{2,0},{4,6},{6,4},{8,10},{10,8},{12,14},{14,12},{1,3},{3,1},... | collective-permute-start | bytes 786440 | tf_op jit(solution)/shard_map/ppermute | solution.py:586
  88.6 8.0 %collective-permute-start.21 = (bf16[128,1024]{1,0:T(8,128)(2,1)S(1)}, bf16[128,1024]{1,0:T(8,128)(2,1)S(1)}, u32[]{:S(2)}, u32[]{:S(2)}) collective-permute-start(bf16[128,1024]{1,0:T(8,128)(2,1)S(1)} %join_pieces.3.refs_7_.refs_8_.refs_3_), channel_id=1, source_target_pairs={{0,1},{1,0},{2,3},{3,2},{4,5},{5,4},{6,7},{7,6},{8,9},{9,8},{10,11... | collective-permute-start | bytes 786440 | tf_op jit(solution)/shard_map/ppermute | solution.py:583
  95.2 0.8 copy-start
  95.2 1.7 %collective-permute-start.23 = (bf16[128,1024]{1,0:T(8,128)(2,1)S(1)}, bf16[128,1024]{1,0:T(8,128)(2,1)S(1)}, u32[]{:S(2)}, u32[]{:S(2)}) collective-permute-start(bf16[128,1024]{1,0:T(8,128)(2,1)S(1)} %hold.5.refs_9_.refs_4_), channel_id=1, source_target_pairs={{0,1},{1,0},{2,3},{3,2},{4,5},{5,4},{6,7},{7,6},{8,9},{9,8},{10,11... | collective-permute-start | bytes 786440 | tf_op jit(solution)/shard_map/ppermute | solution.py:583
  103.7 8.0 %collective-permute-start.24 = (bf16[256,4096]{1,0:T(8,128)(2,1)S(1)}, bf16[256,4096]{1,0:T(8,128)(2,1)S(1)}, u32[]{:S(2)}, u32[]{:S(2)}) collective-permute-start(bf16[256,4096]{1,0:T(8,128)(2,1)S(1)} %get-tuple-element.94), channel_id=1, source_target_pairs={{0,1},{1,0},{2,3},{3,2},{4,5},{5,4},{6,7},{7,6},{8,9},{9,8},{10,11... | collective-permute-start | bytes 6291464 | tf_op jit(solution)/shard_map/ppermute | solution.py:583
  111.5 6.4 %collective-permute-start.25 = (bf16[256,4096]{1,0:T(8,128)(2,1)S(1)}, bf16[256,4096]{1,0:T(8,128)(2,1)S(1)}, u32[]{:S(2)}, u32[]{:S(2)}) collective-permute-start(bf16[256,4096]{1,0:T(8,128)(2,1)S(1)} %get-tuple-element.98), channel_id=1, source_target_pairs={{0,1},{1,0},{2,3},{3,2},{4,5},{5,4},{6,7},{7,6},{8,9},{9,8},{10,11... | collective-permute-start | bytes 6291464 | tf_op jit(solution)/shard_map/ppermute | solution.py:583

commit v5 on v4

--- a/solution.py
+++ b/solution.py
@@ -139,11 +139,11 @@
     each = outs[0].shape[0]
     bit = at_ref[1] & 1
     for i, o_ref in ((bit, outs[0]), (1 - bit, outs[1])):
-        o_ref[...] = total(at_block(i, each)).astype(BF)
+        o_ref[...] = total(at_block(i, each)).astype(o_ref.dtype)
 
 
 def halves_of(rows, rank, direct):
-    return [((rows // 2, rank), BF, "v")] * 2 if direct else [((rows, rank), F32, "v")]
+    return [((rows // 2, rank), F32, "v"), ((rows // 2, rank), BF, "v")] if direct else [((rows, rank), F32, "v")]
 
 
 def project_other(x_o, vs, theirs, c, u, direct):
@@ -541,9 +541,9 @@
     def body(at_ref, a_ref, b_ref, *outs):
         for d in range(m):
             here = at_block((at_ref[1] >> 1) ^ d, each)
-            outs[d][...] = plus(a_ref[here, :], b_ref[here, :]).astype(BF)
-
-    return call(body, "pieces_of", [(a, "v"), (b, "v")], [((each, rank), BF, "v")] * m, after=after, carry=carry)
+            outs[d][...] = plus(a_ref[here, :], b_ref[here, :]).astype(outs[d].dtype)
+
+    return call(body, "pieces_of", [(a, "v"), (b, "v")], [((each, rank), F32 if d == 0 else BF, "v") for d in range(m)], after=after, carry=carry)
 
 
 def add_pieces(parts, after=(), carry=()):

time: 125 us -> 125 us (level)
  no operation moved by 1% of the time
where the time goes in v5:
time: 125 us
  Pallas kernels  92.3 us (74%)
  starting transfers between devices  27.6 us (22%)
  waiting for transfers between devices  2.64 us (2%)
    pallas_call x28, Pallas kernels, call(): pl.pallas_call(whole if n_ahead else lambda *refs: body(Place(), *refs[:n...  92.3 us
    ppermute x16, starting transfers between devices, to(): return lax.ppermute(a, 'col', [(i, i ^ d) for i in range(n)])  24.7 us
    ppermute x10, starting transfers between devices, trade(): return lax.ppermute(a, 'batch', swap)  2.89 us
  transfers between devices with their start and end apart: 26, of which 4 were waited for; matrix products, arithmetic and copies ran while one was open for 1% of the time, Pallas kernels for 62%

profile of v5, /device:TPU:0, one launch (start us, length us, event | category | flops | bytes accessed | tf_op | source)
XLA Modules:
  0.0 124.6 jit_solution(11918692161435218535)
XLA Ops:
  0.6 2.2 %cut_half.2.refs_2_ = bf16[256,8192]{1,0:T(8,128)(2,1)S(1)} custom-call(bf16[256,16384]{1,0:T(8,128)(2,1)} %refs_0_.6), custom_call_target="tpu_custom_call" | custom-call | flops 2529999872 | tf_op jit(solution)/shard_map/cut_half/pallas_call | solution.py:41
  2.9 0.5 collective-permute-start
  3.4 8.0 %project_own.1 = (bf16[256,1024]{1,0:T(8,128)(2,1)S(1)}, bf16[256,8192]{1,0:T(8,128)(2,1)S(1)}, bf16[2048,1024]{1,0:T(8,128)(2,1)S(1)}, bf16[2048,1024]{1,0:T(8,...) custom-call(bf16[256,16384]{1,0:T(8,128)(2,1)} %refs_0_.6, bf16[8192,1024]{1,0:T(8,128)(2,1)} %refs_3_.3, ...), custom_call_target="tpu_custom_call" | custom-call | flops 7646444544 | tf_op jit(solution)/shard_map/project_own/pallas_call | solution.py:41
  11.4 0.1 collective-permute-start.1
  11.5 2.2 %cut_half.3.refs_0_ = bf16[256,8192]{1,0:T(8,128)(2,1)S(1)} custom-call(bf16[256,16384]{1,0:T(8,128)(2,1)} %refs_6_.4, bf16[256,1024]{1,0:T(8,128)(2,1)S(1)} %get-tuple-element.54.refs_1_), custom_call_target="tpu_custom_call" | custom-call | flops 2529999872 | tf_op jit(solution)/shard_map/cut_half/pallas_call | solution.py:41
  13.7 0.5 collective-permute-start.2
  14.2 6.0 %project_other.1 = (f32[128,1024]{1,0:T(8,128)S(1)}, bf16[128,1024]{1,0:T(8,128)(2,1)S(1)}, bf16[256,4096]{1,0:T(8,128)(2,1)S(1)}, bf16[1024,1024]{1,0:T(8,128)(2,1)S(1)}) custom-call(bf16[256,8192]{1,0:T(8,128)(2,1)S(1)} %collective-permute-done.refs_0_.refs_1_, bf16[256,1024]{1,0:T(8,128)(2,1)S(1)} %collective-permute-done.1.refs_1_, ...), custom_call_target="tpu_custom_call" | custom-call | flops 7646444544 | tf_op jit(solution)/shard_map/project_other/pallas_call | solution.py:41
  20.3 2.6 %collective-permute-start.3 = (bf16[128,1024]{1,0:T(8,128)(2,1)S(1)}, bf16[128,1024]{1,0:T(8,128)(2,1)S(1)}, u32[]{:S(2)}, u32[]{:S(2)}) collective-permute-start(bf16[128,1024]{1,0:T(8,128)(2,1)S(1)} %get-tuple-element.65), channel_id=1, source_target_pairs={{0,2},{2,0},{4,6},{6,4},{8,10},{10,8},{12,14},{14,12},{1,3},{3,1},... | collective-permute-start | bytes 786440 | tf_op jit(solution)/shard_map/ppermute | solution.py:586
  22.9 6.9 %back_project.3 = (f32[512,1024]{1,0:T(8,128)S(1)}, f32[1,4096]{1,0:T(1,128)S(1)}, bf16[256,4096]{1,0:T(8,128)(2,1)S(1)}, bf16[1024,1024]{1,0:T(8,128)(2,1)S(1)}) custom-call(bf16[256,8192]{1,0:T(8,128)(2,1)S(1)} %get-tuple-element.53.refs_0_, bf16[256,8192]{1,0:T(8,128)(2,1)S(1)} %collective-permute-done.refs_0_.refs_1_, ...), custom_call_target="tpu_custom_call" | custom-call | flops 7646444544 | tf_op jit(solution)/shard_map/back_project/pallas_call | solution.py:41
  29.8 0.0 collective-permute-done.3.refs_1_
  29.8 0.1 pieces_of.2
  29.9 1.9 %collective-permute-start.4 = (bf16[32,1024]{1,0:T(8,128)(2,1)S(1)}, bf16[32,1024]{1,0:T(8,128)(2,1)S(1)}, u32[]{:S(2)}, u32[]{:S(2)}) collective-permute-start(bf16[32,1024]{1,0:T(8,128)(2,1)S(1)} %get-tuple-element.69), channel_id=1, source_target_pairs={{0,4},{2,6},{4,0},{6,2},{8,12},{10,14},{12,8},{14,10},{1,5},{3,7},... | collective-permute-start | bytes 196616 | tf_op jit(solution)/shard_map/ppermute | solution.py:586
  31.8 2.6 %collective-permute-start.5 = (bf16[32,1024]{1,0:T(8,128)(2,1)S(1)}, bf16[32,1024]{1,0:T(8,128)(2,1)S(1)}, u32[]{:S(2)}, u32[]{:S(2)}) collective-permute-start(bf16[32,1024]{1,0:T(8,128)(2,1)S(1)} %get-tuple-element.70), channel_id=1, source_target_pairs={{0,8},{2,10},{4,12},{6,14},{8,0},{10,2},{12,4},{14,6},{1,9},{3,11}... | collective-permute-start | bytes 196616 | tf_op jit(solution)/shard_map/ppermute | solution.py:586
  34.4 3.7 %back_project.4 = (f32[512,1024]{1,0:T(8,128)S(1)}, f32[1,2048]{1,0:T(1,128)S(1)}, bf16[1024,1024]{1,0:T(8,128)(2,1)S(1)}) custom-call(bf16[256,8192]{1,0:T(8,128)(2,1)S(1)} %get-tuple-element.53.refs_0_, bf16[256,8192]{1,0:T(8,128)(2,1)S(1)} %collective-permute-done.refs_0_.refs_1_, bf16[256,4096]{1,0:T(8,128)(2,1)S(1)} %get-tuple-element.61.refs_2_.refs_0_, ...), custom_call_target="tpu_custom_call" | custom-call | flops 3995722240 | tf_op jit(solution)/shard_map/back_project/pallas_call | solution.py:41
  38.0 1.7 %turn_hidden.2.refs_4_.refs_0_ = bf16[4096,512]{1,0:T(8,128)(2,1)S(1)} custom-call(bf16[256,8192]{1,0:T(8,128)(2,1)S(1)} %get-tuple-element.53.refs_0_, bf16[256,8192]{1,0:T(8,128)(2,1)S(1)} %collective-permute-done.refs_0_.refs_1_, bf16[256,4096]{1,0:T(8,128)(2,1)S(1)} %get-tuple-element.59.refs_2_.refs_0_, ...), custom_call_target="tpu_custom_call" | custom-call | flops 2070000000 | tf_op jit(solution)/shard_map/turn_hidden/pallas_call | solution.py:41
  39.8 0.7 collective-permute-done.6.refs_3_
  40.6 3.2 %collective-permute-start.9 = (bf16[32,1024]{1,0:T(8,128)(2,1)S(1)}, bf16[32,1024]{1,0:T(8,128)(2,1)S(1)}, u32[]{:S(2)}, u32[]{:S(2)}) collective-permute-start(bf16[32,1024]{1,0:T(8,128)(2,1)S(1)} %add_pieces.2.refs_7_.refs_0_), channel_id=1, source_target_pairs={{0,12},{2,14},{4,8},{6,10},{8,4},{10,6},{12,0},{14,2},{1,13},{3,15... | collective-permute-start | bytes 196616 | tf_op jit(solution)/shard_map/ppermute | solution.py:586
  43.7 1.3 %collective-permute-start.7 = (bf16[32,1024]{1,0:T(8,128)(2,1)S(1)}, bf16[32,1024]{1,0:T(8,128)(2,1)S(1)}, u32[]{:S(2)}, u32[]{:S(2)}) collective-permute-start(bf16[32,1024]{1,0:T(8,128)(2,1)S(1)} %add_pieces.2.refs_7_.refs_0_), channel_id=1, source_target_pairs={{0,4},{2,6},{4,0},{6,2},{8,12},{10,14},{12,8},{14,10},{1,5},{3,7},... | collective-permute-start | bytes 196616 | tf_op jit(solution)/shard_map/ppermute | solution.py:586
  45.0 3.8 %back_project.5 = (bf16[256,1024]{1,0:T(8,128)(2,1)S(1)}, f32[256,1024]{1,0:T(8,128)S(1)}, f32[1,2048]{1,0:T(1,128)S(1)}) custom-call(bf16[256,8192]{1,0:T(8,128)(2,1)S(1)} %get-tuple-element.53.refs_0_, bf16[256,8192]{1,0:T(8,128)(2,1)S(1)} %collective-permute-done.refs_0_.refs_1_, bf16[256,4096]{1,0:T(8,128)(2,1)S(1)} %get-tuple-element.61.refs_2_.refs_0_, ...), custom_call_target="tpu_custom_call" | custom-call | flops 3995722240 | tf_op jit(solution)/shard_map/back_project/pallas_call | solution.py:41
  48.8 1.6 %turn_hidden.3.refs_5_.refs_0_ = bf16[4096,512]{1,0:T(8,128)(2,1)S(1)} custom-call(bf16[256,8192]{1,0:T(8,128)(2,1)S(1)} %get-tuple-element.53.refs_0_, bf16[256,8192]{1,0:T(8,128)(2,1)S(1)} %collective-permute-done.refs_0_.refs_1_, bf16[256,4096]{1,0:T(8,128)(2,1)S(1)} %get-tuple-element.61.refs_2_.refs_0_, ...), custom_call_target="tpu_custom_call" | custom-call | flops 2070000000 | tf_op jit(solution)/shard_map/turn_hidden/pallas_call | solution.py:41
  50.4 1.5 %collective-permute-start.11 = (bf16[128,1024]{1,0:T(8,128)(2,1)S(1)}, bf16[128,1024]{1,0:T(8,128)(2,1)S(1)}, u32[]{:S(2)}, u32[]{:S(2)}) collective-permute-start(bf16[128,1024]{1,0:T(8,128)(2,1)S(1)} %get-tuple-element.74.refs_2_.refs_3_.refs_4_), channel_id=1, source_target_pairs={{0,2},{2,0},{4,6},{6,4},{8,10},{10,8},{12,14},{14,12},{1,3},{3,1},... | collective-permute-start | bytes 786440 | tf_op jit(solution)/shard_map/ppermute | solution.py:586
  51.9 0.5 collective-permute-start.13
  52.4 4.1 %turn_x.1.refs_1_.refs_5_.refs_2_.refs_11_.refs_7_ = bf16[8192,512]{1,0:T(8,128)(2,1)} custom-call(bf16[256,8192]{1,0:T(8,128)(2,1)S(1)} %get-tuple-element.53.refs_0_, bf16[256,8192]{1,0:T(8,128)(2,1)S(1)} %collective-permute-done.refs_0_.refs_1_, bf16[128,1024]{1,0:T(8,128)(2,1)S(1)} %get-tuple-element.74.refs_2_.refs_3_.refs_4_), custom_call_target="tpu_custom_call" | custom-call | flops 4140000000 | tf_op jit(solution)/shard_map/turn_x/pallas_call | solution.py:41
  56.5 0.4 collective-permute-done.11.refs_0_
  56.9 0.1 pair_halves.1
  57.0 1.5 %collective-permute-start.14 = (bf16[128,1024]{1,0:T(8,128)(2,1)S(1)}, bf16[128,1024]{1,0:T(8,128)(2,1)S(1)}, u32[]{:S(2)}, u32[]{:S(2)}) collective-permute-start(bf16[128,1024]{1,0:T(8,128)(2,1)S(1)} %get-tuple-element.77), channel_id=1, source_target_pairs={{0,2},{2,0},{4,6},{6,4},{8,10},{10,8},{12,14},{14,12},{1,3},{3,1},... | collective-permute-start | bytes 786440 | tf_op jit(solution)/shard_map/ppermute | solution.py:586
  58.4 6.1 %u_grad.2.refs_2_.refs_5_ = bf16[8192,1024]{1,0:T(8,128)(2,1)} custom-call(bf16[4096,512]{1,0:T(8,128)(2,1)S(1)} %turn_hidden.2.refs_4_.refs_0_, bf16[128,1024]{1,0:T(8,128)(2,1)S(1)} %collective-permute-done.10.refs_1_.refs_2_, bf16[128,1024]{1,0:T(8,128)(2,1)S(1)} %collective-permute-done.12.refs_2_.refs_3_, ...), custom_call_target="tpu_custom_call" | custom-call | flops 7646444544 | tf_op jit(solution)/shard_map/u_grad/pallas_call | solution.py:41
  64.6 1.2 collective-permute-done.14.refs_1_
  65.8 1.2 collective-permute-start.15
  67.1 2.6 %collective-permute-start.16 = (bf16[32,1024]{1,0:T(8,128)(2,1)S(1)}, bf16[32,1024]{1,0:T(8,128)(2,1)S(1)}, u32[]{:S(2)}, u32[]{:S(2)}) collective-permute-start(bf16[32,1024]{1,0:T(8,128)(2,1)S(1)} %get-tuple-element.81), channel_id=1, source_target_pairs={{0,8},{2,10},{4,12},{6,14},{8,0},{10,2},{12,4},{14,6},{1,9},{3,11}... | collective-permute-start | bytes 196616 | tf_op jit(solution)/shard_map/ppermute | solution.py:586
  69.7 0.6 collective-permute-start.17
  70.3 6.2 %u_grad.3 = (bf16[8192,1024]{1,0:T(8,128)(2,1)}, bf16[1024,1024]{1,0:T(8,128)(2,1)S(1)}) custom-call(bf16[4096,512]{1,0:T(8,128)(2,1)S(1)} %turn_hidden.3.refs_5_.refs_0_, bf16[128,1024]{1,0:T(8,128)(2,1)S(1)} %collective-permute-done.10.refs_1_.refs_2_, ...), custom_call_target="tpu_custom_call", output_to_operand_aliasing={{0}: (5, {})} | custom-call | flops 7646444544 | tf_op jit(solution)/shard_map/u_grad/pallas_call | solution.py:41
  76.5 3.3 %collective-permute-start.20 = (bf16[32,1024]{1,0:T(8,128)(2,1)S(1)}, bf16[32,1024]{1,0:T(8,128)(2,1)S(1)}, u32[]{:S(2)}, u32[]{:S(2)}) collective-permute-start(bf16[32,1024]{1,0:T(8,128)(2,1)S(1)} %add_pieces.3.refs_7_.refs_0_), channel_id=1, source_target_pairs={{0,12},{2,14},{4,8},{6,10},{8,4},{10,6},{12,0},{14,2},{1,13},{3,15... | collective-permute-start | bytes 196616 | tf_op jit(solution)/shard_map/ppermute | solution.py:586
  79.8 1.1 collective-permute-start.18
  81.0 6.4 %expand.2 = (f32[512,4096]{1,0:T(8,128)S(1)}, bf16[1024,1024]{1,0:T(8,128)(2,1)S(1)}) custom-call(bf16[8192,1024]{1,0:T(8,128)(2,1)} %refs_0_.9, bf16[1024,1024]{1,0:T(8,128)(2,1)S(1)} %get-tuple-element.79.refs_1_, bf16[128,1024]{1,0:T(8,128)(2,1)S(1)} %collective-permute-done.10.refs_1_.refs_2_, ...), custom_call_target="tpu_custom_call" | custom-call | flops 7646444544 | tf_op jit(solution)/shard_map/expand/pallas_call | solution.py:41
  87.5 1.4 %collective-permute-start.22 = (bf16[128,1024]{1,0:T(8,128)(2,1)S(1)}, bf16[128,1024]{1,0:T(8,128)(2,1)S(1)}, u32[]{:S(2)}, u32[]{:S(2)}) collective-permute-start(bf16[128,1024]{1,0:T(8,128)(2,1)S(1)} %join_pieces.3.refs_7_.refs_8_.refs_3_), channel_id=1, source_target_pairs={{0,2},{2,0},{4,6},{6,4},{8,10},{10,8},{12,14},{14,12},{1,3},{3,1},... | collective-permute-start | bytes 786440 | tf_op jit(solution)/shard_map/ppermute | solution.py:586
  88.9 6.6 %expand.3 = (f32[512,4096]{1,0:T(8,128)S(1)}, bf16[1024,1024]{1,0:T(8,128)(2,1)S(1)}) custom-call(bf16[8192,1024]{1,0:T(8,128)(2,1)} %refs_0_.9, bf16[1024,1024]{1,0:T(8,128)(2,1)S(1)} %get-tuple-element.84.refs_1_, bf16[128,1024]{1,0:T(8,128)(2,1)S(1)} %collective-permute-done.10.refs_1_.refs_2_, ...), custom_call_target="tpu_custom_call" | custom-call | flops 7646444544 | tf_op jit(solution)/shard_map/expand/pallas_call | solution.py:41
  95.5 0.0 copy-start
  95.5 0.6 collective-permute-start.23
  96.1 0.2 copy-done
  96.3 0.6 pad_maximum_fusion.refs_12_
  96.9 0.3 collective-permute-done.23.refs_7_.refs_2_
  97.3 6.8 %input_grad.2 = (bf16[256,16384]{1,0:T(8,128)(2,1)}, bf16[256,4096]{1,0:T(8,128)(2,1)S(1)}, bf16[1024,1024]{1,0:T(8,128)(2,1)S(1)}) custom-call(bf16[256,4096]{1,0:T(8,128)(2,1)S(1)} %get-tuple-element.59.refs_2_.refs_0_, bf16[256,8192]{1,0:T(8,128)(2,1)S(1)} %collective-permute-done.2.refs_3_.refs_1_, f32[512,4096]{1,0:T(8,128)S(1)} %get-tuple-element.85.refs_4_.refs_2_, ...), custom_call_target="tpu_custom_call" | custom-call | flops 7646444544 | tf_op jit(solution)/shard_map/input_grad/pallas_call | solution.py:41
  104.1 0.4 collective-permute-start.24
  104.5 7.4 %input_grad.3 = (bf16[256,16384]{1,0:T(8,128)(2,1)}, bf16[256,4096]{1,0:T(8,128)(2,1)S(1)}, bf16[4096,512]{1,0:T(8,128)(2,1)S(1)}) custom-call(bf16[256,4096]{1,0:T(8,128)(2,1)S(1)} %get-tuple-element.61.refs_2_.refs_0_, bf16[256,8192]{1,0:T(8,128)(2,1)S(1)} %collective-permute-done.2.refs_3_.refs_1_, ...), custom_call_target="tpu_custom_call", output_to_operand_aliasing={{0}: (10, {})} | custom-call | flops 7646444544 | tf_op jit(solution)/shard_map/input_grad/pallas_call | solution.py:41
  111.9 0.2 collective-permute-start.25
  112.1 6.2 %v_grad.2 = (bf16[8192,1024]{1,0:T(8,128)(2,1)}, bf16[256,16384]{1,0:T(8,128)(2,1)}, bf16[4096,512]{1,0:T(8,128)(2,1)S(1)}) custom-call(bf16[4096,512]{1,0:T(8,128)(2,1)S(1)} %get-tuple-element.93.refs_0_, bf16[128,1024]{1,0:T(8,128)(2,1)S(1)} %collective-permute-done.21.refs_6_.refs_1_, ...), custom_call_target="tpu_custom_call", output_to_operand_aliasing={{1}: (6, {})} | custom-call | flops 345000000 | tf_op jit(solution)/shard_map/v_grad/pallas_call | solution.py:41
  118.3 6.2 %v_grad.3 = (bf16[8192,1024]{1,0:T(8,128)(2,1)}, bf16[256,16384]{1,0:T(8,128)(2,1)}) custom-call(bf16[4096,512]{1,0:T(8,128)(2,1)S(1)} %get-tuple-element.96.refs_0_, bf16[128,1024]{1,0:T(8,128)(2,1)S(1)} %collective-permute-done.21.refs_6_.refs_1_, ...), custom_call_target="tpu_custom_call", output_to_operand_aliasing={{0}: (5, {}), {1}: (7, {})} | custom-call | flops 7646444544 | tf_op jit(solution)/shard_map/v_grad/pallas_call | solution.py:41
  (36 shorter events, 0.3 us)
Async XLA Ops:
  2.9 11.4 %collective-permute-start = (bf16[256,8192]{1,0:T(8,128)(2,1)S(1)}, bf16[256,8192]{1,0:T(8,128)(2,1)S(1)}, u32[]{:S(2)}, u32[]{:S(2)}) collective-permute-start(bf16[256,8192]{1,0:T(8,128)(2,1)S(1)} %cut_half.2.refs_2_), channel_id=1, source_target_pairs={{0,1},{1,0},{2,3},{3,2},{4,5},{5,4},{6,7},{7,6},{8,9},{9,8},{10,11... | collective-permute-start | bytes 12582920 | tf_op jit(solution)/shard_map/ppermute | solution.py:583
  11.4 2.3 %collective-permute-start.1 = (bf16[256,1024]{1,0:T(8,128)(2,1)S(1)}, bf16[256,1024]{1,0:T(8,128)(2,1)S(1)}, u32[]{:S(2)}, u32[]{:S(2)}) collective-permute-start(bf16[256,1024]{1,0:T(8,128)(2,1)S(1)} %get-tuple-element.54.refs_1_), channel_id=1, source_target_pairs={{0,1},{1,0},{2,3},{3,2},{4,5},{5,4},{6,7},{7,6},{8,9},{9,8},{10,11... | collective-permute-start | bytes 1572872 | tf_op jit(solution)/shard_map/ppermute | solution.py:583
  13.7 9.2 %collective-permute-start.2 = (bf16[256,8192]{1,0:T(8,128)(2,1)S(1)}, bf16[256,8192]{1,0:T(8,128)(2,1)S(1)}, u32[]{:S(2)}, u32[]{:S(2)}) collective-permute-start(bf16[256,8192]{1,0:T(8,128)(2,1)S(1)} %hold.3), channel_id=1, source_target_pairs={{0,1},{1,0},{2,3},{3,2},{4,5},{5,4},{6,7},{7,6},{8,9},{9,8},{10,11... | collective-permute-start | bytes 12582920 | tf_op jit(solution)/shard_map/ppermute | solution.py:583
  20.3 9.5 %collective-permute-start.3 = (bf16[128,1024]{1,0:T(8,128)(2,1)S(1)}, bf16[128,1024]{1,0:T(8,128)(2,1)S(1)}, u32[]{:S(2)}, u32[]{:S(2)}) collective-permute-start(bf16[128,1024]{1,0:T(8,128)(2,1)S(1)} %get-tuple-element.65), channel_id=1, source_target_pairs={{0,2},{2,0},{4,6},{6,4},{8,10},{10,8},{12,14},{14,12},{1,3},{3,1},... | collective-permute-start | bytes 786440 | tf_op jit(solution)/shard_map/ppermute | solution.py:586
  29.9 9.9 %collective-permute-start.4 = (bf16[32,1024]{1,0:T(8,128)(2,1)S(1)}, bf16[32,1024]{1,0:T(8,128)(2,1)S(1)}, u32[]{:S(2)}, u32[]{:S(2)}) collective-permute-start(bf16[32,1024]{1,0:T(8,128)(2,1)S(1)} %get-tuple-element.69), channel_id=1, source_target_pairs={{0,4},{2,6},{4,0},{6,2},{8,12},{10,14},{12,8},{14,10},{1,5},{3,7},... | collective-permute-start | bytes 196616 | tf_op jit(solution)/shard_map/ppermute | solution.py:586
  31.8 8.0 %collective-permute-start.5 = (bf16[32,1024]{1,0:T(8,128)(2,1)S(1)}, bf16[32,1024]{1,0:T(8,128)(2,1)S(1)}, u32[]{:S(2)}, u32[]{:S(2)}) collective-permute-start(bf16[32,1024]{1,0:T(8,128)(2,1)S(1)} %get-tuple-element.70), channel_id=1, source_target_pairs={{0,8},{2,10},{4,12},{6,14},{8,0},{10,2},{12,4},{14,6},{1,9},{3,11}... | collective-permute-start | bytes 196616 | tf_op jit(solution)/shard_map/ppermute | solution.py:586
  34.4 6.2 %collective-permute-start.6 = (bf16[32,1024]{1,0:T(8,128)(2,1)S(1)}, bf16[32,1024]{1,0:T(8,128)(2,1)S(1)}, u32[]{:S(2)}, u32[]{:S(2)}) collective-permute-start(bf16[32,1024]{1,0:T(8,128)(2,1)S(1)} %get-tuple-element.71), channel_id=1, source_target_pairs={{0,12},{2,14},{4,8},{6,10},{8,4},{10,6},{12,0},{14,2},{1,13},{3,15... | collective-permute-start | bytes 196616 | tf_op jit(solution)/shard_map/ppermute | solution.py:586
  40.6 9.8 %collective-permute-start.9 = (bf16[32,1024]{1,0:T(8,128)(2,1)S(1)}, bf16[32,1024]{1,0:T(8,128)(2,1)S(1)}, u32[]{:S(2)}, u32[]{:S(2)}) collective-permute-start(bf16[32,1024]{1,0:T(8,128)(2,1)S(1)} %add_pieces.2.refs_7_.refs_0_), channel_id=1, source_target_pairs={{0,12},{2,14},{4,8},{6,10},{8,4},{10,6},{12,0},{14,2},{1,13},{3,15... | collective-permute-start | bytes 196616 | tf_op jit(solution)/shard_map/ppermute | solution.py:586
  43.7 6.6 %collective-permute-start.8 = (bf16[32,1024]{1,0:T(8,128)(2,1)S(1)}, bf16[32,1024]{1,0:T(8,128)(2,1)S(1)}, u32[]{:S(2)}, u32[]{:S(2)}) collective-permute-start(bf16[32,1024]{1,0:T(8,128)(2,1)S(1)} %add_pieces.2.refs_7_.refs_0_), channel_id=1, source_target_pairs={{0,8},{2,10},{4,12},{6,14},{8,0},{10,2},{12,4},{14,6},{1,9},{3,11}... | collective-permute-start | bytes 196616 | tf_op jit(solution)/shard_map/ppermute | solution.py:586
  43.7 6.6 %collective-permute-start.7 = (bf16[32,1024]{1,0:T(8,128)(2,1)S(1)}, bf16[32,1024]{1,0:T(8,128)(2,1)S(1)}, u32[]{:S(2)}, u32[]{:S(2)}) collective-permute-start(bf16[32,1024]{1,0:T(8,128)(2,1)S(1)} %add_pieces.2.refs_7_.refs_0_), channel_id=1, source_target_pairs={{0,4},{2,6},{4,0},{6,2},{8,12},{10,14},{12,8},{14,10},{1,5},{3,7},... | collective-permute-start | bytes 196616 | tf_op jit(solution)/shard_map/ppermute | solution.py:586
  50.4 6.4 %collective-permute-start.11 = (bf16[128,1024]{1,0:T(8,128)(2,1)S(1)}, bf16[128,1024]{1,0:T(8,128)(2,1)S(1)}, u32[]{:S(2)}, u32[]{:S(2)}) collective-permute-start(bf16[128,1024]{1,0:T(8,128)(2,1)S(1)} %get-tuple-element.74.refs_2_.refs_3_.refs_4_), channel_id=1, source_target_pairs={{0,2},{2,0},{4,6},{6,4},{8,10},{10,8},{12,14},{14,12},{1,3},{3,1},... | collective-permute-start | bytes 786440 | tf_op jit(solution)/shard_map/ppermute | solution.py:586
  51.9 6.6 %collective-permute-start.10 = (bf16[128,1024]{1,0:T(8,128)(2,1)S(1)}, bf16[128,1024]{1,0:T(8,128)(2,1)S(1)}, u32[]{:S(2)}, u32[]{:S(2)}) collective-permute-start(bf16[128,1024]{1,0:T(8,128)(2,1)S(1)} %get-tuple-element.74.refs_2_.refs_3_.refs_4_), channel_id=1, source_target_pairs={{0,1},{1,0},{2,3},{3,2},{4,5},{5,4},{6,7},{7,6},{8,9},{9,8},{10,11... | collective-permute-start | bytes 786440 | tf_op jit(solution)/shard_map/ppermute | solution.py:583
  51.9 5.0 %collective-permute-start.13 = (bf16[256,1024]{1,0:T(8,128)(2,1)S(1)}, bf16[256,1024]{1,0:T(8,128)(2,1)S(1)}, u32[]{:S(2)}, u32[]{:S(2)}) collective-permute-start(bf16[256,1024]{1,0:T(8,128)(2,1)S(1)} %get-tuple-element.75), channel_id=1, source_target_pairs={{0,1},{1,0},{2,3},{3,2},{4,5},{5,4},{6,7},{7,6},{8,9},{9,8},{10,11... | collective-permute-start | bytes 1572872 | tf_op jit(solution)/shard_map/ppermute | solution.py:583
  56.9 1.6 %collective-permute-start.12 = (bf16[128,1024]{1,0:T(8,128)(2,1)S(1)}, bf16[128,1024]{1,0:T(8,128)(2,1)S(1)}, u32[]{:S(2)}, u32[]{:S(2)}) collective-permute-start(bf16[128,1024]{1,0:T(8,128)(2,1)S(1)} %hold.4.refs_4_.refs_5_), channel_id=1, source_target_pairs={{0,1},{1,0},{2,3},{3,2},{4,5},{5,4},{6,7},{7,6},{8,9},{9,8},{10,11... | collective-permute-start | bytes 786440 | tf_op jit(solution)/shard_map/ppermute | solution.py:583
  57.0 8.8 %collective-permute-start.14 = (bf16[128,1024]{1,0:T(8,128)(2,1)S(1)}, bf16[128,1024]{1,0:T(8,128)(2,1)S(1)}, u32[]{:S(2)}, u32[]{:S(2)}) collective-permute-start(bf16[128,1024]{1,0:T(8,128)(2,1)S(1)} %get-tuple-element.77), channel_id=1, source_target_pairs={{0,2},{2,0},{4,6},{6,4},{8,10},{10,8},{12,14},{14,12},{1,3},{3,1},... | collective-permute-start | bytes 786440 | tf_op jit(solution)/shard_map/ppermute | solution.py:586
  65.8 10.6 %collective-permute-start.15 = (bf16[32,1024]{1,0:T(8,128)(2,1)S(1)}, bf16[32,1024]{1,0:T(8,128)(2,1)S(1)}, u32[]{:S(2)}, u32[]{:S(2)}) collective-permute-start(bf16[32,1024]{1,0:T(8,128)(2,1)S(1)} %get-tuple-element.80), channel_id=1, source_target_pairs={{0,4},{2,6},{4,0},{6,2},{8,12},{10,14},{12,8},{14,10},{1,5},{3,7},... | collective-permute-start | bytes 196616 | tf_op jit(solution)/shard_map/ppermute | solution.py:586
  67.1 9.4 %collective-permute-start.16 = (bf16[32,1024]{1,0:T(8,128)(2,1)S(1)}, bf16[32,1024]{1,0:T(8,128)(2,1)S(1)}, u32[]{:S(2)}, u32[]{:S(2)}) collective-permute-start(bf16[32,1024]{1,0:T(8,128)(2,1)S(1)} %get-tuple-element.81), channel_id=1, source_target_pairs={{0,8},{2,10},{4,12},{6,14},{8,0},{10,2},{12,4},{14,6},{1,9},{3,11}... | collective-permute-start | bytes 196616 | tf_op jit(solution)/shard_map/ppermute | solution.py:586
  69.7 6.8 %collective-permute-start.17 = (bf16[32,1024]{1,0:T(8,128)(2,1)S(1)}, bf16[32,1024]{1,0:T(8,128)(2,1)S(1)}, u32[]{:S(2)}, u32[]{:S(2)}) collective-permute-start(bf16[32,1024]{1,0:T(8,128)(2,1)S(1)} %get-tuple-element.82), channel_id=1, source_target_pairs={{0,12},{2,14},{4,8},{6,10},{8,4},{10,6},{12,0},{14,2},{1,13},{3,15... | collective-permute-start | bytes 196616 | tf_op jit(solution)/shard_map/ppermute | solution.py:586
  76.5 10.9 %collective-permute-start.20 = (bf16[32,1024]{1,0:T(8,128)(2,1)S(1)}, bf16[32,1024]{1,0:T(8,128)(2,1)S(1)}, u32[]{:S(2)}, u32[]{:S(2)}) collective-permute-start(bf16[32,1024]{1,0:T(8,128)(2,1)S(1)} %add_pieces.3.refs_7_.refs_0_), channel_id=1, source_target_pairs={{0,12},{2,14},{4,8},{6,10},{8,4},{10,6},{12,0},{14,2},{1,13},{3,15... | collective-permute-start | bytes 196616 | tf_op jit(solution)/shard_map/ppermute | solution.py:586
  79.8 7.6 %collective-permute-start.19 = (bf16[32,1024]{1,0:T(8,128)(2,1)S(1)}, bf16[32,1024]{1,0:T(8,128)(2,1)S(1)}, u32[]{:S(2)}, u32[]{:S(2)}) collective-permute-start(bf16[32,1024]{1,0:T(8,128)(2,1)S(1)} %add_pieces.3.refs_7_.refs_0_), channel_id=1, source_target_pairs={{0,8},{2,10},{4,12},{6,14},{8,0},{10,2},{12,4},{14,6},{1,9},{3,11}... | collective-permute-start | bytes 196616 | tf_op jit(solution)/shard_map/ppermute | solution.py:586
  79.8 7.6 %collective-permute-start.18 = (bf16[32,1024]{1,0:T(8,128)(2,1)S(1)}, bf16[32,1024]{1,0:T(8,128)(2,1)S(1)}, u32[]{:S(2)}, u32[]{:S(2)}) collective-permute-start(bf16[32,1024]{1,0:T(8,128)(2,1)S(1)} %add_pieces.3.refs_7_.refs_0_), channel_id=1, source_target_pairs={{0,4},{2,6},{4,0},{6,2},{8,12},{10,14},{12,8},{14,10},{1,5},{3,7},... | collective-permute-start | bytes 196616 | tf_op jit(solution)/shard_map/ppermute | solution.py:586
  87.5 8.0 %collective-permute-start.22 = (bf16[128,1024]{1,0:T(8,128)(2,1)S(1)}, bf16[128,1024]{1,0:T(8,128)(2,1)S(1)}, u32[]{:S(2)}, u32[]{:S(2)}) collective-permute-start(bf16[128,1024]{1,0:T(8,128)(2,1)S(1)} %join_pieces.3.refs_7_.refs_8_.refs_3_), channel_id=1, source_target_pairs={{0,2},{2,0},{4,6},{6,4},{8,10},{10,8},{12,14},{14,12},{1,3},{3,1},... | collective-permute-start | bytes 786440 | tf_op jit(solution)/shard_map/ppermute | solution.py:586
  88.9 8.0 %collective-permute-start.21 = (bf16[128,1024]{1,0:T(8,128)(2,1)S(1)}, bf16[128,1024]{1,0:T(8,128)(2,1)S(1)}, u32[]{:S(2)}, u32[]{:S(2)}) collective-permute-start(bf16[128,1024]{1,0:T(8,128)(2,1)S(1)} %join_pieces.3.refs_7_.refs_8_.refs_3_), channel_id=1, source_target_pairs={{0,1},{1,0},{2,3},{3,2},{4,5},{5,4},{6,7},{7,6},{8,9},{9,8},{10,11... | collective-permute-start | bytes 786440 | tf_op jit(solution)/shard_map/ppermute | solution.py:583
  95.5 0.8 copy-start
  95.5 1.7 %collective-permute-start.23 = (bf16[128,1024]{1,0:T(8,128)(2,1)S(1)}, bf16[128,1024]{1,0:T(8,128)(2,1)S(1)}, u32[]{:S(2)}, u32[]{:S(2)}) collective-permute-start(bf16[128,1024]{1,0:T(8,128)(2,1)S(1)} %hold.5.refs_9_.refs_4_), channel_id=1, source_target_pairs={{0,1},{1,0},{2,3},{3,2},{4,5},{5,4},{6,7},{7,6},{8,9},{9,8},{10,11... | collective-permute-start | bytes 786440 | tf_op jit(solution)/shard_map/ppermute | solution.py:583
  104.1 8.0 %collective-permute-start.24 = (bf16[256,4096]{1,0:T(8,128)(2,1)S(1)}, bf16[256,4096]{1,0:T(8,128)(2,1)S(1)}, u32[]{:S(2)}, u32[]{:S(2)}) collective-permute-start(bf16[256,4096]{1,0:T(8,128)(2,1)S(1)} %get-tuple-element.94), channel_id=1, source_target_pairs={{0,1},{1,0},{2,3},{3,2},{4,5},{5,4},{6,7},{7,6},{8,9},{9,8},{10,11... | collective-permute-start | bytes 6291464 | tf_op jit(solution)/shard_map/ppermute | solution.py:583
  111.9 6.4 %collective-permute-start.25 = (bf16[256,4096]{1,0:T(8,128)(2,1)S(1)}, bf16[256,4096]{1,0:T(8,128)(2,1)S(1)}, u32[]{:S(2)}, u32[]{:S(2)}) collective-permute-start(bf16[256,4096]{1,0:T(8,128)(2,1)S(1)} %get-tuple-element.98), channel_id=1, source_target_pairs={{0,1},{1,0},{2,3},{3,2},{4,5},{5,4},{6,7},{7,6},{8,9},{9,8},{10,11... | collective-permute-start | bytes 6291464 | tf_op jit(solution)/shard_map/ppermute | solution.py:583

commit v6 on v5

--- a/solution.py
+++ b/solution.py
@@ -330,8 +330,10 @@
 def factor_grad(name, s, half, turned, p, so_far, placed=None, after=(), ahead=(), work=1):
     rows2, rank = turned.shape[1], p[0].shape[1]
     part = half // 2
-    tw = min(512, part // 2)
+    tw = min(256, part // 2)
     n = part // tw
+    group = min(4, n)
+    slots = 2 * group
     np_ = len(p)
     recv, full = ([placed[0]], placed[1]) if placed else ((), None)
     nr = len(recv)
@@ -359,7 +361,7 @@
             return copy(r_refs[i], f_ref.at[:, there], put_sem.at[i])
 
         def out(k):
-            slot = lax.rem(k, 4)
+            slot = lax.rem(k, slots)
             there = pl.ds(pl.multiple_of(s * part + k * tw, tw), tw)
             return copy(stage.at[slot], o_ref.at[there, :], sems.at[slot])
 
@@ -368,19 +370,19 @@
             put(i).start()
         fill(at_ref, both, p_refs)
 
-        @pl.loop(0, n // 2)
+        @pl.loop(0, n // group)
         def _(kk):
             @pl.when(kk >= 2)
             def _():
-                out(2 * kk - 4).wait()
-                out(2 * kk - 3).wait()
-
-            for i in range(2):
-                k = 2 * kk + i
-                stage[lax.rem(k, 4)] = jnp.dot(t_ref[at_block(k, tw), :], both[...], preferred_element_type=F32).astype(BF)
+                for i in range(group):
+                    out(group * kk + i - slots).wait()
+
+            for i in range(group):
+                k = group * kk + i
+                stage[lax.rem(k, slots)] = jnp.dot(t_ref[at_block(k, tw), :], both[...], preferred_element_type=F32).astype(BF)
                 out(k).start()
 
-        for k in range(max(0, n - 4), n):
+        for k in range(max(0, n - slots), n):
             out(k).wait()
         for i in range(nr):
             put(i).wait()
@@ -391,7 +393,7 @@
         name,
         ins,
         outs,
-        [pltpu.VMEM((4, tw, rank), BF), pltpu.VMEM((rows2, rank), BF), dma(4), dma(max(1, nr))],
+        [pltpu.VMEM((slots, tw, rank), BF), pltpu.VMEM((rows2, rank), BF), dma(slots), dma(max(1, nr))],
         flops=work * rows2 * half * rank,
         aliases=aliases,
         mib=12,

time: 125 us -> 125 us (level)
  no operation moved by 1% of the time
where the time goes in v6:
time: 125 us; the launch traced here: 124 us
  Pallas kernels  91.9 us (74%)
  starting transfers between devices  27.6 us (22%)
  waiting for transfers between devices  2.75 us (2%)
    pallas_call x28, Pallas kernels, call(): pl.pallas_call(whole if n_ahead else lambda *refs: body(Place(), *refs[:n...  91.9 us
    ppermute x16, starting transfers between devices, to(): return lax.ppermute(a, 'col', [(i, i ^ d) for i in range(n)])  24.8 us
    ppermute x10, starting transfers between devices, trade(): return lax.ppermute(a, 'batch', swap)  2.89 us
  transfers between devices with their start and end apart: 26, of which 4 were waited for; matrix products, arithmetic and copies ran while one was open for 1% of the time, Pallas kernels for 62%

profile of v6, /device:TPU:0, one launch (start us, length us, event | category | flops | bytes accessed | tf_op | source)
XLA Modules:
  0.0 124.3 jit_solution(15068771274934385421)
XLA Ops:
  0.6 2.2 %cut_half.2.refs_2_ = bf16[256,8192]{1,0:T(8,128)(2,1)S(1)} custom-call(bf16[256,16384]{1,0:T(8,128)(2,1)} %refs_0_.6), custom_call_target="tpu_custom_call" | custom-call | flops 2529999872 | tf_op jit(solution)/shard_map/cut_half/pallas_call | solution.py:41
  2.9 0.5 collective-permute-start
  3.4 8.0 %project_own.1 = (bf16[256,1024]{1,0:T(8,128)(2,1)S(1)}, bf16[256,8192]{1,0:T(8,128)(2,1)S(1)}, bf16[2048,1024]{1,0:T(8,128)(2,1)S(1)}, bf16[2048,1024]{1,0:T(8,...) custom-call(bf16[256,16384]{1,0:T(8,128)(2,1)} %refs_0_.6, bf16[8192,1024]{1,0:T(8,128)(2,1)} %refs_3_.3, ...), custom_call_target="tpu_custom_call" | custom-call | flops 7646444544 | tf_op jit(solution)/shard_map/project_own/pallas_call | solution.py:41
  11.4 0.1 collective-permute-start.1
  11.5 2.2 %cut_half.3.refs_0_ = bf16[256,8192]{1,0:T(8,128)(2,1)S(1)} custom-call(bf16[256,16384]{1,0:T(8,128)(2,1)} %refs_6_.4, bf16[256,1024]{1,0:T(8,128)(2,1)S(1)} %get-tuple-element.54.refs_1_), custom_call_target="tpu_custom_call" | custom-call | flops 2529999872 | tf_op jit(solution)/shard_map/cut_half/pallas_call | solution.py:41
  13.7 0.5 collective-permute-start.2
  14.2 6.0 %project_other.1 = (f32[128,1024]{1,0:T(8,128)S(1)}, bf16[128,1024]{1,0:T(8,128)(2,1)S(1)}, bf16[256,4096]{1,0:T(8,128)(2,1)S(1)}, bf16[1024,1024]{1,0:T(8,128)(2,1)S(1)}) custom-call(bf16[256,8192]{1,0:T(8,128)(2,1)S(1)} %collective-permute-done.refs_0_.refs_1_, bf16[256,1024]{1,0:T(8,128)(2,1)S(1)} %collective-permute-done.1.refs_1_, ...), custom_call_target="tpu_custom_call" | custom-call | flops 7646444544 | tf_op jit(solution)/shard_map/project_other/pallas_call | solution.py:41
  20.3 2.6 %collective-permute-start.3 = (bf16[128,1024]{1,0:T(8,128)(2,1)S(1)}, bf16[128,1024]{1,0:T(8,128)(2,1)S(1)}, u32[]{:S(2)}, u32[]{:S(2)}) collective-permute-start(bf16[128,1024]{1,0:T(8,128)(2,1)S(1)} %get-tuple-element.65), channel_id=1, source_target_pairs={{0,2},{2,0},{4,6},{6,4},{8,10},{10,8},{12,14},{14,12},{1,3},{3,1},... | collective-permute-start | bytes 786440 | tf_op jit(solution)/shard_map/ppermute | solution.py:588
  22.9 6.9 %back_project.3 = (f32[512,1024]{1,0:T(8,128)S(1)}, f32[1,4096]{1,0:T(1,128)S(1)}, bf16[256,4096]{1,0:T(8,128)(2,1)S(1)}, bf16[1024,1024]{1,0:T(8,128)(2,1)S(1)}) custom-call(bf16[256,8192]{1,0:T(8,128)(2,1)S(1)} %get-tuple-element.53.refs_0_, bf16[256,8192]{1,0:T(8,128)(2,1)S(1)} %collective-permute-done.refs_0_.refs_1_, ...), custom_call_target="tpu_custom_call" | custom-call | flops 7646444544 | tf_op jit(solution)/shard_map/back_project/pallas_call | solution.py:41
  29.8 0.0 collective-permute-done.3.refs_1_
  29.8 0.1 pieces_of.2
  29.9 1.9 %collective-permute-start.4 = (bf16[32,1024]{1,0:T(8,128)(2,1)S(1)}, bf16[32,1024]{1,0:T(8,128)(2,1)S(1)}, u32[]{:S(2)}, u32[]{:S(2)}) collective-permute-start(bf16[32,1024]{1,0:T(8,128)(2,1)S(1)} %get-tuple-element.69), channel_id=1, source_target_pairs={{0,4},{2,6},{4,0},{6,2},{8,12},{10,14},{12,8},{14,10},{1,5},{3,7},... | collective-permute-start | bytes 196616 | tf_op jit(solution)/shard_map/ppermute | solution.py:588
  31.8 2.6 %collective-permute-start.5 = (bf16[32,1024]{1,0:T(8,128)(2,1)S(1)}, bf16[32,1024]{1,0:T(8,128)(2,1)S(1)}, u32[]{:S(2)}, u32[]{:S(2)}) collective-permute-start(bf16[32,1024]{1,0:T(8,128)(2,1)S(1)} %get-tuple-element.70), channel_id=1, source_target_pairs={{0,8},{2,10},{4,12},{6,14},{8,0},{10,2},{12,4},{14,6},{1,9},{3,11}... | collective-permute-start | bytes 196616 | tf_op jit(solution)/shard_map/ppermute | solution.py:588
  34.4 3.7 %back_project.4 = (f32[512,1024]{1,0:T(8,128)S(1)}, f32[1,2048]{1,0:T(1,128)S(1)}, bf16[1024,1024]{1,0:T(8,128)(2,1)S(1)}) custom-call(bf16[256,8192]{1,0:T(8,128)(2,1)S(1)} %get-tuple-element.53.refs_0_, bf16[256,8192]{1,0:T(8,128)(2,1)S(1)} %collective-permute-done.refs_0_.refs_1_, bf16[256,4096]{1,0:T(8,128)(2,1)S(1)} %get-tuple-element.61.refs_2_.refs_0_, ...), custom_call_target="tpu_custom_call" | custom-call | flops 3995722240 | tf_op jit(solution)/shard_map/back_project/pallas_call | solution.py:41
  38.0 1.7 %turn_hidden.2.refs_4_.refs_0_ = bf16[4096,512]{1,0:T(8,128)(2,1)S(1)} custom-call(bf16[256,8192]{1,0:T(8,128)(2,1)S(1)} %get-tuple-element.53.refs_0_, bf16[256,8192]{1,0:T(8,128)(2,1)S(1)} %collective-permute-done.refs_0_.refs_1_, bf16[256,4096]{1,0:T(8,128)(2,1)S(1)} %get-tuple-element.59.refs_2_.refs_0_, ...), custom_call_target="tpu_custom_call" | custom-call | flops 2070000000 | tf_op jit(solution)/shard_map/turn_hidden/pallas_call | solution.py:41
  39.8 0.7 collective-permute-done.6.refs_3_
  40.6 3.2 %collective-permute-start.9 = (bf16[32,1024]{1,0:T(8,128)(2,1)S(1)}, bf16[32,1024]{1,0:T(8,128)(2,1)S(1)}, u32[]{:S(2)}, u32[]{:S(2)}) collective-permute-start(bf16[32,1024]{1,0:T(8,128)(2,1)S(1)} %add_pieces.2.refs_7_.refs_0_), channel_id=1, source_target_pairs={{0,12},{2,14},{4,8},{6,10},{8,4},{10,6},{12,0},{14,2},{1,13},{3,15... | collective-permute-start | bytes 196616 | tf_op jit(solution)/shard_map/ppermute | solution.py:588
  43.7 1.3 %collective-permute-start.7 = (bf16[32,1024]{1,0:T(8,128)(2,1)S(1)}, bf16[32,1024]{1,0:T(8,128)(2,1)S(1)}, u32[]{:S(2)}, u32[]{:S(2)}) collective-permute-start(bf16[32,1024]{1,0:T(8,128)(2,1)S(1)} %add_pieces.2.refs_7_.refs_0_), channel_id=1, source_target_pairs={{0,4},{2,6},{4,0},{6,2},{8,12},{10,14},{12,8},{14,10},{1,5},{3,7},... | collective-permute-start | bytes 196616 | tf_op jit(solution)/shard_map/ppermute | solution.py:588
  45.0 3.8 %back_project.5 = (bf16[256,1024]{1,0:T(8,128)(2,1)S(1)}, f32[256,1024]{1,0:T(8,128)S(1)}, f32[1,2048]{1,0:T(1,128)S(1)}) custom-call(bf16[256,8192]{1,0:T(8,128)(2,1)S(1)} %get-tuple-element.53.refs_0_, bf16[256,8192]{1,0:T(8,128)(2,1)S(1)} %collective-permute-done.refs_0_.refs_1_, bf16[256,4096]{1,0:T(8,128)(2,1)S(1)} %get-tuple-element.61.refs_2_.refs_0_, ...), custom_call_target="tpu_custom_call" | custom-call | flops 3995722240 | tf_op jit(solution)/shard_map/back_project/pallas_call | solution.py:41
  48.8 1.6 %turn_hidden.3.refs_5_.refs_0_ = bf16[4096,512]{1,0:T(8,128)(2,1)S(1)} custom-call(bf16[256,8192]{1,0:T(8,128)(2,1)S(1)} %get-tuple-element.53.refs_0_, bf16[256,8192]{1,0:T(8,128)(2,1)S(1)} %collective-permute-done.refs_0_.refs_1_, bf16[256,4096]{1,0:T(8,128)(2,1)S(1)} %get-tuple-element.61.refs_2_.refs_0_, ...), custom_call_target="tpu_custom_call" | custom-call | flops 2070000000 | tf_op jit(solution)/shard_map/turn_hidden/pallas_call | solution.py:41
  50.4 1.5 %collective-permute-start.11 = (bf16[128,1024]{1,0:T(8,128)(2,1)S(1)}, bf16[128,1024]{1,0:T(8,128)(2,1)S(1)}, u32[]{:S(2)}, u32[]{:S(2)}) collective-permute-start(bf16[128,1024]{1,0:T(8,128)(2,1)S(1)} %get-tuple-element.74.refs_2_.refs_3_.refs_4_), channel_id=1, source_target_pairs={{0,2},{2,0},{4,6},{6,4},{8,10},{10,8},{12,14},{14,12},{1,3},{3,1},... | collective-permute-start | bytes 786440 | tf_op jit(solution)/shard_map/ppermute | solution.py:588
  51.9 0.5 collective-permute-start.13
  52.4 4.1 %turn_x.1.refs_1_.refs_5_.refs_2_.refs_11_.refs_7_ = bf16[8192,512]{1,0:T(8,128)(2,1)} custom-call(bf16[256,8192]{1,0:T(8,128)(2,1)S(1)} %get-tuple-element.53.refs_0_, bf16[256,8192]{1,0:T(8,128)(2,1)S(1)} %collective-permute-done.refs_0_.refs_1_, bf16[128,1024]{1,0:T(8,128)(2,1)S(1)} %get-tuple-element.74.refs_2_.refs_3_.refs_4_), custom_call_target="tpu_custom_call" | custom-call | flops 4140000000 | tf_op jit(solution)/shard_map/turn_x/pallas_call | solution.py:41
  56.5 0.4 collective-permute-done.11.refs_0_
  56.9 0.1 pair_halves.1
  57.0 1.5 %collective-permute-start.14 = (bf16[128,1024]{1,0:T(8,128)(2,1)S(1)}, bf16[128,1024]{1,0:T(8,128)(2,1)S(1)}, u32[]{:S(2)}, u32[]{:S(2)}) collective-permute-start(bf16[128,1024]{1,0:T(8,128)(2,1)S(1)} %get-tuple-element.77), channel_id=1, source_target_pairs={{0,2},{2,0},{4,6},{6,4},{8,10},{10,8},{12,14},{14,12},{1,3},{3,1},... | collective-permute-start | bytes 786440 | tf_op jit(solution)/shard_map/ppermute | solution.py:588
  58.4 6.0 %u_grad.2.refs_2_.refs_5_ = bf16[8192,1024]{1,0:T(8,128)(2,1)} custom-call(bf16[4096,512]{1,0:T(8,128)(2,1)S(1)} %turn_hidden.2.refs_4_.refs_0_, bf16[128,1024]{1,0:T(8,128)(2,1)S(1)} %collective-permute-done.10.refs_1_.refs_2_, bf16[128,1024]{1,0:T(8,128)(2,1)S(1)} %collective-permute-done.12.refs_2_.refs_3_, ...), custom_call_target="tpu_custom_call" | custom-call | flops 7646444544 | tf_op jit(solution)/shard_map/u_grad/pallas_call | solution.py:41
  64.5 1.3 %collective-permute-done.14.refs_1_ = bf16[128,1024]{1,0:T(8,128)(2,1)S(1)} collective-permute-done((bf16[128,1024]{1,0:T(8,128)(2,1)S(1)}, bf16[128,1024]{1,0:T(8,128)(2,1)S(1)}, u32[]{:S(2)}, u32[]{:S(2)}) %collective-permute-start.14) | collective-permute-done | bytes 262176 | tf_op jit(solution)/shard_map/ppermute | solution.py:588
  65.8 1.2 %collective-permute-start.15 = (bf16[32,1024]{1,0:T(8,128)(2,1)S(1)}, bf16[32,1024]{1,0:T(8,128)(2,1)S(1)}, u32[]{:S(2)}, u32[]{:S(2)}) collective-permute-start(bf16[32,1024]{1,0:T(8,128)(2,1)S(1)} %get-tuple-element.80), channel_id=1, source_target_pairs={{0,4},{2,6},{4,0},{6,2},{8,12},{10,14},{12,8},{14,10},{1,5},{3,7},... | collective-permute-start | bytes 196616 | tf_op jit(solution)/shard_map/ppermute | solution.py:588
  67.1 2.6 %collective-permute-start.16 = (bf16[32,1024]{1,0:T(8,128)(2,1)S(1)}, bf16[32,1024]{1,0:T(8,128)(2,1)S(1)}, u32[]{:S(2)}, u32[]{:S(2)}) collective-permute-start(bf16[32,1024]{1,0:T(8,128)(2,1)S(1)} %get-tuple-element.81), channel_id=1, source_target_pairs={{0,8},{2,10},{4,12},{6,14},{8,0},{10,2},{12,4},{14,6},{1,9},{3,11}... | collective-permute-start | bytes 196616 | tf_op jit(solution)/shard_map/ppermute | solution.py:588
  69.7 0.6 collective-permute-start.17
  70.3 6.0 %u_grad.3 = (bf16[8192,1024]{1,0:T(8,128)(2,1)}, bf16[1024,1024]{1,0:T(8,128)(2,1)S(1)}) custom-call(bf16[4096,512]{1,0:T(8,128)(2,1)S(1)} %turn_hidden.3.refs_5_.refs_0_, bf16[128,1024]{1,0:T(8,128)(2,1)S(1)} %collective-permute-done.10.refs_1_.refs_2_, ...), custom_call_target="tpu_custom_call", output_to_operand_aliasing={{0}: (5, {})} | custom-call | flops 7646444544 | tf_op jit(solution)/shard_map/u_grad/pallas_call | solution.py:41
  76.4 3.3 %collective-permute-start.20 = (bf16[32,1024]{1,0:T(8,128)(2,1)S(1)}, bf16[32,1024]{1,0:T(8,128)(2,1)S(1)}, u32[]{:S(2)}, u32[]{:S(2)}) collective-permute-start(bf16[32,1024]{1,0:T(8,128)(2,1)S(1)} %add_pieces.3.refs_7_.refs_0_), channel_id=1, source_target_pairs={{0,12},{2,14},{4,8},{6,10},{8,4},{10,6},{12,0},{14,2},{1,13},{3,15... | collective-permute-start | bytes 196616 | tf_op jit(solution)/shard_map/ppermute | solution.py:588
  79.7 1.1 collective-permute-start.18
  80.8 6.4 %expand.2 = (f32[512,4096]{1,0:T(8,128)S(1)}, bf16[1024,1024]{1,0:T(8,128)(2,1)S(1)}) custom-call(bf16[8192,1024]{1,0:T(8,128)(2,1)} %refs_0_.9, bf16[1024,1024]{1,0:T(8,128)(2,1)S(1)} %get-tuple-element.79.refs_1_, bf16[128,1024]{1,0:T(8,128)(2,1)S(1)} %collective-permute-done.10.refs_1_.refs_2_, ...), custom_call_target="tpu_custom_call" | custom-call | flops 7646444544 | tf_op jit(solution)/shard_map/expand/pallas_call | solution.py:41
  87.3 1.5 %collective-permute-start.22 = (bf16[128,1024]{1,0:T(8,128)(2,1)S(1)}, bf16[128,1024]{1,0:T(8,128)(2,1)S(1)}, u32[]{:S(2)}, u32[]{:S(2)}) collective-permute-start(bf16[128,1024]{1,0:T(8,128)(2,1)S(1)} %join_pieces.3.refs_7_.refs_8_.refs_3_), channel_id=1, source_target_pairs={{0,2},{2,0},{4,6},{6,4},{8,10},{10,8},{12,14},{14,12},{1,3},{3,1},... | collective-permute-start | bytes 786440 | tf_op jit(solution)/shard_map/ppermute | solution.py:588
  88.8 6.6 %expand.3 = (f32[512,4096]{1,0:T(8,128)S(1)}, bf16[1024,1024]{1,0:T(8,128)(2,1)S(1)}) custom-call(bf16[8192,1024]{1,0:T(8,128)(2,1)} %refs_0_.9, bf16[1024,1024]{1,0:T(8,128)(2,1)S(1)} %get-tuple-element.84.refs_1_, bf16[128,1024]{1,0:T(8,128)(2,1)S(1)} %collective-permute-done.10.refs_1_.refs_2_, ...), custom_call_target="tpu_custom_call" | custom-call | flops 7646444544 | tf_op jit(solution)/shard_map/expand/pallas_call | solution.py:41
  95.4 0.0 copy-start
  95.4 0.6 collective-permute-start.23
  96.0 0.2 copy-done
  96.2 0.6 pad_maximum_fusion.refs_12_
  96.8 0.3 collective-permute-done.23.refs_7_.refs_2_
  97.2 6.8 %input_grad.2 = (bf16[256,16384]{1,0:T(8,128)(2,1)}, bf16[256,4096]{1,0:T(8,128)(2,1)S(1)}, bf16[1024,1024]{1,0:T(8,128)(2,1)S(1)}) custom-call(bf16[256,4096]{1,0:T(8,128)(2,1)S(1)} %get-tuple-element.59.refs_2_.refs_0_, bf16[256,8192]{1,0:T(8,128)(2,1)S(1)} %collective-permute-done.2.refs_3_.refs_1_, f32[512,4096]{1,0:T(8,128)S(1)} %get-tuple-element.85.refs_4_.refs_2_, ...), custom_call_target="tpu_custom_call" | custom-call | flops 7646444544 | tf_op jit(solution)/shard_map/input_grad/pallas_call | solution.py:41
  103.9 0.4 collective-permute-start.24
  104.4 7.4 %input_grad.3 = (bf16[256,16384]{1,0:T(8,128)(2,1)}, bf16[256,4096]{1,0:T(8,128)(2,1)S(1)}, bf16[4096,512]{1,0:T(8,128)(2,1)S(1)}) custom-call(bf16[256,4096]{1,0:T(8,128)(2,1)S(1)} %get-tuple-element.61.refs_2_.refs_0_, bf16[256,8192]{1,0:T(8,128)(2,1)S(1)} %collective-permute-done.2.refs_3_.refs_1_, ...), custom_call_target="tpu_custom_call", output_to_operand_aliasing={{0}: (10, {})} | custom-call | flops 7646444544 | tf_op jit(solution)/shard_map/input_grad/pallas_call | solution.py:41
  111.8 0.2 collective-permute-start.25
  112.0 6.1 %v_grad.2 = (bf16[8192,1024]{1,0:T(8,128)(2,1)}, bf16[256,16384]{1,0:T(8,128)(2,1)}, bf16[4096,512]{1,0:T(8,128)(2,1)S(1)}) custom-call(bf16[4096,512]{1,0:T(8,128)(2,1)S(1)} %get-tuple-element.93.refs_0_, bf16[128,1024]{1,0:T(8,128)(2,1)S(1)} %collective-permute-done.21.refs_6_.refs_1_, ...), custom_call_target="tpu_custom_call", output_to_operand_aliasing={{1}: (6, {})} | custom-call | flops 345000000 | tf_op jit(solution)/shard_map/v_grad/pallas_call | solution.py:41
  118.0 6.1 %v_grad.3 = (bf16[8192,1024]{1,0:T(8,128)(2,1)}, bf16[256,16384]{1,0:T(8,128)(2,1)}) custom-call(bf16[4096,512]{1,0:T(8,128)(2,1)S(1)} %get-tuple-element.96.refs_0_, bf16[128,1024]{1,0:T(8,128)(2,1)S(1)} %collective-permute-done.21.refs_6_.refs_1_, ...), custom_call_target="tpu_custom_call", output_to_operand_aliasing={{0}: (5, {}), {1}: (7, {})} | custom-call | flops 7646444544 | tf_op jit(solution)/shard_map/v_grad/pallas_call | solution.py:41
  (36 shorter events, 0.3 us)
Async XLA Ops:
  2.9 11.4 %collective-permute-start = (bf16[256,8192]{1,0:T(8,128)(2,1)S(1)}, bf16[256,8192]{1,0:T(8,128)(2,1)S(1)}, u32[]{:S(2)}, u32[]{:S(2)}) collective-permute-start(bf16[256,8192]{1,0:T(8,128)(2,1)S(1)} %cut_half.2.refs_2_), channel_id=1, source_target_pairs={{0,1},{1,0},{2,3},{3,2},{4,5},{5,4},{6,7},{7,6},{8,9},{9,8},{10,11... | collective-permute-start | bytes 12582920 | tf_op jit(solution)/shard_map/ppermute | solution.py:585
  11.4 2.3 %collective-permute-start.1 = (bf16[256,1024]{1,0:T(8,128)(2,1)S(1)}, bf16[256,1024]{1,0:T(8,128)(2,1)S(1)}, u32[]{:S(2)}, u32[]{:S(2)}) collective-permute-start(bf16[256,1024]{1,0:T(8,128)(2,1)S(1)} %get-tuple-element.54.refs_1_), channel_id=1, source_target_pairs={{0,1},{1,0},{2,3},{3,2},{4,5},{5,4},{6,7},{7,6},{8,9},{9,8},{10,11... | collective-permute-start | bytes 1572872 | tf_op jit(solution)/shard_map/ppermute | solution.py:585
  13.7 9.2 %collective-permute-start.2 = (bf16[256,8192]{1,0:T(8,128)(2,1)S(1)}, bf16[256,8192]{1,0:T(8,128)(2,1)S(1)}, u32[]{:S(2)}, u32[]{:S(2)}) collective-permute-start(bf16[256,8192]{1,0:T(8,128)(2,1)S(1)} %hold.3), channel_id=1, source_target_pairs={{0,1},{1,0},{2,3},{3,2},{4,5},{5,4},{6,7},{7,6},{8,9},{9,8},{10,11... | collective-permute-start | bytes 12582920 | tf_op jit(solution)/shard_map/ppermute | solution.py:585
  20.3 9.5 %collective-permute-start.3 = (bf16[128,1024]{1,0:T(8,128)(2,1)S(1)}, bf16[128,1024]{1,0:T(8,128)(2,1)S(1)}, u32[]{:S(2)}, u32[]{:S(2)}) collective-permute-start(bf16[128,1024]{1,0:T(8,128)(2,1)S(1)} %get-tuple-element.65), channel_id=1, source_target_pairs={{0,2},{2,0},{4,6},{6,4},{8,10},{10,8},{12,14},{14,12},{1,3},{3,1},... | collective-permute-start | bytes 786440 | tf_op jit(solution)/shard_map/ppermute | solution.py:588
  29.9 9.9 %collective-permute-start.4 = (bf16[32,1024]{1,0:T(8,128)(2,1)S(1)}, bf16[32,1024]{1,0:T(8,128)(2,1)S(1)}, u32[]{:S(2)}, u32[]{:S(2)}) collective-permute-start(bf16[32,1024]{1,0:T(8,128)(2,1)S(1)} %get-tuple-element.69), channel_id=1, source_target_pairs={{0,4},{2,6},{4,0},{6,2},{8,12},{10,14},{12,8},{14,10},{1,5},{3,7},... | collective-permute-start | bytes 196616 | tf_op jit(solution)/shard_map/ppermute | solution.py:588
  31.8 8.0 %collective-permute-start.5 = (bf16[32,1024]{1,0:T(8,128)(2,1)S(1)}, bf16[32,1024]{1,0:T(8,128)(2,1)S(1)}, u32[]{:S(2)}, u32[]{:S(2)}) collective-permute-start(bf16[32,1024]{1,0:T(8,128)(2,1)S(1)} %get-tuple-element.70), channel_id=1, source_target_pairs={{0,8},{2,10},{4,12},{6,14},{8,0},{10,2},{12,4},{14,6},{1,9},{3,11}... | collective-permute-start | bytes 196616 | tf_op jit(solution)/shard_map/ppermute | solution.py:588
  34.4 6.2 %collective-permute-start.6 = (bf16[32,1024]{1,0:T(8,128)(2,1)S(1)}, bf16[32,1024]{1,0:T(8,128)(2,1)S(1)}, u32[]{:S(2)}, u32[]{:S(2)}) collective-permute-start(bf16[32,1024]{1,0:T(8,128)(2,1)S(1)} %get-tuple-element.71), channel_id=1, source_target_pairs={{0,12},{2,14},{4,8},{6,10},{8,4},{10,6},{12,0},{14,2},{1,13},{3,15... | collective-permute-start | bytes 196616 | tf_op jit(solution)/shard_map/ppermute | solution.py:588
  40.6 9.8 %collective-permute-start.9 = (bf16[32,1024]{1,0:T(8,128)(2,1)S(1)}, bf16[32,1024]{1,0:T(8,128)(2,1)S(1)}, u32[]{:S(2)}, u32[]{:S(2)}) collective-permute-start(bf16[32,1024]{1,0:T(8,128)(2,1)S(1)} %add_pieces.2.refs_7_.refs_0_), channel_id=1, source_target_pairs={{0,12},{2,14},{4,8},{6,10},{8,4},{10,6},{12,0},{14,2},{1,13},{3,15... | collective-permute-start | bytes 196616 | tf_op jit(solution)/shard_map/ppermute | solution.py:588
  43.7 6.6 %collective-permute-start.8 = (bf16[32,1024]{1,0:T(8,128)(2,1)S(1)}, bf16[32,1024]{1,0:T(8,128)(2,1)S(1)}, u32[]{:S(2)}, u32[]{:S(2)}) collective-permute-start(bf16[32,1024]{1,0:T(8,128)(2,1)S(1)} %add_pieces.2.refs_7_.refs_0_), channel_id=1, source_target_pairs={{0,8},{2,10},{4,12},{6,14},{8,0},{10,2},{12,4},{14,6},{1,9},{3,11}... | collective-permute-start | bytes 196616 | tf_op jit(solution)/shard_map/ppermute | solution.py:588
  43.7 6.6 %collective-permute-start.7 = (bf16[32,1024]{1,0:T(8,128)(2,1)S(1)}, bf16[32,1024]{1,0:T(8,128)(2,1)S(1)}, u32[]{:S(2)}, u32[]{:S(2)}) collective-permute-start(bf16[32,1024]{1,0:T(8,128)(2,1)S(1)} %add_pieces.2.refs_7_.refs_0_), channel_id=1, source_target_pairs={{0,4},{2,6},{4,0},{6,2},{8,12},{10,14},{12,8},{14,10},{1,5},{3,7},... | collective-permute-start | bytes 196616 | tf_op jit(solution)/shard_map/ppermute | solution.py:588
  50.4 6.4 %collective-permute-start.11 = (bf16[128,1024]{1,0:T(8,128)(2,1)S(1)}, bf16[128,1024]{1,0:T(8,128)(2,1)S(1)}, u32[]{:S(2)}, u32[]{:S(2)}) collective-permute-start(bf16[128,1024]{1,0:T(8,128)(2,1)S(1)} %get-tuple-element.74.refs_2_.refs_3_.refs_4_), channel_id=1, source_target_pairs={{0,2},{2,0},{4,6},{6,4},{8,10},{10,8},{12,14},{14,12},{1,3},{3,1},... | collective-permute-start | bytes 786440 | tf_op jit(solution)/shard_map/ppermute | solution.py:588
  51.9 6.6 %collective-permute-start.10 = (bf16[128,1024]{1,0:T(8,128)(2,1)S(1)}, bf16[128,1024]{1,0:T(8,128)(2,1)S(1)}, u32[]{:S(2)}, u32[]{:S(2)}) collective-permute-start(bf16[128,1024]{1,0:T(8,128)(2,1)S(1)} %get-tuple-element.74.refs_2_.refs_3_.refs_4_), channel_id=1, source_target_pairs={{0,1},{1,0},{2,3},{3,2},{4,5},{5,4},{6,7},{7,6},{8,9},{9,8},{10,11... | collective-permute-start | bytes 786440 | tf_op jit(solution)/shard_map/ppermute | solution.py:585
  51.9 5.0 %collective-permute-start.13 = (bf16[256,1024]{1,0:T(8,128)(2,1)S(1)}, bf16[256,1024]{1,0:T(8,128)(2,1)S(1)}, u32[]{:S(2)}, u32[]{:S(2)}) collective-permute-start(bf16[256,1024]{1,0:T(8,128)(2,1)S(1)} %get-tuple-element.75), channel_id=1, source_target_pairs={{0,1},{1,0},{2,3},{3,2},{4,5},{5,4},{6,7},{7,6},{8,9},{9,8},{10,11... | collective-permute-start | bytes 1572872 | tf_op jit(solution)/shard_map/ppermute | solution.py:585
  56.9 1.6 %collective-permute-start.12 = (bf16[128,1024]{1,0:T(8,128)(2,1)S(1)}, bf16[128,1024]{1,0:T(8,128)(2,1)S(1)}, u32[]{:S(2)}, u32[]{:S(2)}) collective-permute-start(bf16[128,1024]{1,0:T(8,128)(2,1)S(1)} %hold.4.refs_4_.refs_5_), channel_id=1, source_target_pairs={{0,1},{1,0},{2,3},{3,2},{4,5},{5,4},{6,7},{7,6},{8,9},{9,8},{10,11... | collective-permute-start | bytes 786440 | tf_op jit(solution)/shard_map/ppermute | solution.py:585
  57.0 8.8 %collective-permute-start.14 = (bf16[128,1024]{1,0:T(8,128)(2,1)S(1)}, bf16[128,1024]{1,0:T(8,128)(2,1)S(1)}, u32[]{:S(2)}, u32[]{:S(2)}) collective-permute-start(bf16[128,1024]{1,0:T(8,128)(2,1)S(1)} %get-tuple-element.77), channel_id=1, source_target_pairs={{0,2},{2,0},{4,6},{6,4},{8,10},{10,8},{12,14},{14,12},{1,3},{3,1},... | collective-permute-start | bytes 786440 | tf_op jit(solution)/shard_map/ppermute | solution.py:588
  65.8 10.5 %collective-permute-start.15 = (bf16[32,1024]{1,0:T(8,128)(2,1)S(1)}, bf16[32,1024]{1,0:T(8,128)(2,1)S(1)}, u32[]{:S(2)}, u32[]{:S(2)}) collective-permute-start(bf16[32,1024]{1,0:T(8,128)(2,1)S(1)} %get-tuple-element.80), channel_id=1, source_target_pairs={{0,4},{2,6},{4,0},{6,2},{8,12},{10,14},{12,8},{14,10},{1,5},{3,7},... | collective-permute-start | bytes 196616 | tf_op jit(solution)/shard_map/ppermute | solution.py:588
  67.1 9.3 %collective-permute-start.16 = (bf16[32,1024]{1,0:T(8,128)(2,1)S(1)}, bf16[32,1024]{1,0:T(8,128)(2,1)S(1)}, u32[]{:S(2)}, u32[]{:S(2)}) collective-permute-start(bf16[32,1024]{1,0:T(8,128)(2,1)S(1)} %get-tuple-element.81), channel_id=1, source_target_pairs={{0,8},{2,10},{4,12},{6,14},{8,0},{10,2},{12,4},{14,6},{1,9},{3,11}... | collective-permute-start | bytes 196616 | tf_op jit(solution)/shard_map/ppermute | solution.py:588
  69.7 6.6 %collective-permute-start.17 = (bf16[32,1024]{1,0:T(8,128)(2,1)S(1)}, bf16[32,1024]{1,0:T(8,128)(2,1)S(1)}, u32[]{:S(2)}, u32[]{:S(2)}) collective-permute-start(bf16[32,1024]{1,0:T(8,128)(2,1)S(1)} %get-tuple-element.82), channel_id=1, source_target_pairs={{0,12},{2,14},{4,8},{6,10},{8,4},{10,6},{12,0},{14,2},{1,13},{3,15... | collective-permute-start | bytes 196616 | tf_op jit(solution)/shard_map/ppermute | solution.py:588
  76.4 10.9 %collective-permute-start.20 = (bf16[32,1024]{1,0:T(8,128)(2,1)S(1)}, bf16[32,1024]{1,0:T(8,128)(2,1)S(1)}, u32[]{:S(2)}, u32[]{:S(2)}) collective-permute-start(bf16[32,1024]{1,0:T(8,128)(2,1)S(1)} %add_pieces.3.refs_7_.refs_0_), channel_id=1, source_target_pairs={{0,12},{2,14},{4,8},{6,10},{8,4},{10,6},{12,0},{14,2},{1,13},{3,15... | collective-permute-start | bytes 196616 | tf_op jit(solution)/shard_map/ppermute | solution.py:588
  79.7 7.6 %collective-permute-start.19 = (bf16[32,1024]{1,0:T(8,128)(2,1)S(1)}, bf16[32,1024]{1,0:T(8,128)(2,1)S(1)}, u32[]{:S(2)}, u32[]{:S(2)}) collective-permute-start(bf16[32,1024]{1,0:T(8,128)(2,1)S(1)} %add_pieces.3.refs_7_.refs_0_), channel_id=1, source_target_pairs={{0,8},{2,10},{4,12},{6,14},{8,0},{10,2},{12,4},{14,6},{1,9},{3,11}... | collective-permute-start | bytes 196616 | tf_op jit(solution)/shard_map/ppermute | solution.py:588
  79.7 7.6 %collective-permute-start.18 = (bf16[32,1024]{1,0:T(8,128)(2,1)S(1)}, bf16[32,1024]{1,0:T(8,128)(2,1)S(1)}, u32[]{:S(2)}, u32[]{:S(2)}) collective-permute-start(bf16[32,1024]{1,0:T(8,128)(2,1)S(1)} %add_pieces.3.refs_7_.refs_0_), channel_id=1, source_target_pairs={{0,4},{2,6},{4,0},{6,2},{8,12},{10,14},{12,8},{14,10},{1,5},{3,7},... | collective-permute-start | bytes 196616 | tf_op jit(solution)/shard_map/ppermute | solution.py:588
  87.3 8.0 %collective-permute-start.22 = (bf16[128,1024]{1,0:T(8,128)(2,1)S(1)}, bf16[128,1024]{1,0:T(8,128)(2,1)S(1)}, u32[]{:S(2)}, u32[]{:S(2)}) collective-permute-start(bf16[128,1024]{1,0:T(8,128)(2,1)S(1)} %join_pieces.3.refs_7_.refs_8_.refs_3_), channel_id=1, source_target_pairs={{0,2},{2,0},{4,6},{6,4},{8,10},{10,8},{12,14},{14,12},{1,3},{3,1},... | collective-permute-start | bytes 786440 | tf_op jit(solution)/shard_map/ppermute | solution.py:588
  88.8 8.0 %collective-permute-start.21 = (bf16[128,1024]{1,0:T(8,128)(2,1)S(1)}, bf16[128,1024]{1,0:T(8,128)(2,1)S(1)}, u32[]{:S(2)}, u32[]{:S(2)}) collective-permute-start(bf16[128,1024]{1,0:T(8,128)(2,1)S(1)} %join_pieces.3.refs_7_.refs_8_.refs_3_), channel_id=1, source_target_pairs={{0,1},{1,0},{2,3},{3,2},{4,5},{5,4},{6,7},{7,6},{8,9},{9,8},{10,11... | collective-permute-start | bytes 786440 | tf_op jit(solution)/shard_map/ppermute | solution.py:585
  95.4 0.8 copy-start
  95.4 1.7 %collective-permute-start.23 = (bf16[128,1024]{1,0:T(8,128)(2,1)S(1)}, bf16[128,1024]{1,0:T(8,128)(2,1)S(1)}, u32[]{:S(2)}, u32[]{:S(2)}) collective-permute-start(bf16[128,1024]{1,0:T(8,128)(2,1)S(1)} %hold.5.refs_9_.refs_4_), channel_id=1, source_target_pairs={{0,1},{1,0},{2,3},{3,2},{4,5},{5,4},{6,7},{7,6},{8,9},{9,8},{10,11... | collective-permute-start | bytes 786440 | tf_op jit(solution)/shard_map/ppermute | solution.py:585
  103.9 8.0 %collective-permute-start.24 = (bf16[256,4096]{1,0:T(8,128)(2,1)S(1)}, bf16[256,4096]{1,0:T(8,128)(2,1)S(1)}, u32[]{:S(2)}, u32[]{:S(2)}) collective-permute-start(bf16[256,4096]{1,0:T(8,128)(2,1)S(1)} %get-tuple-element.94), channel_id=1, source_target_pairs={{0,1},{1,0},{2,3},{3,2},{4,5},{5,4},{6,7},{7,6},{8,9},{9,8},{10,11... | collective-permute-start | bytes 6291464 | tf_op jit(solution)/shard_map/ppermute | solution.py:585
  111.8 6.3 %collective-permute-start.25 = (bf16[256,4096]{1,0:T(8,128)(2,1)S(1)}, bf16[256,4096]{1,0:T(8,128)(2,1)S(1)}, u32[]{:S(2)}, u32[]{:S(2)}) collective-permute-start(bf16[256,4096]{1,0:T(8,128)(2,1)S(1)} %get-tuple-element.98), channel_id=1, source_target_pairs={{0,1},{1,0},{2,3},{3,2},{4,5},{5,4},{6,7},{7,6},{8,9},{9,8},{10,11... | collective-permute-start | bytes 6291464 | tf_op jit(solution)/shard_map/ppermute | solution.py:585
